TPU v7x, 32 devices: a whole 2x2x4 slice. The times are simulated.
32 devices in a mesh: fsdp: 8 (over z, core), grp: 2 (over y), tp: 2 (over x).
Axes of the slice: x: 2, y: 2, z: 4, core: 2. Of those that a mesh axis runs over, the one named last changes fastest.
Arguments:
- hidden_states: bfloat16 [4, 128, 8192], P(None, ('fsdp', 'grp'), 'tp'), may hold values from -6 to 6
- queries: bfloat16 [4, 128, 64, 128], P(None, ('fsdp', 'grp'), 'tp'), as said below
- cache_keys: bfloat16 [128, 768, 8, 128], P(('fsdp', 'grp'), None, 'tp'), as said below
- cache_values: bfloat16 [128, 768, 8, 128], P(('fsdp', 'grp'), None, 'tp'), may hold values from -6 to 6
- cache_lengths: int32 [128], P(('fsdp', 'grp')), may hold values from 2 to 768, as said below
- projection_weight_matrices: bfloat16 [2, 8192, 1024], P(None, None, 'tp'), may hold values from -0.0625 to 0.0625
- factor_down: bfloat16 [2, 8192, 64], P(None, ('fsdp', 'grp')), may hold values from -0.0625 to 0.0625
- factor_up: bfloat16 [2, 64, 1024], P(None, None, ('fsdp', 'grp')), may hold values from -0.375 to 0.375
Outputs:
- merged: bfloat16 [2, 8192, 1024], P(None, None, 'tp')
- attended: bfloat16 [4, 128, 64, 128], P(None, ('fsdp', 'grp'), 'tp')
Inputs may be any that keep to these rules, and one draw needn't show every extreme that they name: `cache_lengths`: at least 2; some row has exactly 768. `queries`: real-valued. `cache_keys`: real-valued.
All inputs are finite; a program needn't handle non-finite values.
Results may differ from a plain program's by a relative error of at most 0.0066.
Values may be sent and summed in bfloat16 or wider, within the bound.
No kernel may reach another device: no remote copies, remote signals or barrier semaphores. Data moves between devices by JAX's collectives and lax.ppermute only.
A program may use at most 192 MiB of HBM per device.

v0:
```python
import functools
import math

import jax
import jax.numpy as jnp
from jax import lax
from jax.experimental import pallas as pl
from jax.experimental.pallas import tpu as pltpu
from jax.sharding import PartitionSpec as P

AXES = ("fsdp", "grp", "tp")
ADAPTER_SCALING = 2.0
LOG2E = math.log2(math.e)
MIB = 1024 * 1024
ANY = pl.BlockSpec(memory_space=pl.ANY)
HBM = pl.BlockSpec(memory_space=pltpu.HBM)
VMEM = pl.BlockSpec(memory_space=pltpu.VMEM)
SMEM = pl.BlockSpec(memory_space=pltpu.SMEM)


class Layout:
    def __init__(self, mesh):
        self.fsdp, self.grp, self.tp = (mesh.shape[a] for a in AXES)
        self.depth = self.fsdp // 2
        self.ring = self.depth * self.grp
        self.block = self.depth // self.tp

    def flat(self, z, core, g, t):
        return ((z * 2 + core) * self.grp + g) * self.tp + t

    def devices(self):
        for z in range(self.depth):
            for core in range(2):
                for g in range(self.grp):
                    for t in range(self.tp):
                        yield z, core, g, t

    def place(self, z, g):
        return g * self.depth + (z if g % 2 == 0 else self.depth - 1 - z)

    def at(self, position):
        g, z = divmod(position, self.depth)
        return (z if g % 2 == 0 else self.depth - 1 - z), g

    def ring_step(self):
        pairs = []
        for z, core, g, t in self.devices():
            to_z, to_g = self.at((self.place(z, g) + (1 - 2 * core)) % self.ring)
            pairs.append((self.flat(z, core, g, t), self.flat(to_z, core, to_g, t)))
        return pairs

    def plane_swap(self):
        return [(self.flat(z, c, g, t), self.flat(z, c, g, t ^ 1)) for z, c, g, t in self.devices()]

    def core_swap(self):
        return [
            (self.flat(z, c, g, t), self.flat(z, 1 - c, g, t)) for z, c, g, t in self.devices()
        ]

    def feature_step(self, step):
        return [
            (self.flat(z, c, g, (t + step) % self.tp), self.flat(z, c, g, t))
            for z, c, g, t in self.devices()
        ]


TYPICAL = pl.CostEstimate(flops=6 * 10**8, bytes_accessed=10**7, transcendentals=0)


def over(x, n):
    return x >> (n.bit_length() - 1) if n & (n - 1) == 0 else x // n


def within(x, n):
    return x & (n - 1) if n & (n - 1) == 0 else x % n


def after_all(arrays, token):
    return lax.optimization_barrier((arrays, token))


def pinned(x, space=pltpu.HBM):
    return pltpu.with_memory_space_constraint(x, space)


def sort_rows(lengths, order):
    rows = lengths.shape[0]
    held = [lengths[r] for r in range(rows)]
    for r in range(rows):
        rank = jnp.int32(0)
        for other in range(rows):
            if other != r:
                ahead = held[other] >= held[r] if other < r else held[other] > held[r]
                rank = rank + ahead.astype(jnp.int32)
        order[rank] = r


def by_length(length, sizes, act):
    below = 0
    for slots in sizes:

        @pl.when((length > below) & (length <= slots))
        def _():
            act(slots)

        below = slots


def up_columns(up):
    return jnp.concatenate([up[k] for k in range(up.shape[0])], axis=1)


def plane_part():
    return lax.rem(lax.axis_index("tp"), 2)


def begin_all(down, up, len_hbm, q_hbm, pair, rest, lengths, order, q_ref, up_buf, sems, more):
    lanes = pair.shape[3]
    depth = down.shape[2]
    tiles = depth // lanes
    part = plane_part()
    copies = [
        pltpu.make_async_copy(
            down.at[k, :, pl.ds(i * lanes, lanes)], array.at[0, i], sems.at[which, i]
        )
        for which, (k, array) in enumerate(((part, pair), (1 - part, rest)))
        for i in range(tiles)
    ]
    up_copy = pltpu.make_async_copy(up, up_buf, more.at[0])
    len_copy = pltpu.make_async_copy(len_hbm, lengths, more.at[1])
    q_copy = pltpu.make_async_copy(q_hbm, q_ref, more.at[2])
    for copy in [len_copy, up_copy] + copies + [q_copy]:
        copy.start()
    len_copy.wait()
    sort_rows(lengths, order)
    up_copy.wait()
    columns = up_columns(up_buf)
    pair[0, tiles, :, : columns.shape[1]] = columns
    for copy in copies + [q_copy]:
        copy.wait()


def begin(down, up, lengths, queries):
    count, rank, depth = down.shape
    tiles = depth // 128
    scalars = pltpu.SMEM(lengths.shape, jnp.int32)
    return pl.pallas_call(
        begin_all,
        out_shape=(
            pltpu.VMEM((2, tiles + 1, rank, 128), down.dtype),
            pltpu.VMEM((2, tiles, rank, 128), down.dtype),
            scalars,
            scalars,
            pltpu.VMEM(queries.shape, queries.dtype),
        ),
        in_specs=[HBM] * 4,
        out_specs=(VMEM, VMEM, SMEM, SMEM, VMEM),
        scratch_shapes=[
            pltpu.VMEM(up.shape, up.dtype),
            pltpu.SemaphoreType.DMA((count, tiles)),
            pltpu.SemaphoreType.DMA((3,)),
        ],
        compiler_params=pltpu.CompilerParams(vmem_limit_bytes=2 * MIB),
        cost_estimate=TYPICAL,
        name="begin",
    )(pinned(down), pinned(up), pinned(lengths), pinned(queries))


def pack_other(down, up, _, __, pair, rest):
    lanes = pair.shape[3]
    tiles = down.shape[2] // lanes
    part = plane_part()
    for i in range(tiles):
        cols = slice(i * lanes, (i + 1) * lanes)
        pair[1, i] = down[part, :, cols]
        rest[1, i] = down[1 - part, :, cols]
    columns = up_columns(up)
    pair[1, tiles, :, : columns.shape[1]] = columns


def pack(down, up, pair, rest):
    return pl.pallas_call(
        pack_other,
        out_shape=(like(pair), like(rest)),
        in_specs=[VMEM] * 4,
        out_specs=(VMEM, VMEM),
        input_output_aliases={2: 0, 3: 1},
        compiler_params=pltpu.CompilerParams(vmem_limit_bytes=2 * MIB),
        cost_estimate=TYPICAL,
        name="pack_other",
    )(down, up, pinned(pair, pltpu.VMEM), pinned(rest, pltpu.VMEM))


def attend_cache(pairs, ready, sizes, scale, *refs):
    lengths, order, q_ref, k_hbm, v_hbm = refs[:5]
    k_buf, v_buf, *outs, sems = refs[-5:]
    done = pairs[0]
    o_ref, lse_ref = outs[:2]
    steps, _, heads, size = q_ref.shape
    kv = k_hbm.shape[1] // sizes[-1]
    lanes = steps * heads

    def copies(which, pair, slots):
        span = pl.ds(0, slots * kv)
        hbm, buf = ((k_hbm, k_buf), (v_hbm, v_buf))[which]
        return [
            pltpu.make_async_copy(
                hbm.at[order[2 * pair + i], span],
                buf.at[2 * pair + i, span],
                sems.at[pair, i, which],
            )
            for i in range(2)
        ]

    def start(pair, slots):
        for copy in copies(0, pair, slots) + copies(1, pair, slots):
            copy.start()

    def finish(which, pair, slots):
        for i in which:
            for copy in copies(i, pair, slots):
                copy.wait()

    for pair in range(*ready):
        by_length(lengths[order[2 * pair]], sizes, functools.partial(start, pair))

    row_head = over(within(lax.broadcasted_iota(jnp.int32, (lanes, size), 0), heads), heads // kv)
    slot_head = within(lax.broadcasted_iota(jnp.int32, (lanes, size), 1), kv)
    head_bias = jnp.where(row_head == slot_head, 0.0, -jnp.inf)

    def attend(pair):
        def compute(slots):
            def wait(which):
                @pl.when(pair >= ready[0])
                def _():
                    finish((which,), pair, slots)

            n = slots * kv
            bias = jnp.concatenate([head_bias[:, : min(n, size)]] * max(n // size, 1), axis=1)
            column = lax.broadcasted_iota(jnp.int32, (1, n), 1)
            wait(0)
            scores = []
            for i in range(2):
                row = order[2 * pair + i]
                q = q_ref[:, row].reshape(lanes, size)
                s = lax.dot_general(
                    q,
                    k_buf[2 * pair + i, :n],
                    (((1,), (1,)), ((), ())),
                    preferred_element_type=jnp.float32,
                )
                closed = jnp.where(column < lengths[row] * kv, 0.0, -jnp.inf)
                scores.append(s + (bias + closed))
            highest = [jnp.max(s, axis=1, keepdims=True) * scale for s in scores]
            weights = [jnp.exp2(s * scale - h) for s, h in zip(scores, highest)]
            totals = [jnp.sum(p, axis=1, keepdims=True) for p in weights]
            wait(1)
            for i in range(2):
                o = jnp.dot(
                    weights[i].astype(jnp.bfloat16),
                    v_buf[2 * pair + i, :n],
                    preferred_element_type=jnp.float32,
                )
                spot = 2 * (pair - done) + i
                o_ref[spot] = o / totals[i]
                lse = highest[i] + jnp.log(totals[i]) * LOG2E
                lse_ref[spot] = jnp.broadcast_to(lse, (lanes, size))

        by_length(lengths[order[2 * pair]], sizes, compute)

    if pairs[1] - pairs[0] == 1:
        attend(pairs[0])
    else:
        pl.loop(*pairs)(attend)
    for pair in range(max(pairs[1], ready[0]), ready[1]):
        by_length(lengths[order[2 * pair]], sizes, functools.partial(finish, (0, 1), pair))


def like(x):
    return pltpu.VMEM(x.shape, x.dtype)


def cache_attention(pairs, ready, rows_args, caches, buffers, sizes, after):
    lengths, order, queries = rows_args
    keys, values = caches
    rows, steps, _, heads, size = (keys.shape[0], *queries.shape)
    slots = sizes[-1]
    scale = LOG2E / math.sqrt(size)
    count = 2 * (pairs[1] - pairs[0])
    piece = pltpu.VMEM((count, steps * heads, size), jnp.float32)
    operands = [pinned(x, pltpu.SMEM) for x in (lengths, order)]
    operands += [pinned(queries, pltpu.VMEM)]
    operands += [pinned(keys), pinned(values)]
    aliases = {len(operands) + i: i for i in range(len(buffers))}
    specs = [SMEM, SMEM, VMEM, HBM, HBM] + [VMEM] * len(buffers) + [ANY] * len(after)
    operands += [pinned(b, pltpu.VMEM) for b in buffers] + after
    out_shape = [like(keys), like(values), piece, piece]
    return pl.pallas_call(
        functools.partial(attend_cache, pairs, ready, sizes, scale),
        out_shape=out_shape,
        in_specs=specs,
        out_specs=[VMEM] * len(out_shape),
        input_output_aliases=aliases,
        scratch_shapes=[
            pltpu.SemaphoreType.DMA((rows // 2, 2, 2)),
        ],
        compiler_params=pltpu.CompilerParams(vmem_limit_bytes=8 * MIB),
        cost_estimate=TYPICAL,
        name="cache_attention",
    )(*operands)


def project_old(lay, n_hidden, *refs):
    w_buf, *hidden = refs[: 1 + n_hidden]
    out_ref, h_ref = refs[-2:]
    tp = lax.axis_index("tp")
    for i, h in enumerate(hidden):
        h_ref[lax.rem(tp + i, lay.tp)] = h[...]
    features = h_ref.shape[2]
    chunk = min(features, 1024)
    for k in range(2):
        total = jnp.zeros(out_ref.shape[1:], jnp.float32)
        for t in range(lay.tp):
            for low in range(0, features, chunk):
                start = t * features + low
                total += jnp.dot(
                    h_ref[t, :, low : low + chunk],
                    w_buf[k, start : start + chunk, :],
                    preferred_element_type=jnp.float32,
                )
        out_ref[k] = total


def project(lay, w_buf, hidden, after):
    tokens, features = hidden[0].shape
    return pl.pallas_call(
        functools.partial(project_old, lay, len(hidden)),
        out_shape=(
            pltpu.VMEM((2, tokens, w_buf.shape[2]), jnp.float32),
            pltpu.VMEM((lay.tp, tokens, features), jnp.bfloat16),
        ),
        in_specs=[VMEM] * (1 + len(hidden)) + [ANY] * len(after),
        out_specs=(VMEM, VMEM),
        compiler_params=pltpu.CompilerParams(vmem_limit_bytes=4 * MIB),
        cost_estimate=TYPICAL,
        name="project",
    )(pinned(w_buf, pltpu.VMEM), *hidden, *after)


class Place:
    def __init__(self, lay):
        fsdp, self.grp, self.tp = (lax.axis_index(a) for a in AXES)
        self.z, self.core = fsdp // 2, lax.rem(fsdp, 2)
        self.lay = lay
        there = jnp.where(lax.rem(self.grp, 2) == 0, self.z, lay.depth - 1 - self.z)
        self.own = self.grp * lay.depth + there
        self.per_lane = lay.fsdp * lay.grp // lay.tp
        self.part = plane_part()

    def find(self, plan, downs):
        lay, found = self.lay, []
        for (step, flip, other), down in zip(plan, downs):
            towards = (1 - 2 * self.core if flip else 2 * self.core - 1) * step
            spot = lax.rem(self.own + (lay.ring + towards), lay.ring)
            g = spot // lay.depth
            along = lax.rem(spot, lay.depth)
            zz = jnp.where(lax.rem(g, 2) == 0, along, lay.depth - 1 - along)
            for i in range(2):
                core = lax.rem(self.core + (i + flip), 2)
                index = (zz * 2 + core) * lay.grp + g
                found.append((down.at[i], index, 1 - self.part if other else self.part))
        return found

    def low(self, shards, h_ref, tiles):
        total = jnp.zeros((h_ref.shape[1], shards[0][0].shape[1]), jnp.float32) if shards else 0.0
        for down, index, _ in shards:
            depth = tiles * down.shape[-1]
            column = pl.multiple_of(lax.rem(index, self.per_lane) * depth, depth)
            term = lax.dot_general(
                h_ref[index // self.per_lane, :, pl.ds(column, depth)],
                jnp.concatenate([down[i] for i in range(tiles)], axis=1),
                (((1,), (1,)), ((), ())),
                preferred_element_type=jnp.float32,
            )
            total += term
        return total


def by_projection(place, plan, shards):
    crossed = [other for _, _, other in plan for _ in range(2)]
    return [
        (place.part, [s for s, other in zip(shards, crossed) if not other]),
        (1 - place.part, [s for s, other in zip(shards, crossed) if other]),
    ]


def merge_some(lay, plan, first, n_caches, scale, *refs):
    refs = list(refs)

    def take(n):
        out = refs[:n]
        del refs[:n]
        return out

    last = n_caches > 0
    downs = take(len(plan))
    h_buf, weights = take(2)
    if last:
        old, order, q_ref = take(3)
        caches = [take(2) for _ in range(n_caches)]
        u_buf, low_in, _ = take(3)
        m_hbm, out_hbm, m_buf, sems, low, out_buf, out_sem = refs[-7:]
    elif first:
        m_hbm, u_buf, low, m_buf, sems, u_parts = refs[-6:]
    else:
        u_buf, low_in, _ = take(3)
        m_hbm, low, m_buf, sems = refs[-4:]
    depth, width = m_buf.shape[1:]
    pairs = weights.shape[0]
    cut = min(width, 256)
    lanes = downs[0].shape[-1]
    tiles = depth // lanes
    place = Place(lay)
    shards = place.find(plan, downs)
    groups = by_projection(place, plan, shards)

    if last:
        low[...] = low_in[...]
        for part, group in groups:
            low[part] += place.low(group, h_buf, tiles)
        new = []
        for k in range(pairs):
            high = low[k].astype(jnp.bfloat16)
            rest = (low[k] - high.astype(jnp.float32)).astype(jnp.bfloat16)
            new.append(
                (
                    old[k]
                    + jnp.dot(high, u_buf[k], preferred_element_type=jnp.float32)
                    + jnp.dot(rest, u_buf[k], preferred_element_type=jnp.float32)
                ).astype(jnp.bfloat16)
            )
        add_new_tokens(q_ref, order, caches, new, out_buf, scale)
        out_copy = pltpu.make_async_copy(out_buf, out_hbm, out_sem)
        out_copy.start()
    elif first:
        columns = width // place.per_lane
        for down, index, _ in groups[0][1]:

            @pl.when(index // place.per_lane == place.tp)
            def _():
                u_parts[lax.rem(index, place.per_lane)] = down[tiles, :, : pairs * columns]

        for k in range(pairs):
            u_buf[k] = ADAPTER_SCALING * jnp.concatenate(
                [
                    u_parts[i, :, k * columns : (k + 1) * columns]
                    for i in range(place.per_lane)
                ],
                axis=1,
            )

    chunk = min(depth, 256)
    copies = []
    for j, (down, index, k) in enumerate(shards):
        start = pl.multiple_of(index * depth, depth)
        for begin in range(0, depth, chunk):
            rows = slice(begin, begin + chunk)
            tile = begin // lanes
            d = jnp.concatenate([down[tile + i] for i in range(chunk // lanes)], axis=1)
            for side in range(width // cut):
                cols = slice(side * cut, (side + 1) * cut)
                added = lax.dot_general(
                    d,
                    u_buf[k, :, cols],
                    (((0,), (0,)), ((), ())),
                    preferred_element_type=jnp.float32,
                )
                w = weights[k, pl.ds(start + begin, chunk), cols]
                m_buf[j, rows, cols] = (w.astype(jnp.float32) + added).astype(jnp.bfloat16)
        copy = pltpu.make_async_copy(m_buf.at[j], m_hbm.at[k, pl.ds(start, depth), :], sems.at[j])
        copy.start()
        copies.append(copy)

    if not last:
        low[...] = jnp.zeros_like(low) if first else low_in[...]
        for part, group in groups:
            low[part] += place.low(group, h_buf, tiles)
    for copy in copies + ([out_copy] if last else []):
        copy.wait()


def add_new_tokens(q_ref, order, caches, new, out_buf, scale):
    steps, rows, heads, size = q_ref.shape
    kv = new[0].shape[1] // size
    new = [
        jnp.concatenate([x[:, g * size : (g + 1) * size] for g in range(kv)], axis=0) for x in new
    ]
    n = kv * steps * rows
    lanes = steps * heads
    left = lax.broadcasted_iota(jnp.int32, (lanes, n), 0)
    right = lax.broadcasted_iota(jnp.int32, (lanes, n), 1)
    same_head = over(within(left, heads), heads // kv) == over(right, steps * rows)
    earlier = within(over(right, rows), steps) <= over(left, heads)
    right_row = jnp.where(same_head & earlier, within(right, rows), -1)

    def all_rows(pieces):
        return jnp.concatenate(list(pieces), axis=0)

    q = all_rows(q_ref[:, order[spot]].reshape(lanes, size) for spot in range(rows))
    s = lax.dot_general(q, new[0], (((1,), (1,)), ((), ())), preferred_element_type=jnp.float32)
    bias = all_rows(
        jnp.where(right_row == order[spot], 0.0, -jnp.inf) for spot in range(rows)
    )
    s = s * scale + bias
    lse = all_rows(ref[i] for _, ref in caches for i in range(ref.shape[0]))
    highest = jnp.maximum(jnp.max(s, axis=1, keepdims=True), lse)
    p = jnp.exp2(s - highest[:, :n])
    old = jnp.exp2(lse - highest)
    divisor = jnp.sum(p, axis=1, keepdims=True) + old
    o = old * all_rows(ref[i] for ref, _ in caches for i in range(ref.shape[0]))
    o = (o + jnp.dot(p.astype(jnp.bfloat16), new[1], preferred_element_type=jnp.float32)) / divisor
    for spot in range(rows):
        piece = o[spot * lanes : (spot + 1) * lanes].astype(out_buf.dtype)
        out_buf[:, order[spot]] = piece.reshape(steps, heads, size)


def merge(lay, shape, entries, states, weights, state, final, after):
    pairs, total, width = shape
    tokens, rank = states.shape[1], entries[0][3].shape[-2]
    depth = total // (lay.fsdp * lay.grp)
    per_lane = lay.fsdp * lay.grp // lay.tp
    n = 2 * len(entries)
    merged = pltpu.HBM(shape, jnp.bfloat16)
    low_shape = (pairs, tokens, rank)
    operands = [e[3] for e in entries] + [pinned(states, pltpu.VMEM), pinned(weights, pltpu.VMEM)]
    specs = [VMEM] * len(operands)
    scratch = [pltpu.VMEM((n, depth, width), jnp.bfloat16), pltpu.SemaphoreType.DMA((n,))]
    aliases = {}
    n_caches, scale = 0, 0.0
    if state is not None and final is None:
        m_prev, u_buf, low = state
        operands += [pinned(u_buf, pltpu.VMEM), pinned(low, pltpu.VMEM), pinned(m_prev)]
        specs += [VMEM, VMEM, HBM]
        aliases = {len(operands) - 1: 0}
        out_shape = [merged, pltpu.VMEM(low_shape, jnp.float32)]
        out_specs = [HBM, VMEM]
    elif final is None:
        out_shape = [
            merged,
            pltpu.VMEM((pairs, rank, width), jnp.bfloat16),
            pltpu.VMEM(low_shape, jnp.float32),
        ]
        out_specs = [HBM, VMEM, VMEM]
        scratch.append(pltpu.VMEM((per_lane, rank, pairs * width // per_lane), jnp.bfloat16))
    else:
        olds, order, queries, caches = final
        m_prev, u_buf, low = state
        operands += [olds, pinned(order, pltpu.SMEM), pinned(queries, pltpu.VMEM), *caches]
        specs += [VMEM, SMEM, VMEM] + [VMEM] * len(caches)
        operands += [pinned(u_buf, pltpu.VMEM), pinned(low, pltpu.VMEM), pinned(m_prev)]
        specs += [VMEM, VMEM, HBM]
        aliases = {len(operands) - 1: 0}
        out_shape = [merged, pltpu.HBM(queries.shape, jnp.bfloat16)]
        out_specs = [HBM, HBM]
        scratch += [
            pltpu.VMEM(low_shape, jnp.float32),
            pltpu.VMEM(queries.shape, jnp.bfloat16),
            pltpu.SemaphoreType.DMA,
        ]
        n_caches, scale = len(caches) // 2, LOG2E / math.sqrt(queries.shape[3])
    return pl.pallas_call(
        functools.partial(merge_some, lay, [e[:3] for e in entries], state is None, n_caches, scale),
        out_shape=out_shape,
        in_specs=specs + [ANY] * len(after),
        out_specs=out_specs,
        input_output_aliases=aliases,
        scratch_shapes=scratch,
        compiler_params=pltpu.CompilerParams(vmem_limit_bytes=20 * MIB),
        cost_estimate=TYPICAL,
        name="merge",
    )(*operands, *after)


def shards(
    lay,
    hidden_states,
    queries,
    cache_keys,
    cache_values,
    cache_lengths,
    projection_weight_matrices,
    factor_down,
    factor_up,
):
    send = functools.partial(lax.ppermute, axis_name=AXES)
    steps, rows, features = hidden_states.shape
    slots, kv, size = cache_keys.shape[1:]
    shape = projection_weight_matrices.shape
    sizes = tuple(slots * i // 24 for i in (1, 4, 8, 16, 24))
    own = jnp.swapaxes(factor_down, 1, 2)
    tokens = hidden_states.reshape(steps * rows, features)
    keys = cache_keys.reshape(rows, slots * kv, size)
    values = cache_values.reshape(rows, slots * kv, size)
    swap, ring, planes = lay.core_swap(), lay.ring_step(), lay.plane_swap()
    pair_count = rows // 2
    last_step = lay.ring // 2
    buffers, caches = [], []

    other, other_up = send(own, perm=swap), send(factor_up, perm=swap)
    pair, rest, *rows_args = begin(own, factor_up, cache_lengths, queries)
    pair, rest = pack(other, other_up, pair, rest)

    def attention(pairs, ready, after):
        nonlocal buffers
        out = cache_attention(pairs, ready, rows_args, (keys, values), buffers, sizes, after)
        buffers = list(out[:2])
        caches.extend(out[2:])
        return out[2]

    entries = [(0, 0, 0, pair), (0, 0, 1, rest)]
    sent = send(pair, perm=ring)
    hidden = [tokens] + [send(tokens, perm=lay.feature_step(i)) for i in range(1, lay.tp)]
    token = attention((0, 1), (0, 2), [pair])
    came, token = after_all(sent, token)
    crossing, crossed = [], []
    for step in range(1, last_step):
        entries.append((step, 0, 0, came))
        over_there = [(s, send(x, perm=swap)) for s, x in crossed]
        across = [(step, send(came, perm=planes))]
        swapped = send(came, perm=swap)
        sent = send(came, perm=ring)
        if step == 1:
            token = attention((1, 2), (2, pair_count), [token])
        elif step == 2:
            token = attention((2, pair_count), (pair_count, pair_count), [token])
        elif step == 3:
            olds, states = project(lay, projection_weight_matrices, hidden, [token])
            token = olds
        (came, hidden, arrived, swapped, held), token = after_all(
            (sent, hidden, [x for _, x in crossing], swapped, [x for _, x in over_there]), token
        )
        entries.append((step, 1, 0, swapped))
        entries += [(s, 1, 1, x) for (s, _), x in zip(over_there, held)]
        crossed = [(s, x) for (s, _), x in zip(crossing, arrived)]
        entries += [(s, 0, 1, x) for s, x in crossed]
        crossing = across
    weights = projection_weight_matrices
    entries.append((last_step, 0, 0, came))
    own_plane = [e for e in entries if not e[2]]
    others = [e for e in entries if e[2]]
    late = [(last_step, 0, 1, send(came, perm=planes))]
    late += [(s, 1, 1, send(x, perm=swap)) for s, x in crossed]
    m, u, low = merge(lay, shape, own_plane, states, weights, None, None, [token])
    (step, x), = crossing
    x, low = after_all(x, low)
    late.append((step, 1, 1, send(x, perm=swap)))
    others.append((step, 0, 1, x))
    m, low = merge(lay, shape, others, states, weights, [m, u, low], None, [])
    arrived, low = after_all([x for _, _, _, x in late], low)
    late = [(*e[:3], x) for e, x in zip(late, arrived)]
    _, order, q = rows_args
    final = (olds, order, q, caches)
    return tuple(merge(lay, shape, late, states, weights, [m, u, low], final, []))


def solution(mesh):
    return jax.shard_map(
        functools.partial(shards, Layout(mesh)),
        mesh=mesh,
        in_specs=(
            P(None, ("fsdp", "grp"), "tp"),
            P(None, ("fsdp", "grp"), "tp", None),
            P(("fsdp", "grp"), None, "tp", None),
            P(("fsdp", "grp"), None, "tp", None),
            P(("fsdp", "grp")),
            P(None, None, "tp"),
            P(None, ("fsdp", "grp"), None),
            P(None, None, ("fsdp", "grp")),
        ),
        out_specs=(P(None, None, "tp"), P(None, ("fsdp", "grp"), "tp", None)),
        check_vma=False,
    )
```

profile of v0, /device:TPU:0, one launch (start us, length us, event | category | flops | bytes accessed | tf_op | source)
XLA Modules:
  0.0 38.9 jit_solution(862461005726712142)
XLA Ops:
  0.6 0.5 %collective-permute-start = (bf16[2,64,512]{2,1,0:T(8,128)(2,1)}, bf16[2,64,512]{2,1,0:T(8,128)(2,1)S(1)}, u32[]{:S(2)}, u32[]{:S(2)}) collective-permute-start(bf16[2,64,512]{2,1,0:T(8,128)(2,1)} %bitcast.14), channel_id=1, source_target_pairs={{0,4},{1,5},{2,6},{3,7},{4,0},{5,1},{6,2},{7,3},{8,12},{9,13},{10,... | collective-permute-start | bytes 393224 | tf_op jit(solution)/shard_map/ppermute | solution.py:609
  1.1 0.1 collective-permute-start.1
  1.2 1.2 %begin.1 = (bf16[2,5,64,128]{3,2,1,0:T(8,128)(2,1)S(1)}, bf16[2,4,64,128]{3,2,1,0:T(8,128)(2,1)S(1)}, s32[8]{0:T(128)S(4)}, s32[8]{0:T(128)S(4)}, bf16[4,8,32,128]{3,2,1,0:T(8,128)(2,1)S(1)}) custom-call(bf16[2,64,512]{2,1,0:T(8,128)(2,1)} %bitcast.15, bf16[2,64,64]{2,1,0:T(8,128)(2,1)} %up.1, s32[8]{0:T(128)} %len_hbm.1, bf16[4,8,32,128]{3,2,1,0:T(8,128)(2,1)} %q_hbm.1), custom_call_target="tpu_custom_call" | custom-call | flops 600000000 | bytes 10000000 | tf_op jit(solution)/shard_map/begin/pallas_call | solution.py:147
  2.4 0.1 collective-permute-done.1.up
  2.6 0.0 collective-permute-done.down
  2.6 0.1 pack_other.1
  2.6 2.9 %collective-permute-start.2 = (bf16[2,5,64,128]{3,2,1,0:T(8,128)(2,1)S(1)}, bf16[2,5,64,128]{3,2,1,0:T(8,128)(2,1)S(1)}, u32[]{:S(2)}, u32[]{:S(2)}) collective-permute-start(bf16[2,5,64,128]{3,2,1,0:T(8,128)(2,1)S(1)} %get-tuple-element.52.refs_5_.refs_0_), channel_id=1, source_target_pairs={{0,8},{1,9},{2,0},{3,1},{4,6},{5,7},{6,14},{7,15},{8,16},{9,17},{1... | collective-permute-start | bytes 491528 | tf_op jit(solution)/shard_map/ppermute | solution.py:621
  5.6 1.5 %collective-permute-start.4 = (bf16[32,4096]{1,0:T(8,128)(2,1)}, bf16[32,4096]{1,0:T(8,128)(2,1)S(1)}, u32[]{:S(2)}, u32[]{:S(2)}) collective-permute-start(bf16[32,4096]{1,0:T(8,128)(2,1)} %bitcast.6), channel_id=1, source_target_pairs={{1,0},{0,1},{3,2},{2,3},{5,4},{4,5},{7,6},{6,7},{9,8},{8,9},{11,10... | collective-permute-start | bytes 786440 | tf_op jit(solution)/shard_map/ppermute | solution.py:622
  7.0 3.3 %cache_attention.3 = (bf16[8,3072,128]{2,1,0:T(8,128)(2,1)S(1)}, bf16[8,3072,128]{2,1,0:T(8,128)(2,1)S(1)}, f32[2,128,128]{2,1,0:T(8,128)S(1)}, f32[2,128,128]{2,1,0:T(8,128)S(1)}) custom-call(s32[8]{0:T(128)S(4)} %get-tuple-element.53.refs_0_, s32[8]{0:T(128)S(4)} %get-tuple-element.54.refs_1_.refs_6_, ...), custom_call_target="tpu_custom_call" | custom-call | flops 600000000 | bytes 10000000 | tf_op jit(solution)/shard_map/cache_attention/pallas_call | solution.py:298
  10.4 0.0 collective-permute-done.2.refs_1_
  10.4 1.6 %collective-permute-start.3 = (bf16[2,5,64,128]{3,2,1,0:T(8,128)(2,1)S(1)}, bf16[2,5,64,128]{3,2,1,0:T(8,128)(2,1)S(1)}, u32[]{:S(2)}, u32[]{:S(2)}) collective-permute-start(bf16[2,5,64,128]{3,2,1,0:T(8,128)(2,1)S(1)} %collective-permute-done.2.refs_1_), channel_id=1, source_target_pairs={{0,8},{1,9},{2,0},{3,1},{4,6},{5,7},{6,14},{7,15},{8,16},{9,17},{1... | collective-permute-start | bytes 491528 | tf_op jit(solution)/shard_map/ppermute | solution.py:631
  12.0 0.0 collective-permute-start.5
  12.0 0.5 %collective-permute-start.7 = (bf16[2,5,64,128]{3,2,1,0:T(8,128)(2,1)S(1)}, bf16[2,5,64,128]{3,2,1,0:T(8,128)(2,1)S(1)}, u32[]{:S(2)}, u32[]{:S(2)}) collective-permute-start(bf16[2,5,64,128]{3,2,1,0:T(8,128)(2,1)S(1)} %collective-permute-done.2.refs_1_), channel_id=1, source_target_pairs={{0,1},{1,0},{2,3},{3,2},{4,5},{5,4},{6,7},{7,6},{8,9},{9,8},{10,11... | collective-permute-start | bytes 491528 | tf_op jit(solution)/shard_map/ppermute | solution.py:629
  12.6 1.4 %cache_attention.4 = (bf16[8,3072,128]{2,1,0:T(8,128)(2,1)S(1)}, bf16[8,3072,128]{2,1,0:T(8,128)(2,1)S(1)}, f32[2,128,128]{2,1,0:T(8,128)S(1)}, f32[2,128,128]{2,1,0:T(8,128)S(1)}) custom-call(s32[8]{0:T(128)S(4)} %get-tuple-element.53.refs_0_, s32[8]{0:T(128)S(4)} %get-tuple-element.54.refs_1_.refs_6_, ...), custom_call_target="tpu_custom_call", output_to_operand_aliasing={{0}: (5, {}), {1}: (6, {})} | custom-call | flops 600000000 | bytes 10000000 | tf_op jit(solution)/shard_map/cache_attention/pallas_call | solution.py:298
  14.0 0.0 collective-permute-done.4.refs_2_
  14.0 1.7 %collective-permute-done.3.refs_3_ = bf16[2,5,64,128]{3,2,1,0:T(8,128)(2,1)S(1)} collective-permute-done((bf16[2,5,64,128]{3,2,1,0:T(8,128)(2,1)S(1)}, bf16[2,5,64,128]{3,2,1,0:T(8,128)(2,1)S(1)}, u32[]{:S(2)}, u32[]{:S(2)}) %collective-permute-start.3) | collective-permute-done | bytes 163872 | tf_op jit(solution)/shard_map/ppermute | solution.py:631
  15.8 0.0 collective-permute-done.5.refs_2_
  15.8 1.6 %collective-permute-start.6 = (bf16[2,5,64,128]{3,2,1,0:T(8,128)(2,1)S(1)}, bf16[2,5,64,128]{3,2,1,0:T(8,128)(2,1)S(1)}, u32[]{:S(2)}, u32[]{:S(2)}) collective-permute-start(bf16[2,5,64,128]{3,2,1,0:T(8,128)(2,1)S(1)} %collective-permute-done.3.refs_3_), channel_id=1, source_target_pairs={{0,8},{1,9},{2,0},{3,1},{4,6},{5,7},{6,14},{7,15},{8,16},{9,17},{1... | collective-permute-start | bytes 491528 | tf_op jit(solution)/shard_map/ppermute | solution.py:631
  17.3 0.0 collective-permute-start.8
  17.3 0.5 %collective-permute-start.10 = (bf16[2,5,64,128]{3,2,1,0:T(8,128)(2,1)S(1)}, bf16[2,5,64,128]{3,2,1,0:T(8,128)(2,1)S(1)}, u32[]{:S(2)}, u32[]{:S(2)}) collective-permute-start(bf16[2,5,64,128]{3,2,1,0:T(8,128)(2,1)S(1)} %collective-permute-done.3.refs_3_), channel_id=1, source_target_pairs={{0,1},{1,0},{2,3},{3,2},{4,5},{5,4},{6,7},{7,6},{8,9},{9,8},{10,11... | collective-permute-start | bytes 491528 | tf_op jit(solution)/shard_map/ppermute | solution.py:629
  17.9 1.2 %cache_attention.5 = (bf16[8,3072,128]{2,1,0:T(8,128)(2,1)S(1)}, bf16[8,3072,128]{2,1,0:T(8,128)(2,1)S(1)}, f32[4,128,128]{2,1,0:T(8,128)S(1)}, f32[4,128,128]{2,1,0:T(8,128)S(1)}) custom-call(s32[8]{0:T(128)S(4)} %get-tuple-element.53.refs_0_, s32[8]{0:T(128)S(4)} %get-tuple-element.54.refs_1_.refs_6_, ...), custom_call_target="tpu_custom_call", output_to_operand_aliasing={{0}: (5, {}), {1}: (6, {})} | custom-call | flops 600000000 | bytes 10000000 | tf_op jit(solution)/shard_map/cache_attention/pallas_call | solution.py:298
  19.1 0.0 collective-permute-done.7.refs_1_
  19.1 2.0 %collective-permute-done.6.refs_5_ = bf16[2,5,64,128]{3,2,1,0:T(8,128)(2,1)S(1)} collective-permute-done((bf16[2,5,64,128]{3,2,1,0:T(8,128)(2,1)S(1)}, bf16[2,5,64,128]{3,2,1,0:T(8,128)(2,1)S(1)}, u32[]{:S(2)}, u32[]{:S(2)}) %collective-permute-start.6) | collective-permute-done | bytes 163872 | tf_op jit(solution)/shard_map/ppermute | solution.py:631
  21.1 0.0 collective-permute-done.8.refs_4_
  21.1 0.0 collective-permute-start.11
  21.1 0.5 %collective-permute-start.12 = (bf16[2,5,64,128]{3,2,1,0:T(8,128)(2,1)S(1)}, bf16[2,5,64,128]{3,2,1,0:T(8,128)(2,1)S(1)}, u32[]{:S(2)}, u32[]{:S(2)}) collective-permute-start(bf16[2,5,64,128]{3,2,1,0:T(8,128)(2,1)S(1)} %collective-permute-done.7.refs_1_), channel_id=1, source_target_pairs={{0,4},{1,5},{2,6},{3,7},{4,0},{5,1},{6,2},{7,3},{8,12},{9,13},{10,... | collective-permute-start | bytes 491528 | tf_op jit(solution)/shard_map/ppermute | solution.py:628
  21.6 1.6 %collective-permute-start.9 = (bf16[2,5,64,128]{3,2,1,0:T(8,128)(2,1)S(1)}, bf16[2,5,64,128]{3,2,1,0:T(8,128)(2,1)S(1)}, u32[]{:S(2)}, u32[]{:S(2)}) collective-permute-start(bf16[2,5,64,128]{3,2,1,0:T(8,128)(2,1)S(1)} %collective-permute-done.6.refs_5_), channel_id=1, source_target_pairs={{0,8},{1,9},{2,0},{3,1},{4,6},{5,7},{6,14},{7,15},{8,16},{9,17},{1... | collective-permute-start | bytes 491528 | tf_op jit(solution)/shard_map/ppermute | solution.py:631
  23.2 0.5 %collective-permute-start.15 = (bf16[2,5,64,128]{3,2,1,0:T(8,128)(2,1)S(1)}, bf16[2,5,64,128]{3,2,1,0:T(8,128)(2,1)S(1)}, u32[]{:S(2)}, u32[]{:S(2)}) collective-permute-start(bf16[2,5,64,128]{3,2,1,0:T(8,128)(2,1)S(1)} %collective-permute-done.6.refs_5_), channel_id=1, source_target_pairs={{0,1},{1,0},{2,3},{3,2},{4,5},{5,4},{6,7},{7,6},{8,9},{9,8},{10,11... | collective-permute-start | bytes 491528 | tf_op jit(solution)/shard_map/ppermute | solution.py:629
  23.7 0.0 slice-done
  23.7 0.0 slice-done.1
  23.7 0.0 slice-done.2
  23.7 0.0 slice-done.3
  23.7 0.0 copy-done
  23.7 3.0 %project.1 = (f32[2,32,512]{2,1,0:T(8,128)S(1)}, bf16[2,32,4096]{2,1,0:T(8,128)(2,1)S(1)}) custom-call(bf16[2,8192,512]{2,1,0:T(8,128)(2,1)S(1)} %bitcast.5, bf16[32,4096]{1,0:T(8,128)(2,1)S(1)} %bitcast.7, bf16[32,4096]{1,0:T(8,128)(2,1)S(1)} %collective-permute-done.4.refs_2_, f32[4,128,128]{2,1,0:T(8,128)S(1)} %get-tuple-element.73.refs_3_.refs_12_), custom_call_target="tpu_custom_call" | custom-call | flops 600000000 | bytes 10000000 | tf_op jit(solution)/shard_map/project/pallas_call | solution.py:336
  26.7 0.0 collective-permute-done.10.refs_3_
  26.7 0.0 collective-permute-done.11.refs_6_
  26.7 0.0 collective-permute-done.12.refs_2_
  26.7 0.2 collective-permute-done.9.refs_7_
  26.9 1.4 %collective-permute-start.13 = (bf16[2,5,64,128]{3,2,1,0:T(8,128)(2,1)S(1)}, bf16[2,5,64,128]{3,2,1,0:T(8,128)(2,1)S(1)}, u32[]{:S(2)}, u32[]{:S(2)}) collective-permute-start(bf16[2,5,64,128]{3,2,1,0:T(8,128)(2,1)S(1)} %collective-permute-done.9.refs_7_), channel_id=1, source_target_pairs={{0,1},{1,0},{2,3},{3,2},{4,5},{5,4},{6,7},{7,6},{8,9},{9,8},{10,11... | collective-permute-start | bytes 491528 | tf_op jit(solution)/shard_map/ppermute | solution.py:651
  28.3 4.2 %merge.3 = (bf16[2,8192,512]{2,1,0:T(8,128)(2,1)}, bf16[2,64,512]{2,1,0:T(8,128)(2,1)S(1)}, f32[2,32,64]{2,1,0:T(8,128)S(1)}) custom-call(bf16[2,5,64,128]{3,2,1,0:T(8,128)(2,1)S(1)} %get-tuple-element.52.refs_5_.refs_0_, bf16[2,5,64,128]{3,2,1,0:T(8,128)(2,1)S(1)} %collective-permute-done.2.refs_1_, ...), custom_call_target="tpu_custom_call" | custom-call | flops 600000000 | bytes 10000000 | tf_op jit(solution)/shard_map/merge/pallas_call | solution.py:571
  32.5 0.0 collective-permute-done.15.refs_4_
  32.5 0.1 collective-permute-start.16
  32.6 0.5 %collective-permute-start.14 = (bf16[2,5,64,128]{3,2,1,0:T(8,128)(2,1)S(1)}, bf16[2,5,64,128]{3,2,1,0:T(8,128)(2,1)S(1)}, u32[]{:S(2)}, u32[]{:S(2)}) collective-permute-start(bf16[2,5,64,128]{3,2,1,0:T(8,128)(2,1)S(1)} %collective-permute-done.10.refs_3_), channel_id=1, source_target_pairs={{0,4},{1,5},{2,6},{3,7},{4,0},{5,1},{6,2},{7,3},{8,12},{9,13},{10,... | collective-permute-start | bytes 491528 | tf_op jit(solution)/shard_map/ppermute | solution.py:652
  33.1 2.7 %merge.4 = (bf16[2,8192,512]{2,1,0:T(8,128)(2,1)}, f32[2,32,64]{2,1,0:T(8,128)S(1)}) custom-call(bf16[2,4,64,128]{3,2,1,0:T(8,128)(2,1)S(1)} %get-tuple-element.84.refs_0_, bf16[2,5,64,128]{3,2,1,0:T(8,128)(2,1)S(1)} %collective-permute-done.7.refs_1_, bf16[2,5,64,128]{3,2,1,0:T(8,128)(2,1)S(1)} %collective-permute-done.12.refs_2_, ...), custom_call_target="tpu_custom_call", output_to_operand_aliasing={{0}: (9, {})} | custom-call | flops 600000000 | bytes 10000000 | tf_op jit(solution)/shard_map/merge/pallas_call | solution.py:571
  35.8 0.0 collective-permute-done.16.refs_2_
  35.8 0.0 collective-permute-done.13.refs_0_
  35.8 0.0 collective-permute-done.14.refs_1_
  35.8 2.9 %merge.5 = (bf16[2,8192,512]{2,1,0:T(8,128)(2,1)}, bf16[4,8,32,128]{3,2,1,0:T(8,128)(2,1)}) custom-call(bf16[2,5,64,128]{3,2,1,0:T(8,128)(2,1)S(1)} %collective-permute-done.13.refs_0_, bf16[2,5,64,128]{3,2,1,0:T(8,128)(2,1)S(1)} %collective-permute-done.14.refs_1_, ...), custom_call_target="tpu_custom_call", output_to_operand_aliasing={{0}: (16, {})} | custom-call | flops 600000000 | bytes 10000000 | tf_op jit(solution)/shard_map/merge/pallas_call | solution.py:571
  (6 shorter events, 0.0 us)
Async XLA Ops:
  0.6 1.9 %collective-permute-start = (bf16[2,64,512]{2,1,0:T(8,128)(2,1)}, bf16[2,64,512]{2,1,0:T(8,128)(2,1)S(1)}, u32[]{:S(2)}, u32[]{:S(2)}) collective-permute-start(bf16[2,64,512]{2,1,0:T(8,128)(2,1)} %bitcast.14), channel_id=1, source_target_pairs={{0,4},{1,5},{2,6},{3,7},{4,0},{5,1},{6,2},{7,3},{8,12},{9,13},{10,... | collective-permute-start | bytes 393224 | tf_op jit(solution)/shard_map/ppermute | solution.py:609
  1.1 1.4 %collective-permute-start.1 = (bf16[2,64,64]{2,1,0:T(8,128)(2,1)}, bf16[2,64,64]{2,1,0:T(8,128)(2,1)S(1)}, u32[]{:S(2)}, u32[]{:S(2)}) collective-permute-start(bf16[2,64,64]{2,1,0:T(8,128)(2,1)} %up.1), channel_id=1, source_target_pairs={{0,4},{1,5},{2,6},{3,7},{4,0},{5,1},{6,2},{7,3},{8,12},{9,13},{10,... | collective-permute-start | bytes 49160 | tf_op jit(solution)/shard_map/ppermute | solution.py:609
  2.6 7.7 %collective-permute-start.2 = (bf16[2,5,64,128]{3,2,1,0:T(8,128)(2,1)S(1)}, bf16[2,5,64,128]{3,2,1,0:T(8,128)(2,1)S(1)}, u32[]{:S(2)}, u32[]{:S(2)}) collective-permute-start(bf16[2,5,64,128]{3,2,1,0:T(8,128)(2,1)S(1)} %get-tuple-element.52.refs_5_.refs_0_), channel_id=1, source_target_pairs={{0,8},{1,9},{2,0},{3,1},{4,6},{5,7},{6,14},{7,15},{8,16},{9,17},{1... | collective-permute-start | bytes 491528 | tf_op jit(solution)/shard_map/ppermute | solution.py:621
  5.6 8.5 %collective-permute-start.4 = (bf16[32,4096]{1,0:T(8,128)(2,1)}, bf16[32,4096]{1,0:T(8,128)(2,1)S(1)}, u32[]{:S(2)}, u32[]{:S(2)}) collective-permute-start(bf16[32,4096]{1,0:T(8,128)(2,1)} %bitcast.6), channel_id=1, source_target_pairs={{1,0},{0,1},{3,2},{2,3},{5,4},{4,5},{7,6},{6,7},{9,8},{8,9},{11,10... | collective-permute-start | bytes 786440 | tf_op jit(solution)/shard_map/ppermute | solution.py:622
  10.4 5.4 %collective-permute-start.3 = (bf16[2,5,64,128]{3,2,1,0:T(8,128)(2,1)S(1)}, bf16[2,5,64,128]{3,2,1,0:T(8,128)(2,1)S(1)}, u32[]{:S(2)}, u32[]{:S(2)}) collective-permute-start(bf16[2,5,64,128]{3,2,1,0:T(8,128)(2,1)S(1)} %collective-permute-done.2.refs_1_), channel_id=1, source_target_pairs={{0,8},{1,9},{2,0},{3,1},{4,6},{5,7},{6,14},{7,15},{8,16},{9,17},{1... | collective-permute-start | bytes 491528 | tf_op jit(solution)/shard_map/ppermute | solution.py:631
  12.0 3.7 %collective-permute-start.5 = (bf16[2,5,64,128]{3,2,1,0:T(8,128)(2,1)S(1)}, bf16[2,5,64,128]{3,2,1,0:T(8,128)(2,1)S(1)}, u32[]{:S(2)}, u32[]{:S(2)}) collective-permute-start(bf16[2,5,64,128]{3,2,1,0:T(8,128)(2,1)S(1)} %collective-permute-done.2.refs_1_), channel_id=1, source_target_pairs={{0,4},{1,5},{2,6},{3,7},{4,0},{5,1},{6,2},{7,3},{8,12},{9,13},{10,... | collective-permute-start | bytes 491528 | tf_op jit(solution)/shard_map/ppermute | solution.py:630
  12.0 7.1 %collective-permute-start.7 = (bf16[2,5,64,128]{3,2,1,0:T(8,128)(2,1)S(1)}, bf16[2,5,64,128]{3,2,1,0:T(8,128)(2,1)S(1)}, u32[]{:S(2)}, u32[]{:S(2)}) collective-permute-start(bf16[2,5,64,128]{3,2,1,0:T(8,128)(2,1)S(1)} %collective-permute-done.2.refs_1_), channel_id=1, source_target_pairs={{0,1},{1,0},{2,3},{3,2},{4,5},{5,4},{6,7},{7,6},{8,9},{9,8},{10,11... | collective-permute-start | bytes 491528 | tf_op jit(solution)/shard_map/ppermute | solution.py:629
  12.6 11.2 %slice-start = ((s8[16777216]{0:T(1024)(128)(4,1)}), s8[4194304]{0:T(1024)(128)(4,1)S(1)}, s32[]{:S(2)}) async-start(s8[16777216]{0:T(1024)(128)(4,1)} %bitcast.4), calls=%async_computation | async-start | bytes 8388608
  12.6 11.2 %slice-start.1 = ((s8[16777216]{0:T(1024)(128)(4,1)}), s8[4194304]{0:T(1024)(128)(4,1)S(1)}, s32[]{:S(2)}) async-start(s8[16777216]{0:T(1024)(128)(4,1)} %bitcast.4), calls=%async_computation.1 | async-start | bytes 8388608
  15.8 8.0 %slice-start.2 = ((s8[16777216]{0:T(1024)(128)(4,1)}), s8[4194304]{0:T(1024)(128)(4,1)S(1)}, s32[]{:S(2)}) async-start(s8[16777216]{0:T(1024)(128)(4,1)} %bitcast.4), calls=%async_computation.2 | async-start | bytes 8388608
  15.8 5.3 %collective-permute-start.6 = (bf16[2,5,64,128]{3,2,1,0:T(8,128)(2,1)S(1)}, bf16[2,5,64,128]{3,2,1,0:T(8,128)(2,1)S(1)}, u32[]{:S(2)}, u32[]{:S(2)}) collective-permute-start(bf16[2,5,64,128]{3,2,1,0:T(8,128)(2,1)S(1)} %collective-permute-done.3.refs_3_), channel_id=1, source_target_pairs={{0,8},{1,9},{2,0},{3,1},{4,6},{5,7},{6,14},{7,15},{8,16},{9,17},{1... | collective-permute-start | bytes 491528 | tf_op jit(solution)/shard_map/ppermute | solution.py:631
  17.3 3.7 %collective-permute-start.8 = (bf16[2,5,64,128]{3,2,1,0:T(8,128)(2,1)S(1)}, bf16[2,5,64,128]{3,2,1,0:T(8,128)(2,1)S(1)}, u32[]{:S(2)}, u32[]{:S(2)}) collective-permute-start(bf16[2,5,64,128]{3,2,1,0:T(8,128)(2,1)S(1)} %collective-permute-done.3.refs_3_), channel_id=1, source_target_pairs={{0,4},{1,5},{2,6},{3,7},{4,0},{5,1},{6,2},{7,3},{8,12},{9,13},{10,... | collective-permute-start | bytes 491528 | tf_op jit(solution)/shard_map/ppermute | solution.py:630
  17.3 9.4 %collective-permute-start.10 = (bf16[2,5,64,128]{3,2,1,0:T(8,128)(2,1)S(1)}, bf16[2,5,64,128]{3,2,1,0:T(8,128)(2,1)S(1)}, u32[]{:S(2)}, u32[]{:S(2)}) collective-permute-start(bf16[2,5,64,128]{3,2,1,0:T(8,128)(2,1)S(1)} %collective-permute-done.3.refs_3_), channel_id=1, source_target_pairs={{0,1},{1,0},{2,3},{3,2},{4,5},{5,4},{6,7},{7,6},{8,9},{9,8},{10,11... | collective-permute-start | bytes 491528 | tf_op jit(solution)/shard_map/ppermute | solution.py:629
  17.9 5.8 %slice-start.3 = ((s8[16777216]{0:T(1024)(128)(4,1)}), s8[4194304]{0:T(1024)(128)(4,1)S(1)}, s32[]{:S(2)}) async-start(s8[16777216]{0:T(1024)(128)(4,1)} %bitcast.4), calls=%async_computation.3 | async-start | bytes 8388608
  17.9 5.8 %copy-start = (bf16[4,8,4096]{2,1,0:T(8,128)(2,1)S(1)}, bf16[4,8,4096]{2,1,0:T(8,128)(2,1)}, u32[]{:S(2)}) copy-start(bf16[4,8,4096]{2,1,0:T(8,128)(2,1)} %param.8) | copy-start | bytes 786436
  21.1 5.6 %collective-permute-start.11 = (bf16[2,5,64,128]{3,2,1,0:T(8,128)(2,1)S(1)}, bf16[2,5,64,128]{3,2,1,0:T(8,128)(2,1)S(1)}, u32[]{:S(2)}, u32[]{:S(2)}) collective-permute-start(bf16[2,5,64,128]{3,2,1,0:T(8,128)(2,1)S(1)} %collective-permute-done.6.refs_5_), channel_id=1, source_target_pairs={{0,4},{1,5},{2,6},{3,7},{4,0},{5,1},{6,2},{7,3},{8,12},{9,13},{10,... | collective-permute-start | bytes 491528 | tf_op jit(solution)/shard_map/ppermute | solution.py:630
  21.1 5.6 %collective-permute-start.12 = (bf16[2,5,64,128]{3,2,1,0:T(8,128)(2,1)S(1)}, bf16[2,5,64,128]{3,2,1,0:T(8,128)(2,1)S(1)}, u32[]{:S(2)}, u32[]{:S(2)}) collective-permute-start(bf16[2,5,64,128]{3,2,1,0:T(8,128)(2,1)S(1)} %collective-permute-done.7.refs_1_), channel_id=1, source_target_pairs={{0,4},{1,5},{2,6},{3,7},{4,0},{5,1},{6,2},{7,3},{8,12},{9,13},{10,... | collective-permute-start | bytes 491528 | tf_op jit(solution)/shard_map/ppermute | solution.py:628
  21.6 5.3 %collective-permute-start.9 = (bf16[2,5,64,128]{3,2,1,0:T(8,128)(2,1)S(1)}, bf16[2,5,64,128]{3,2,1,0:T(8,128)(2,1)S(1)}, u32[]{:S(2)}, u32[]{:S(2)}) collective-permute-start(bf16[2,5,64,128]{3,2,1,0:T(8,128)(2,1)S(1)} %collective-permute-done.6.refs_5_), channel_id=1, source_target_pairs={{0,8},{1,9},{2,0},{3,1},{4,6},{5,7},{6,14},{7,15},{8,16},{9,17},{1... | collective-permute-start | bytes 491528 | tf_op jit(solution)/shard_map/ppermute | solution.py:631
  23.2 9.3 %collective-permute-start.15 = (bf16[2,5,64,128]{3,2,1,0:T(8,128)(2,1)S(1)}, bf16[2,5,64,128]{3,2,1,0:T(8,128)(2,1)S(1)}, u32[]{:S(2)}, u32[]{:S(2)}) collective-permute-start(bf16[2,5,64,128]{3,2,1,0:T(8,128)(2,1)S(1)} %collective-permute-done.6.refs_5_), channel_id=1, source_target_pairs={{0,1},{1,0},{2,3},{3,2},{4,5},{5,4},{6,7},{7,6},{8,9},{9,8},{10,11... | collective-permute-start | bytes 491528 | tf_op jit(solution)/shard_map/ppermute | solution.py:629
  26.9 8.9 %collective-permute-start.13 = (bf16[2,5,64,128]{3,2,1,0:T(8,128)(2,1)S(1)}, bf16[2,5,64,128]{3,2,1,0:T(8,128)(2,1)S(1)}, u32[]{:S(2)}, u32[]{:S(2)}) collective-permute-start(bf16[2,5,64,128]{3,2,1,0:T(8,128)(2,1)S(1)} %collective-permute-done.9.refs_7_), channel_id=1, source_target_pairs={{0,1},{1,0},{2,3},{3,2},{4,5},{5,4},{6,7},{7,6},{8,9},{9,8},{10,11... | collective-permute-start | bytes 491528 | tf_op jit(solution)/shard_map/ppermute | solution.py:651
  32.5 3.3 %collective-permute-start.16 = (bf16[2,5,64,128]{3,2,1,0:T(8,128)(2,1)S(1)}, bf16[2,5,64,128]{3,2,1,0:T(8,128)(2,1)S(1)}, u32[]{:S(2)}, u32[]{:S(2)}) collective-permute-start(bf16[2,5,64,128]{3,2,1,0:T(8,128)(2,1)S(1)} %collective-permute-done.15.refs_4_), channel_id=1, source_target_pairs={{0,4},{1,5},{2,6},{3,7},{4,0},{5,1},{6,2},{7,3},{8,12},{9,13},{10,... | collective-permute-start | bytes 491528 | tf_op jit(solution)/shard_map/ppermute | solution.py:656
  32.6 3.3 %collective-permute-start.14 = (bf16[2,5,64,128]{3,2,1,0:T(8,128)(2,1)S(1)}, bf16[2,5,64,128]{3,2,1,0:T(8,128)(2,1)S(1)}, u32[]{:S(2)}, u32[]{:S(2)}) collective-permute-start(bf16[2,5,64,128]{3,2,1,0:T(8,128)(2,1)S(1)} %collective-permute-done.10.refs_3_), channel_id=1, source_target_pairs={{0,4},{1,5},{2,6},{3,7},{4,0},{5,1},{6,2},{7,3},{8,12},{9,13},{10,... | collective-permute-start | bytes 491528 | tf_op jit(solution)/shard_map/ppermute | solution.py:652
where the time goes:
time: 39.1 us; the launch traced here: 38.9 us
  Pallas kernels  20 us (51%)
  starting transfers between devices  13.9 us (36%)
  waiting for transfers between devices  4.06 us (10%)
  between operations  0.97 us (2%)
    pallas_call x3, Pallas kernels, merge(): pl.pallas_call(functools.partial(merge_some, lay, [e[:3] for e in entries...  9.78 us
    pallas_call x3, Pallas kernels, cache_attention(): pl.pallas_call(functools.partial(attend_cache, pairs, ready, sizes, scale...  5.98 us
    ppermute x3, starting transfers between devices, shards(): sent = send(came, perm=ring)  4.79 us
    ppermute x3, waiting for transfers between devices, shards(): sent = send(came, perm=ring)  3.88 us
    pallas_call x1, Pallas kernels, project(): pl.pallas_call(functools.partial(project_old, lay, len(hidden)), out_shap...  2.96 us
    ppermute x1, starting transfers between devices, shards(): sent = send(pair, perm=ring)  2.91 us
    ppermute x3, starting transfers between devices, shards(): across = [(step, send(came, perm=planes))]  1.61 us
    ppermute x1, starting transfers between devices, shards(): send(tokens, perm=lay.feature_step(i))  1.49 us
  transfers between devices with their start and end apart: 17, of which 4 were waited for; matrix products, arithmetic and copies ran while one was open for 0% of the time, Pallas kernels for 44%

commit v1 on v0

--- a/solution.py
+++ b/solution.py
@@ -310,41 +310,45 @@
     )(*operands)
 
 
-def project_old(lay, n_hidden, *refs):
-    w_buf, *hidden = refs[: 1 + n_hidden]
-    out_ref, h_ref = refs[-2:]
-    tp = lax.axis_index("tp")
-    for i, h in enumerate(hidden):
-        h_ref[lax.rem(tp + i, lay.tp)] = h[...]
+def project_old(part, lay, n_hidden, *refs):
+    w_ref = refs[0]
+    if part == 0:
+        out_ref, h_ref = refs[-2:]
+        tp = lax.axis_index("tp")
+        for i, h in enumerate(refs[1 : 1 + n_hidden]):
+            h_ref[lax.rem(tp + i, lay.tp)] = h[...]
+    else:
+        h_ref, out_ref = refs[1], refs[-1]
     features = h_ref.shape[2]
     chunk = min(features, 1024)
-    for k in range(2):
-        total = jnp.zeros(out_ref.shape[1:], jnp.float32)
-        for t in range(lay.tp):
-            for low in range(0, features, chunk):
-                start = t * features + low
-                total += jnp.dot(
-                    h_ref[t, :, low : low + chunk],
-                    w_buf[k, start : start + chunk, :],
-                    preferred_element_type=jnp.float32,
-                )
-        out_ref[k] = total
-
-
-def project(lay, w_buf, hidden, after):
-    tokens, features = hidden[0].shape
+    total = jnp.zeros(out_ref.shape, jnp.float32)
+    for t in range(lay.tp):
+        for low in range(0, features, chunk):
+            start = t * features + low
+            total += jnp.dot(
+                h_ref[t, :, low : low + chunk],
+                w_ref[part, start : start + chunk, :],
+                preferred_element_type=jnp.float32,
+            )
+    out_ref[...] = total
+
+
+def project(part, lay, weights, hidden, after):
+    tokens, features = hidden[0].shape[-2:]
+    out_shape = [pltpu.VMEM((tokens, weights.shape[2]), jnp.float32)]
+    if part == 0:
+        out_shape.append(pltpu.VMEM((lay.tp, tokens, features), jnp.bfloat16))
+    else:
+        hidden = [pinned(h, pltpu.VMEM) for h in hidden]
     return pl.pallas_call(
-        functools.partial(project_old, lay, len(hidden)),
-        out_shape=(
-            pltpu.VMEM((2, tokens, w_buf.shape[2]), jnp.float32),
-            pltpu.VMEM((lay.tp, tokens, features), jnp.bfloat16),
-        ),
+        functools.partial(project_old, part, lay, len(hidden)),
+        out_shape=out_shape,
         in_specs=[VMEM] * (1 + len(hidden)) + [ANY] * len(after),
-        out_specs=(VMEM, VMEM),
+        out_specs=[VMEM] * len(out_shape),
         compiler_params=pltpu.CompilerParams(vmem_limit_bytes=4 * MIB),
         cost_estimate=TYPICAL,
         name="project",
-    )(pinned(w_buf, pltpu.VMEM), *hidden, *after)
+    )(pinned(weights, pltpu.VMEM), *hidden, *after)
 
 
 class Place:
@@ -394,7 +398,26 @@
     ]
 
 
-def merge_some(lay, plan, first, n_caches, scale, *refs):
+def low_some(lay, plan, tiles, *refs):
+    downs, h_ref, out_ref = refs[: len(plan)], refs[len(plan)], refs[-1]
+    place = Place(lay)
+    for part, group in by_projection(place, plan, place.find(plan, downs)):
+        out_ref[part] = place.low(group, h_ref, tiles)
+
+
+def project_low(lay, entries, states, pairs, tiles, after):
+    return pl.pallas_call(
+        functools.partial(low_some, lay, [e[:3] for e in entries], tiles),
+        out_shape=pltpu.VMEM((pairs, states.shape[1], entries[0][3].shape[-2]), jnp.float32),
+        in_specs=[VMEM] * (len(entries) + 1) + [ANY] * len(after),
+        out_specs=VMEM,
+        compiler_params=pltpu.CompilerParams(vmem_limit_bytes=2 * MIB),
+        cost_estimate=TYPICAL,
+        name="project_low",
+    )(*[e[3] for e in entries], pinned(states, pltpu.VMEM), *after)
+
+
+def merge_some(lay, plan, has_low, first, n_caches, scale, *refs):
     refs = list(refs)
 
     def take(n):
@@ -406,11 +429,13 @@
     downs = take(len(plan))
     h_buf, weights = take(2)
     if last:
-        old, order, q_ref = take(3)
+        old = take(2)
+        order, q_ref = take(2)
         caches = [take(2) for _ in range(n_caches)]
         u_buf, low_in, _ = take(3)
         m_hbm, out_hbm, m_buf, sems, low, out_buf, out_sem = refs[-7:]
     elif first:
+        (low_in,) = take(1)
         m_hbm, u_buf, low, m_buf, sems, u_parts = refs[-6:]
     else:
         u_buf, low_in, _ = take(3)
@@ -434,7 +459,7 @@
             rest = (low[k] - high.astype(jnp.float32)).astype(jnp.bfloat16)
             new.append(
                 (
-                    old[k]
+                    old[k][...]
                     + jnp.dot(high, u_buf[k], preferred_element_type=jnp.float32)
                     + jnp.dot(rest, u_buf[k], preferred_element_type=jnp.float32)
                 ).astype(jnp.bfloat16)
@@ -482,9 +507,14 @@
         copies.append(copy)
 
     if not last:
-        low[...] = jnp.zeros_like(low) if first else low_in[...]
-        for part, group in groups:
-            low[part] += place.low(group, h_buf, tiles)
+        low[...] = low_in[...]
+        for part, group in by_projection(
+            place,
+            [e for e, done in zip(plan, has_low) if not done],
+            [s for i, s in enumerate(shards) if not has_low[i // 2]],
+        ):
+            if group:
+                low[part] += place.low(group, h_buf, tiles)
     for copy in copies + ([out_copy] if last else []):
         copy.wait()
 
@@ -524,7 +554,7 @@
         out_buf[:, order[spot]] = piece.reshape(steps, heads, size)
 
 
-def merge(lay, shape, entries, states, weights, state, final, after):
+def merge(lay, shape, entries, has_low, states, weights, state, final, after):
     pairs, total, width = shape
     tokens, rank = states.shape[1], entries[0][3].shape[-2]
     depth = total // (lay.fsdp * lay.grp)
@@ -537,7 +567,7 @@
     scratch = [pltpu.VMEM((n, depth, width), jnp.bfloat16), pltpu.SemaphoreType.DMA((n,))]
     aliases = {}
     n_caches, scale = 0, 0.0
-    if state is not None and final is None:
+    if isinstance(state, list) and final is None:
         m_prev, u_buf, low = state
         operands += [pinned(u_buf, pltpu.VMEM), pinned(low, pltpu.VMEM), pinned(m_prev)]
         specs += [VMEM, VMEM, HBM]
@@ -545,6 +575,8 @@
         out_shape = [merged, pltpu.VMEM(low_shape, jnp.float32)]
         out_specs = [HBM, VMEM]
     elif final is None:
+        operands.append(pinned(state, pltpu.VMEM))
+        specs.append(VMEM)
         out_shape = [
             merged,
             pltpu.VMEM((pairs, rank, width), jnp.bfloat16),
@@ -555,8 +587,8 @@
     else:
         olds, order, queries, caches = final
         m_prev, u_buf, low = state
-        operands += [olds, pinned(order, pltpu.SMEM), pinned(queries, pltpu.VMEM), *caches]
-        specs += [VMEM, SMEM, VMEM] + [VMEM] * len(caches)
+        operands += [*olds, pinned(order, pltpu.SMEM), pinned(queries, pltpu.VMEM), *caches]
+        specs += [VMEM, VMEM, SMEM, VMEM] + [VMEM] * len(caches)
         operands += [pinned(u_buf, pltpu.VMEM), pinned(low, pltpu.VMEM), pinned(m_prev)]
         specs += [VMEM, VMEM, HBM]
         aliases = {len(operands) - 1: 0}
@@ -569,7 +601,15 @@
         ]
         n_caches, scale = len(caches) // 2, LOG2E / math.sqrt(queries.shape[3])
     return pl.pallas_call(
-        functools.partial(merge_some, lay, [e[:3] for e in entries], state is None, n_caches, scale),
+        functools.partial(
+            merge_some,
+            lay,
+            [e[:3] for e in entries],
+            has_low,
+            not isinstance(state, list),
+            n_caches,
+            scale,
+        ),
         out_shape=out_shape,
         in_specs=specs + [ANY] * len(after),
         out_specs=out_specs,
@@ -633,9 +673,14 @@
             token = attention((1, 2), (2, pair_count), [token])
         elif step == 2:
             token = attention((2, pair_count), (pair_count, pair_count), [token])
+            old_keys, states = project(0, lay, projection_weight_matrices, hidden, [token])
+            token = old_keys
         elif step == 3:
-            olds, states = project(lay, projection_weight_matrices, hidden, [token])
-            token = olds
+            (token,) = project(1, lay, projection_weight_matrices, [states], [token])
+            olds = [old_keys, token]
+            n_low = len(entries)
+            tiles = own.shape[2] // 128
+            token = low = project_low(lay, entries, states, shape[0], tiles, [token])
         (came, hidden, arrived, swapped, held), token = after_all(
             (sent, hidden, [x for _, x in crossing], swapped, [x for _, x in over_there]), token
         )
@@ -646,21 +691,26 @@
         crossing = across
     weights = projection_weight_matrices
     entries.append((last_step, 0, 0, came))
-    own_plane = [e for e in entries if not e[2]]
-    others = [e for e in entries if e[2]]
+    own_plane = [i for i, e in enumerate(entries) if not e[2]]
+    others = [i for i, e in enumerate(entries) if e[2]]
+
+    def some(chosen):
+        return [entries[i] for i in chosen], [i < n_low for i in chosen]
+
     late = [(last_step, 0, 1, send(came, perm=planes))]
     late += [(s, 1, 1, send(x, perm=swap)) for s, x in crossed]
-    m, u, low = merge(lay, shape, own_plane, states, weights, None, None, [token])
+    m, u, low = merge(lay, shape, *some(own_plane), states, weights, low, None, [token])
     (step, x), = crossing
     x, low = after_all(x, low)
     late.append((step, 1, 1, send(x, perm=swap)))
-    others.append((step, 0, 1, x))
-    m, low = merge(lay, shape, others, states, weights, [m, u, low], None, [])
+    others.append(len(entries))
+    entries.append((step, 0, 1, x))
+    m, low = merge(lay, shape, *some(others), states, weights, [m, u, low], None, [])
     arrived, low = after_all([x for _, _, _, x in late], low)
     late = [(*e[:3], x) for e, x in zip(late, arrived)]
     _, order, q = rows_args
     final = (olds, order, q, caches)
-    return tuple(merge(lay, shape, late, states, weights, [m, u, low], final, []))
+    return tuple(merge(lay, shape, late, None, states, weights, [m, u, low], final, []))
 
 
 def solution(mesh):

time: 39.1 us -> 39.5 us (1.010)
  waiting for transfers between devices: 4.06 us -> 2.51 us
  local copies, waits for them, and re-layouts: 0.02 us -> 1.02 us
  starting transfers between devices: 13.9 us -> 14.3 us
    ppermute x3, starting transfers between devices: 1.61 us -> 3.44 us  [shards(): across = [(step, send(came, perm=planes))]]
    ppermute x3, waiting for transfers between devices: 3.88 us -> 2.06 us  [shards(): sent = send(came, perm=ring)]
    ppermute x3, starting transfers between devices: 4.79 us -> 3.66 us  [shards(): sent = send(came, perm=ring)]
    unnamed x10, local copies, waits for them, and re-layouts: 0.02 us -> 1.02 us
    pallas_call x1 -> x3, Pallas kernels: 2.96 us -> 3.48 us  [the longest x2 3.04 us: project(): pl.pallas_call(functools.partial(project_old, part, lay, len(hidden)), ou...]
where the time goes in v1:
time: 39.5 us; the launch traced here: 39 us
  Pallas kernels  20.2 us (51%)
  starting transfers between devices  14.3 us (36%)
  waiting for transfers between devices  2.51 us (6%)
  local copies, waits for them, and re-layouts  1.02 us (3%)
  between operations  1 us (3%)
    pallas_call x3, Pallas kernels, merge(): pl.pallas_call(functools.partial(merge_some, lay, [e[:3] for e in entries...  9.77 us
    pallas_call x3, Pallas kernels, cache_attention(): pl.pallas_call(functools.partial(attend_cache, pairs, ready, sizes, scale...  5.72 us
    ppermute x3, starting transfers between devices, shards(): sent = send(came, perm=ring)  3.66 us
    ppermute x3, starting transfers between devices, shards(): across = [(step, send(came, perm=planes))]  3.44 us
    pallas_call x2, Pallas kernels, project(): pl.pallas_call(functools.partial(project_old, part, lay, len(hidden)), ou...  3.04 us
    ppermute x1, starting transfers between devices, shards(): sent = send(pair, perm=ring)  2.91 us
    ppermute x3, waiting for transfers between devices, shards(): sent = send(came, perm=ring)  2.06 us
    ppermute x1, starting transfers between devices, shards(): send(tokens, perm=lay.feature_step(i))  1.49 us
  transfers between devices with their start and end apart: 17, of which 4 were waited for; matrix products, arithmetic and copies ran while one was open for 0% of the time, Pallas kernels for 44%

profile of v1, /device:TPU:0, one launch (start us, length us, event | category | flops | bytes accessed | tf_op | source)
XLA Modules:
  0.0 39.0 jit_solution(14932077513977985018)
XLA Ops:
  0.6 0.5 %collective-permute-start = (bf16[2,64,512]{2,1,0:T(8,128)(2,1)}, bf16[2,64,512]{2,1,0:T(8,128)(2,1)S(1)}, u32[]{:S(2)}, u32[]{:S(2)}) collective-permute-start(bf16[2,64,512]{2,1,0:T(8,128)(2,1)} %bitcast.14), channel_id=1, source_target_pairs={{0,4},{1,5},{2,6},{3,7},{4,0},{5,1},{6,2},{7,3},{8,12},{9,13},{10,... | collective-permute-start | bytes 393224 | tf_op jit(solution)/shard_map/ppermute | solution.py:649
  1.1 0.1 collective-permute-start.1
  1.2 1.2 %begin.1 = (bf16[2,5,64,128]{3,2,1,0:T(8,128)(2,1)S(1)}, bf16[2,4,64,128]{3,2,1,0:T(8,128)(2,1)S(1)}, s32[8]{0:T(128)S(4)}, s32[8]{0:T(128)S(4)}, bf16[4,8,32,128]{3,2,1,0:T(8,128)(2,1)S(1)}) custom-call(bf16[2,64,512]{2,1,0:T(8,128)(2,1)} %bitcast.15, bf16[2,64,64]{2,1,0:T(8,128)(2,1)} %up.1, s32[8]{0:T(128)} %len_hbm.1, bf16[4,8,32,128]{3,2,1,0:T(8,128)(2,1)} %q_hbm.1), custom_call_target="tpu_custom_call" | custom-call | flops 600000000 | bytes 10000000 | tf_op jit(solution)/shard_map/begin/pallas_call | solution.py:147
  2.4 0.1 collective-permute-done.1.up
  2.6 0.0 collective-permute-done.down
  2.6 0.1 pack_other.1
  2.6 2.9 %collective-permute-start.2 = (bf16[2,5,64,128]{3,2,1,0:T(8,128)(2,1)S(1)}, bf16[2,5,64,128]{3,2,1,0:T(8,128)(2,1)S(1)}, u32[]{:S(2)}, u32[]{:S(2)}) collective-permute-start(bf16[2,5,64,128]{3,2,1,0:T(8,128)(2,1)S(1)} %get-tuple-element.50.refs_5_.refs_0_), channel_id=1, source_target_pairs={{0,8},{1,9},{2,0},{3,1},{4,6},{5,7},{6,14},{7,15},{8,16},{9,17},{1... | collective-permute-start | bytes 491528 | tf_op jit(solution)/shard_map/ppermute | solution.py:661
  5.6 1.5 %collective-permute-start.4 = (bf16[32,4096]{1,0:T(8,128)(2,1)}, bf16[32,4096]{1,0:T(8,128)(2,1)S(1)}, u32[]{:S(2)}, u32[]{:S(2)}) collective-permute-start(bf16[32,4096]{1,0:T(8,128)(2,1)} %bitcast.6), channel_id=1, source_target_pairs={{1,0},{0,1},{3,2},{2,3},{5,4},{4,5},{7,6},{6,7},{9,8},{8,9},{11,10... | collective-permute-start | bytes 786440 | tf_op jit(solution)/shard_map/ppermute | solution.py:662
  7.0 3.3 %cache_attention.3 = (bf16[8,3072,128]{2,1,0:T(8,128)(2,1)S(1)}, bf16[8,3072,128]{2,1,0:T(8,128)(2,1)S(1)}, f32[2,128,128]{2,1,0:T(8,128)S(1)}, f32[2,128,128]{2,1,0:T(8,128)S(1)}) custom-call(s32[8]{0:T(128)S(4)} %get-tuple-element.51.refs_0_, s32[8]{0:T(128)S(4)} %get-tuple-element.52.refs_1_.refs_7_, ...), custom_call_target="tpu_custom_call" | custom-call | flops 600000000 | bytes 10000000 | tf_op jit(solution)/shard_map/cache_attention/pallas_call | solution.py:298
  10.4 0.0 collective-permute-done.2.refs_2_.refs_1_
  10.4 1.0 %collective-permute-start.3 = (bf16[2,5,64,128]{3,2,1,0:T(8,128)(2,1)S(1)}, bf16[2,5,64,128]{3,2,1,0:T(8,128)(2,1)S(1)}, u32[]{:S(2)}, u32[]{:S(2)}) collective-permute-start(bf16[2,5,64,128]{3,2,1,0:T(8,128)(2,1)S(1)} %collective-permute-done.2.refs_2_.refs_1_), channel_id=1, source_target_pairs={{0,8},{1,9},{2,0},{3,1},{4,6},{5,7},{6,14},{7,15},{8,16},{9,17},{1... | collective-permute-start | bytes 491528 | tf_op jit(solution)/shard_map/ppermute | solution.py:671
  11.4 0.0 collective-permute-start.5
  11.4 1.0 %collective-permute-start.7 = (bf16[2,5,64,128]{3,2,1,0:T(8,128)(2,1)S(1)}, bf16[2,5,64,128]{3,2,1,0:T(8,128)(2,1)S(1)}, u32[]{:S(2)}, u32[]{:S(2)}) collective-permute-start(bf16[2,5,64,128]{3,2,1,0:T(8,128)(2,1)S(1)} %collective-permute-done.2.refs_2_.refs_1_), channel_id=1, source_target_pairs={{0,1},{1,0},{2,3},{3,2},{4,5},{5,4},{6,7},{7,6},{8,9},{9,8},{10,11... | collective-permute-start | bytes 491528 | tf_op jit(solution)/shard_map/ppermute | solution.py:669
  12.4 1.2 %cache_attention.4 = (bf16[8,3072,128]{2,1,0:T(8,128)(2,1)S(1)}, bf16[8,3072,128]{2,1,0:T(8,128)(2,1)S(1)}, f32[2,128,128]{2,1,0:T(8,128)S(1)}, f32[2,128,128]{2,1,0:T(8,128)S(1)}) custom-call(s32[8]{0:T(128)S(4)} %get-tuple-element.51.refs_0_, s32[8]{0:T(128)S(4)} %get-tuple-element.52.refs_1_.refs_7_, ...), custom_call_target="tpu_custom_call", output_to_operand_aliasing={{0}: (5, {}), {1}: (6, {})} | custom-call | flops 600000000 | bytes 10000000 | tf_op jit(solution)/shard_map/cache_attention/pallas_call | solution.py:298
  13.6 0.3 collective-permute-done.4.refs_2_
  13.8 1.9 %collective-permute-done.3.refs_4_.refs_3_ = bf16[2,5,64,128]{3,2,1,0:T(8,128)(2,1)S(1)} collective-permute-done((bf16[2,5,64,128]{3,2,1,0:T(8,128)(2,1)S(1)}, bf16[2,5,64,128]{3,2,1,0:T(8,128)(2,1)S(1)}, u32[]{:S(2)}, u32[]{:S(2)}) %collective-permute-start.3) | collective-permute-done | bytes 163872 | tf_op jit(solution)/shard_map/ppermute | solution.py:671
  15.8 0.0 collective-permute-done.5.refs_3_.refs_2_
  15.8 1.0 %collective-permute-start.6 = (bf16[2,5,64,128]{3,2,1,0:T(8,128)(2,1)S(1)}, bf16[2,5,64,128]{3,2,1,0:T(8,128)(2,1)S(1)}, u32[]{:S(2)}, u32[]{:S(2)}) collective-permute-start(bf16[2,5,64,128]{3,2,1,0:T(8,128)(2,1)S(1)} %collective-permute-done.3.refs_4_.refs_3_), channel_id=1, source_target_pairs={{0,8},{1,9},{2,0},{3,1},{4,6},{5,7},{6,14},{7,15},{8,16},{9,17},{1... | collective-permute-start | bytes 491528 | tf_op jit(solution)/shard_map/ppermute | solution.py:671
  16.7 0.0 collective-permute-start.8
  16.7 1.0 %collective-permute-start.10 = (bf16[2,5,64,128]{3,2,1,0:T(8,128)(2,1)S(1)}, bf16[2,5,64,128]{3,2,1,0:T(8,128)(2,1)S(1)}, u32[]{:S(2)}, u32[]{:S(2)}) collective-permute-start(bf16[2,5,64,128]{3,2,1,0:T(8,128)(2,1)S(1)} %collective-permute-done.3.refs_4_.refs_3_), channel_id=1, source_target_pairs={{0,1},{1,0},{2,3},{3,2},{4,5},{5,4},{6,7},{7,6},{8,9},{9,8},{10,11... | collective-permute-start | bytes 491528 | tf_op jit(solution)/shard_map/ppermute | solution.py:669
  17.7 1.2 %cache_attention.5 = (bf16[8,3072,128]{2,1,0:T(8,128)(2,1)S(1)}, bf16[8,3072,128]{2,1,0:T(8,128)(2,1)S(1)}, f32[4,128,128]{2,1,0:T(8,128)S(1)}, f32[4,128,128]{2,1,0:T(8,128)S(1)}) custom-call(s32[8]{0:T(128)S(4)} %get-tuple-element.51.refs_0_, s32[8]{0:T(128)S(4)} %get-tuple-element.52.refs_1_.refs_7_, ...), custom_call_target="tpu_custom_call", output_to_operand_aliasing={{0}: (5, {}), {1}: (6, {})} | custom-call | flops 600000000 | bytes 10000000 | tf_op jit(solution)/shard_map/cache_attention/pallas_call | solution.py:298
  18.9 0.0 slice-done
  18.9 0.0 slice-done.1
  19.0 1.0 %slice-done.3 = s8[4194304]{0:T(1024)(128)(4,1)S(1)} async-done(((s8[16777216]{0:T(1024)(128)(4,1)}), s8[4194304]{0:T(1024)(128)(4,1)S(1)}, s32[]{:S(2)}) %slice-start.3) | async-done | bytes 4194328
  20.0 1.5 %project.2 = (f32[32,512]{1,0:T(8,128)S(1)}, bf16[2,32,4096]{2,1,0:T(8,128)(2,1)S(1)}) custom-call(bf16[2,8192,512]{2,1,0:T(8,128)(2,1)S(1)} %bitcast.5, bf16[32,4096]{1,0:T(8,128)(2,1)S(1)} %bitcast.7, bf16[32,4096]{1,0:T(8,128)(2,1)S(1)} %collective-permute-done.4.refs_2_, f32[4,128,128]{2,1,0:T(8,128)S(1)} %get-tuple-element.66.refs_3_.refs_13_), custom_call_target="tpu_custom_call" | custom-call | flops 600000000 | bytes 10000000 | tf_op jit(solution)/shard_map/project/pallas_call | solution.py:343
  21.5 0.0 collective-permute-done.7.refs_6_.refs_1_
  21.5 0.0 collective-permute-done.6.refs_7_.refs_5_
  21.5 0.0 collective-permute-done.8.refs_5_.refs_4_
  21.5 0.2 collective-permute-start.11
  21.8 0.3 collective-permute-start.12
  22.1 1.7 %collective-permute-start.9 = (bf16[2,5,64,128]{3,2,1,0:T(8,128)(2,1)S(1)}, bf16[2,5,64,128]{3,2,1,0:T(8,128)(2,1)S(1)}, u32[]{:S(2)}, u32[]{:S(2)}) collective-permute-start(bf16[2,5,64,128]{3,2,1,0:T(8,128)(2,1)S(1)} %collective-permute-done.6.refs_7_.refs_5_), channel_id=1, source_target_pairs={{0,8},{1,9},{2,0},{3,1},{4,6},{5,7},{6,14},{7,15},{8,16},{9,17},{1... | collective-permute-start | bytes 491528 | tf_op jit(solution)/shard_map/ppermute | solution.py:671
  23.8 1.5 %collective-permute-start.15 = (bf16[2,5,64,128]{3,2,1,0:T(8,128)(2,1)S(1)}, bf16[2,5,64,128]{3,2,1,0:T(8,128)(2,1)S(1)}, u32[]{:S(2)}, u32[]{:S(2)}) collective-permute-start(bf16[2,5,64,128]{3,2,1,0:T(8,128)(2,1)S(1)} %collective-permute-done.6.refs_7_.refs_5_), channel_id=1, source_target_pairs={{0,1},{1,0},{2,3},{3,2},{4,5},{5,4},{6,7},{7,6},{8,9},{9,8},{10,11... | collective-permute-start | bytes 491528 | tf_op jit(solution)/shard_map/ppermute | solution.py:669
  25.3 1.5 %project.3.refs_9_.refs_6_ = f32[32,512]{1,0:T(8,128)S(1)} custom-call(bf16[2,8192,512]{2,1,0:T(8,128)(2,1)S(1)} %bitcast.5, bf16[2,32,4096]{2,1,0:T(8,128)(2,1)S(1)} %get-tuple-element.73.refs_1_.refs_8_.refs_5_.refs_3_, f32[32,512]{1,0:T(8,128)S(1)} %get-tuple-element.74.refs_2_.refs_5_), custom_call_target="tpu_custom_call" | custom-call | flops 600000000 | bytes 10000000 | tf_op jit(solution)/shard_map/project/pallas_call | solution.py:343
  26.8 0.4 %project_low.1.refs_10_.refs_11_ = f32[2,32,64]{2,1,0:T(8,128)S(1)} custom-call(bf16[2,5,64,128]{3,2,1,0:T(8,128)(2,1)S(1)} %get-tuple-element.50.refs_5_.refs_0_, bf16[2,4,64,128]{3,2,1,0:T(8,128)(2,1)S(1)} %get-tuple-element.70.refs_1_.refs_0_, bf16[2,5,64,128]{3,2,1,0:T(8,128)(2,1)S(1)} %collective-permute-done.2.refs_2_.refs_1_, ...), custom_call_target="tpu_custom_call" | custom-call | flops 600000000 | bytes 10000000 | tf_op jit(solution)/shard_map/project_low/pallas_call | solution.py:409
  27.3 0.0 collective-permute-done.10.refs_3_
  27.3 0.0 collective-permute-done.11.refs_6_
  27.3 0.0 collective-permute-done.12.refs_2_
  27.3 0.1 collective-permute-done.9.refs_7_
  27.4 1.0 %collective-permute-start.13 = (bf16[2,5,64,128]{3,2,1,0:T(8,128)(2,1)S(1)}, bf16[2,5,64,128]{3,2,1,0:T(8,128)(2,1)S(1)}, u32[]{:S(2)}, u32[]{:S(2)}) collective-permute-start(bf16[2,5,64,128]{3,2,1,0:T(8,128)(2,1)S(1)} %collective-permute-done.9.refs_7_), channel_id=1, source_target_pairs={{0,1},{1,0},{2,3},{3,2},{4,5},{5,4},{6,7},{7,6},{8,9},{9,8},{10,11... | collective-permute-start | bytes 491528 | tf_op jit(solution)/shard_map/ppermute | solution.py:700
  28.4 4.2 %merge.3 = (bf16[2,8192,512]{2,1,0:T(8,128)(2,1)}, bf16[2,64,512]{2,1,0:T(8,128)(2,1)S(1)}, f32[2,32,64]{2,1,0:T(8,128)S(1)}) custom-call(bf16[2,5,64,128]{3,2,1,0:T(8,128)(2,1)S(1)} %get-tuple-element.50.refs_5_.refs_0_, bf16[2,5,64,128]{3,2,1,0:T(8,128)(2,1)S(1)} %collective-permute-done.2.refs_2_.refs_1_, ...), custom_call_target="tpu_custom_call" | custom-call | flops 600000000 | bytes 10000000 | tf_op jit(solution)/shard_map/merge/pallas_call | solution.py:603
  32.6 0.0 collective-permute-done.15.refs_4_
  32.6 0.1 collective-permute-start.16
  32.7 0.5 %collective-permute-start.14 = (bf16[2,5,64,128]{3,2,1,0:T(8,128)(2,1)S(1)}, bf16[2,5,64,128]{3,2,1,0:T(8,128)(2,1)S(1)}, u32[]{:S(2)}, u32[]{:S(2)}) collective-permute-start(bf16[2,5,64,128]{3,2,1,0:T(8,128)(2,1)S(1)} %collective-permute-done.10.refs_3_), channel_id=1, source_target_pairs={{0,4},{1,5},{2,6},{3,7},{4,0},{5,1},{6,2},{7,3},{8,12},{9,13},{10,... | collective-permute-start | bytes 491528 | tf_op jit(solution)/shard_map/ppermute | solution.py:701
  33.2 2.7 %merge.4 = (bf16[2,8192,512]{2,1,0:T(8,128)(2,1)}, f32[2,32,64]{2,1,0:T(8,128)S(1)}) custom-call(bf16[2,4,64,128]{3,2,1,0:T(8,128)(2,1)S(1)} %get-tuple-element.70.refs_1_.refs_0_, bf16[2,5,64,128]{3,2,1,0:T(8,128)(2,1)S(1)} %collective-permute-done.7.refs_6_.refs_1_, ...), custom_call_target="tpu_custom_call", output_to_operand_aliasing={{0}: (9, {})} | custom-call | flops 600000000 | bytes 10000000 | tf_op jit(solution)/shard_map/merge/pallas_call | solution.py:603
  35.9 0.0 collective-permute-done.16.refs_2_
  35.9 0.0 collective-permute-done.13.refs_0_
  35.9 0.0 collective-permute-done.14.refs_1_
  36.0 2.9 %merge.5 = (bf16[2,8192,512]{2,1,0:T(8,128)(2,1)}, bf16[4,8,32,128]{3,2,1,0:T(8,128)(2,1)}) custom-call(bf16[2,5,64,128]{3,2,1,0:T(8,128)(2,1)S(1)} %collective-permute-done.13.refs_0_, bf16[2,5,64,128]{3,2,1,0:T(8,128)(2,1)S(1)} %collective-permute-done.14.refs_1_, ...), custom_call_target="tpu_custom_call", output_to_operand_aliasing={{0}: (17, {})} | custom-call | flops 600000000 | bytes 10000000 | tf_op jit(solution)/shard_map/merge/pallas_call | solution.py:603
  (8 shorter events, 0.0 us)
Async XLA Ops:
  0.6 1.9 %collective-permute-start = (bf16[2,64,512]{2,1,0:T(8,128)(2,1)}, bf16[2,64,512]{2,1,0:T(8,128)(2,1)S(1)}, u32[]{:S(2)}, u32[]{:S(2)}) collective-permute-start(bf16[2,64,512]{2,1,0:T(8,128)(2,1)} %bitcast.14), channel_id=1, source_target_pairs={{0,4},{1,5},{2,6},{3,7},{4,0},{5,1},{6,2},{7,3},{8,12},{9,13},{10,... | collective-permute-start | bytes 393224 | tf_op jit(solution)/shard_map/ppermute | solution.py:649
  1.1 1.4 %collective-permute-start.1 = (bf16[2,64,64]{2,1,0:T(8,128)(2,1)}, bf16[2,64,64]{2,1,0:T(8,128)(2,1)S(1)}, u32[]{:S(2)}, u32[]{:S(2)}) collective-permute-start(bf16[2,64,64]{2,1,0:T(8,128)(2,1)} %up.1), channel_id=1, source_target_pairs={{0,4},{1,5},{2,6},{3,7},{4,0},{5,1},{6,2},{7,3},{8,12},{9,13},{10,... | collective-permute-start | bytes 49160 | tf_op jit(solution)/shard_map/ppermute | solution.py:649
  2.6 7.7 %collective-permute-start.2 = (bf16[2,5,64,128]{3,2,1,0:T(8,128)(2,1)S(1)}, bf16[2,5,64,128]{3,2,1,0:T(8,128)(2,1)S(1)}, u32[]{:S(2)}, u32[]{:S(2)}) collective-permute-start(bf16[2,5,64,128]{3,2,1,0:T(8,128)(2,1)S(1)} %get-tuple-element.50.refs_5_.refs_0_), channel_id=1, source_target_pairs={{0,8},{1,9},{2,0},{3,1},{4,6},{5,7},{6,14},{7,15},{8,16},{9,17},{1... | collective-permute-start | bytes 491528 | tf_op jit(solution)/shard_map/ppermute | solution.py:661
  5.6 8.3 %collective-permute-start.4 = (bf16[32,4096]{1,0:T(8,128)(2,1)}, bf16[32,4096]{1,0:T(8,128)(2,1)S(1)}, u32[]{:S(2)}, u32[]{:S(2)}) collective-permute-start(bf16[32,4096]{1,0:T(8,128)(2,1)} %bitcast.6), channel_id=1, source_target_pairs={{1,0},{0,1},{3,2},{2,3},{5,4},{4,5},{7,6},{6,7},{9,8},{8,9},{11,10... | collective-permute-start | bytes 786440 | tf_op jit(solution)/shard_map/ppermute | solution.py:662
  10.4 5.4 %collective-permute-start.3 = (bf16[2,5,64,128]{3,2,1,0:T(8,128)(2,1)S(1)}, bf16[2,5,64,128]{3,2,1,0:T(8,128)(2,1)S(1)}, u32[]{:S(2)}, u32[]{:S(2)}) collective-permute-start(bf16[2,5,64,128]{3,2,1,0:T(8,128)(2,1)S(1)} %collective-permute-done.2.refs_2_.refs_1_), channel_id=1, source_target_pairs={{0,8},{1,9},{2,0},{3,1},{4,6},{5,7},{6,14},{7,15},{8,16},{9,17},{1... | collective-permute-start | bytes 491528 | tf_op jit(solution)/shard_map/ppermute | solution.py:671
  11.4 4.4 %collective-permute-start.5 = (bf16[2,5,64,128]{3,2,1,0:T(8,128)(2,1)S(1)}, bf16[2,5,64,128]{3,2,1,0:T(8,128)(2,1)S(1)}, u32[]{:S(2)}, u32[]{:S(2)}) collective-permute-start(bf16[2,5,64,128]{3,2,1,0:T(8,128)(2,1)S(1)} %collective-permute-done.2.refs_2_.refs_1_), channel_id=1, source_target_pairs={{0,4},{1,5},{2,6},{3,7},{4,0},{5,1},{6,2},{7,3},{8,12},{9,13},{10,... | collective-permute-start | bytes 491528 | tf_op jit(solution)/shard_map/ppermute | solution.py:670
  11.4 10.1 %collective-permute-start.7 = (bf16[2,5,64,128]{3,2,1,0:T(8,128)(2,1)S(1)}, bf16[2,5,64,128]{3,2,1,0:T(8,128)(2,1)S(1)}, u32[]{:S(2)}, u32[]{:S(2)}) collective-permute-start(bf16[2,5,64,128]{3,2,1,0:T(8,128)(2,1)S(1)} %collective-permute-done.2.refs_2_.refs_1_), channel_id=1, source_target_pairs={{0,1},{1,0},{2,3},{3,2},{4,5},{5,4},{6,7},{7,6},{8,9},{9,8},{10,11... | collective-permute-start | bytes 491528 | tf_op jit(solution)/shard_map/ppermute | solution.py:669
  12.4 6.6 %slice-start = ((s8[16777216]{0:T(1024)(128)(4,1)}), s8[4194304]{0:T(1024)(128)(4,1)S(1)}, s32[]{:S(2)}) async-start(s8[16777216]{0:T(1024)(128)(4,1)} %bitcast.4), calls=%async_computation | async-start | bytes 8388608
  12.4 6.6 %slice-start.1 = ((s8[16777216]{0:T(1024)(128)(4,1)}), s8[4194304]{0:T(1024)(128)(4,1)S(1)}, s32[]{:S(2)}) async-start(s8[16777216]{0:T(1024)(128)(4,1)} %bitcast.4), calls=%async_computation.1 | async-start | bytes 8388608
  15.8 3.2 %slice-start.2 = ((s8[16777216]{0:T(1024)(128)(4,1)}), s8[4194304]{0:T(1024)(128)(4,1)S(1)}, s32[]{:S(2)}) async-start(s8[16777216]{0:T(1024)(128)(4,1)} %bitcast.4), calls=%async_computation.2 | async-start | bytes 8388608
  15.8 5.7 %collective-permute-start.6 = (bf16[2,5,64,128]{3,2,1,0:T(8,128)(2,1)S(1)}, bf16[2,5,64,128]{3,2,1,0:T(8,128)(2,1)S(1)}, u32[]{:S(2)}, u32[]{:S(2)}) collective-permute-start(bf16[2,5,64,128]{3,2,1,0:T(8,128)(2,1)S(1)} %collective-permute-done.3.refs_4_.refs_3_), channel_id=1, source_target_pairs={{0,8},{1,9},{2,0},{3,1},{4,6},{5,7},{6,14},{7,15},{8,16},{9,17},{1... | collective-permute-start | bytes 491528 | tf_op jit(solution)/shard_map/ppermute | solution.py:671
  16.7 4.8 %collective-permute-start.8 = (bf16[2,5,64,128]{3,2,1,0:T(8,128)(2,1)S(1)}, bf16[2,5,64,128]{3,2,1,0:T(8,128)(2,1)S(1)}, u32[]{:S(2)}, u32[]{:S(2)}) collective-permute-start(bf16[2,5,64,128]{3,2,1,0:T(8,128)(2,1)S(1)} %collective-permute-done.3.refs_4_.refs_3_), channel_id=1, source_target_pairs={{0,4},{1,5},{2,6},{3,7},{4,0},{5,1},{6,2},{7,3},{8,12},{9,13},{10,... | collective-permute-start | bytes 491528 | tf_op jit(solution)/shard_map/ppermute | solution.py:670
  16.7 10.6 %collective-permute-start.10 = (bf16[2,5,64,128]{3,2,1,0:T(8,128)(2,1)S(1)}, bf16[2,5,64,128]{3,2,1,0:T(8,128)(2,1)S(1)}, u32[]{:S(2)}, u32[]{:S(2)}) collective-permute-start(bf16[2,5,64,128]{3,2,1,0:T(8,128)(2,1)S(1)} %collective-permute-done.3.refs_4_.refs_3_), channel_id=1, source_target_pairs={{0,1},{1,0},{2,3},{3,2},{4,5},{5,4},{6,7},{7,6},{8,9},{9,8},{10,11... | collective-permute-start | bytes 491528 | tf_op jit(solution)/shard_map/ppermute | solution.py:669
  17.7 2.3 %slice-start.3 = ((s8[16777216]{0:T(1024)(128)(4,1)}), s8[4194304]{0:T(1024)(128)(4,1)S(1)}, s32[]{:S(2)}) async-start(s8[16777216]{0:T(1024)(128)(4,1)} %bitcast.4), calls=%async_computation.3 | async-start | bytes 8388608
  17.7 2.3 %copy-start = (bf16[4,8,4096]{2,1,0:T(8,128)(2,1)S(1)}, bf16[4,8,4096]{2,1,0:T(8,128)(2,1)}, u32[]{:S(2)}) copy-start(bf16[4,8,4096]{2,1,0:T(8,128)(2,1)} %param.8) | copy-start | bytes 786436
  21.5 5.8 %collective-permute-start.11 = (bf16[2,5,64,128]{3,2,1,0:T(8,128)(2,1)S(1)}, bf16[2,5,64,128]{3,2,1,0:T(8,128)(2,1)S(1)}, u32[]{:S(2)}, u32[]{:S(2)}) collective-permute-start(bf16[2,5,64,128]{3,2,1,0:T(8,128)(2,1)S(1)} %collective-permute-done.6.refs_7_.refs_5_), channel_id=1, source_target_pairs={{0,4},{1,5},{2,6},{3,7},{4,0},{5,1},{6,2},{7,3},{8,12},{9,13},{10,... | collective-permute-start | bytes 491528 | tf_op jit(solution)/shard_map/ppermute | solution.py:670
  21.8 5.5 %collective-permute-start.12 = (bf16[2,5,64,128]{3,2,1,0:T(8,128)(2,1)S(1)}, bf16[2,5,64,128]{3,2,1,0:T(8,128)(2,1)S(1)}, u32[]{:S(2)}, u32[]{:S(2)}) collective-permute-start(bf16[2,5,64,128]{3,2,1,0:T(8,128)(2,1)S(1)} %collective-permute-done.7.refs_6_.refs_1_), channel_id=1, source_target_pairs={{0,4},{1,5},{2,6},{3,7},{4,0},{5,1},{6,2},{7,3},{8,12},{9,13},{10,... | collective-permute-start | bytes 491528 | tf_op jit(solution)/shard_map/ppermute | solution.py:668
  22.1 5.3 %collective-permute-start.9 = (bf16[2,5,64,128]{3,2,1,0:T(8,128)(2,1)S(1)}, bf16[2,5,64,128]{3,2,1,0:T(8,128)(2,1)S(1)}, u32[]{:S(2)}, u32[]{:S(2)}) collective-permute-start(bf16[2,5,64,128]{3,2,1,0:T(8,128)(2,1)S(1)} %collective-permute-done.6.refs_7_.refs_5_), channel_id=1, source_target_pairs={{0,8},{1,9},{2,0},{3,1},{4,6},{5,7},{6,14},{7,15},{8,16},{9,17},{1... | collective-permute-start | bytes 491528 | tf_op jit(solution)/shard_map/ppermute | solution.py:671
  23.8 8.8 %collective-permute-start.15 = (bf16[2,5,64,128]{3,2,1,0:T(8,128)(2,1)S(1)}, bf16[2,5,64,128]{3,2,1,0:T(8,128)(2,1)S(1)}, u32[]{:S(2)}, u32[]{:S(2)}) collective-permute-start(bf16[2,5,64,128]{3,2,1,0:T(8,128)(2,1)S(1)} %collective-permute-done.6.refs_7_.refs_5_), channel_id=1, source_target_pairs={{0,1},{1,0},{2,3},{3,2},{4,5},{5,4},{6,7},{7,6},{8,9},{9,8},{10,11... | collective-permute-start | bytes 491528 | tf_op jit(solution)/shard_map/ppermute | solution.py:669
  27.4 8.5 %collective-permute-start.13 = (bf16[2,5,64,128]{3,2,1,0:T(8,128)(2,1)S(1)}, bf16[2,5,64,128]{3,2,1,0:T(8,128)(2,1)S(1)}, u32[]{:S(2)}, u32[]{:S(2)}) collective-permute-start(bf16[2,5,64,128]{3,2,1,0:T(8,128)(2,1)S(1)} %collective-permute-done.9.refs_7_), channel_id=1, source_target_pairs={{0,1},{1,0},{2,3},{3,2},{4,5},{5,4},{6,7},{7,6},{8,9},{9,8},{10,11... | collective-permute-start | bytes 491528 | tf_op jit(solution)/shard_map/ppermute | solution.py:700
  32.6 3.3 %collective-permute-start.16 = (bf16[2,5,64,128]{3,2,1,0:T(8,128)(2,1)S(1)}, bf16[2,5,64,128]{3,2,1,0:T(8,128)(2,1)S(1)}, u32[]{:S(2)}, u32[]{:S(2)}) collective-permute-start(bf16[2,5,64,128]{3,2,1,0:T(8,128)(2,1)S(1)} %collective-permute-done.15.refs_4_), channel_id=1, source_target_pairs={{0,4},{1,5},{2,6},{3,7},{4,0},{5,1},{6,2},{7,3},{8,12},{9,13},{10,... | collective-permute-start | bytes 491528 | tf_op jit(solution)/shard_map/ppermute | solution.py:705
  32.7 3.3 %collective-permute-start.14 = (bf16[2,5,64,128]{3,2,1,0:T(8,128)(2,1)S(1)}, bf16[2,5,64,128]{3,2,1,0:T(8,128)(2,1)S(1)}, u32[]{:S(2)}, u32[]{:S(2)}) collective-permute-start(bf16[2,5,64,128]{3,2,1,0:T(8,128)(2,1)S(1)} %collective-permute-done.10.refs_3_), channel_id=1, source_target_pairs={{0,4},{1,5},{2,6},{3,7},{4,0},{5,1},{6,2},{7,3},{8,12},{9,13},{10,... | collective-permute-start | bytes 491528 | tf_op jit(solution)/shard_map/ppermute | solution.py:701

commit v2 on v0

--- a/solution.py
+++ b/solution.py
@@ -636,8 +636,11 @@
         elif step == 3:
             olds, states = project(lay, projection_weight_matrices, hidden, [token])
             token = olds
+        arrived = [x for _, x in crossing]
+        if step + 1 == last_step:
+            (sent, arrived), token = after_all((sent, arrived), token)
         (came, hidden, arrived, swapped, held), token = after_all(
-            (sent, hidden, [x for _, x in crossing], swapped, [x for _, x in over_there]), token
+            (sent, hidden, arrived, swapped, [x for _, x in over_there]), token
         )
         entries.append((step, 1, 0, swapped))
         entries += [(s, 1, 1, x) for (s, _), x in zip(over_there, held)]

time: 39.1 us -> 39.1 us (level)
  waiting for transfers between devices: 4.06 us -> 3.35 us
  Pallas kernels: 20 us -> 20.5 us
    ppermute x3, waiting for transfers between devices: 3.88 us -> 3.17 us  [shards(): sent = send(came, perm=ring)]
    pallas_call x3, Pallas kernels: 5.98 us -> 6.54 us  [cache_attention(): pl.pallas_call(functools.partial(attend_cache, pairs, ready, sizes, scale...]
  transfers between devices with their start and end apart: 17 -> 17, of which waited for: 4 -> 3; matrix products, arithmetic and copies ran while one was open for 0% -> 0% of each run, Pallas kernels for 44% -> 45%
where the time goes in v2:
time: 39.1 us; the launch traced here: 38.9 us
  Pallas kernels  20.5 us (52%)
  starting transfers between devices  14 us (36%)
  waiting for transfers between devices  3.35 us (9%)
  between operations  0.98 us (3%)
    pallas_call x3, Pallas kernels, merge(): pl.pallas_call(functools.partial(merge_some, lay, [e[:3] for e in entries...  9.78 us
    pallas_call x3, Pallas kernels, cache_attention(): pl.pallas_call(functools.partial(attend_cache, pairs, ready, sizes, scale...  6.54 us
    ppermute x3, starting transfers between devices, shards(): sent = send(came, perm=ring)  4.78 us
    ppermute x3, waiting for transfers between devices, shards(): sent = send(came, perm=ring)  3.17 us
    pallas_call x1, Pallas kernels, project(): pl.pallas_call(functools.partial(project_old, lay, len(hidden)), out_shap...  2.95 us
    ppermute x1, starting transfers between devices, shards(): sent = send(pair, perm=ring)  2.91 us
    ppermute x3, starting transfers between devices, shards(): across = [(step, send(came, perm=planes))]  1.6 us
    ppermute x1, starting transfers between devices, shards(): late = [(last_step, 0, 1, send(came, perm=planes))]  1.56 us
  transfers between devices with their start and end apart: 17, of which 3 were waited for; matrix products, arithmetic and copies ran while one was open for 0% of the time, Pallas kernels for 45%

profile of v2, /device:TPU:0, one launch (start us, length us, event | category | flops | bytes accessed | tf_op | source)
XLA Modules:
  0.0 38.9 jit_solution(16980761978722227456)
XLA Ops:
  0.6 0.5 %collective-permute-start = (bf16[2,64,512]{2,1,0:T(8,128)(2,1)}, bf16[2,64,512]{2,1,0:T(8,128)(2,1)S(1)}, u32[]{:S(2)}, u32[]{:S(2)}) collective-permute-start(bf16[2,64,512]{2,1,0:T(8,128)(2,1)} %bitcast.14), channel_id=1, source_target_pairs={{0,4},{1,5},{2,6},{3,7},{4,0},{5,1},{6,2},{7,3},{8,12},{9,13},{10,... | collective-permute-start | bytes 393224 | tf_op jit(solution)/shard_map/ppermute | solution.py:609
  1.1 0.1 collective-permute-start.1
  1.2 1.2 %begin.1 = (bf16[2,5,64,128]{3,2,1,0:T(8,128)(2,1)S(1)}, bf16[2,4,64,128]{3,2,1,0:T(8,128)(2,1)S(1)}, s32[8]{0:T(128)S(4)}, s32[8]{0:T(128)S(4)}, bf16[4,8,32,128]{3,2,1,0:T(8,128)(2,1)S(1)}) custom-call(bf16[2,64,512]{2,1,0:T(8,128)(2,1)} %bitcast.15, bf16[2,64,64]{2,1,0:T(8,128)(2,1)} %up.1, s32[8]{0:T(128)} %len_hbm.1, bf16[4,8,32,128]{3,2,1,0:T(8,128)(2,1)} %q_hbm.1), custom_call_target="tpu_custom_call" | custom-call | flops 600000000 | bytes 10000000 | tf_op jit(solution)/shard_map/begin/pallas_call | solution.py:147
  2.4 0.1 collective-permute-done.1.up
  2.6 0.0 collective-permute-done.down
  2.6 0.1 pack_other.1
  2.6 2.9 %collective-permute-start.2 = (bf16[2,5,64,128]{3,2,1,0:T(8,128)(2,1)S(1)}, bf16[2,5,64,128]{3,2,1,0:T(8,128)(2,1)S(1)}, u32[]{:S(2)}, u32[]{:S(2)}) collective-permute-start(bf16[2,5,64,128]{3,2,1,0:T(8,128)(2,1)S(1)} %get-tuple-element.55.refs_5_.refs_0_), channel_id=1, source_target_pairs={{0,8},{1,9},{2,0},{3,1},{4,6},{5,7},{6,14},{7,15},{8,16},{9,17},{1... | collective-permute-start | bytes 491528 | tf_op jit(solution)/shard_map/ppermute | solution.py:621
  5.6 1.5 %collective-permute-start.4 = (bf16[32,4096]{1,0:T(8,128)(2,1)}, bf16[32,4096]{1,0:T(8,128)(2,1)S(1)}, u32[]{:S(2)}, u32[]{:S(2)}) collective-permute-start(bf16[32,4096]{1,0:T(8,128)(2,1)} %bitcast.6), channel_id=1, source_target_pairs={{1,0},{0,1},{3,2},{2,3},{5,4},{4,5},{7,6},{6,7},{9,8},{8,9},{11,10... | collective-permute-start | bytes 786440 | tf_op jit(solution)/shard_map/ppermute | solution.py:622
  7.0 3.3 %cache_attention.3 = (bf16[8,3072,128]{2,1,0:T(8,128)(2,1)S(1)}, bf16[8,3072,128]{2,1,0:T(8,128)(2,1)S(1)}, f32[2,128,128]{2,1,0:T(8,128)S(1)}, f32[2,128,128]{2,1,0:T(8,128)S(1)}) custom-call(s32[8]{0:T(128)S(4)} %get-tuple-element.56.refs_0_, s32[8]{0:T(128)S(4)} %get-tuple-element.57.refs_1_.refs_6_, ...), custom_call_target="tpu_custom_call" | custom-call | flops 600000000 | bytes 10000000 | tf_op jit(solution)/shard_map/cache_attention/pallas_call | solution.py:298
  10.4 0.0 collective-permute-done.2.refs_1_
  10.4 1.6 %collective-permute-start.3 = (bf16[2,5,64,128]{3,2,1,0:T(8,128)(2,1)S(1)}, bf16[2,5,64,128]{3,2,1,0:T(8,128)(2,1)S(1)}, u32[]{:S(2)}, u32[]{:S(2)}) collective-permute-start(bf16[2,5,64,128]{3,2,1,0:T(8,128)(2,1)S(1)} %collective-permute-done.2.refs_1_), channel_id=1, source_target_pairs={{0,8},{1,9},{2,0},{3,1},{4,6},{5,7},{6,14},{7,15},{8,16},{9,17},{1... | collective-permute-start | bytes 491528 | tf_op jit(solution)/shard_map/ppermute | solution.py:631
  12.0 0.0 collective-permute-start.5
  12.0 0.5 %collective-permute-start.7 = (bf16[2,5,64,128]{3,2,1,0:T(8,128)(2,1)S(1)}, bf16[2,5,64,128]{3,2,1,0:T(8,128)(2,1)S(1)}, u32[]{:S(2)}, u32[]{:S(2)}) collective-permute-start(bf16[2,5,64,128]{3,2,1,0:T(8,128)(2,1)S(1)} %collective-permute-done.2.refs_1_), channel_id=1, source_target_pairs={{0,1},{1,0},{2,3},{3,2},{4,5},{5,4},{6,7},{7,6},{8,9},{9,8},{10,11... | collective-permute-start | bytes 491528 | tf_op jit(solution)/shard_map/ppermute | solution.py:629
  12.6 1.9 %cache_attention.4 = (bf16[8,3072,128]{2,1,0:T(8,128)(2,1)S(1)}, bf16[8,3072,128]{2,1,0:T(8,128)(2,1)S(1)}, f32[2,128,128]{2,1,0:T(8,128)S(1)}, f32[2,128,128]{2,1,0:T(8,128)S(1)}) custom-call(s32[8]{0:T(128)S(4)} %get-tuple-element.56.refs_0_, s32[8]{0:T(128)S(4)} %get-tuple-element.57.refs_1_.refs_6_, ...), custom_call_target="tpu_custom_call", output_to_operand_aliasing={{0}: (5, {}), {1}: (6, {})} | custom-call | flops 600000000 | bytes 10000000 | tf_op jit(solution)/shard_map/cache_attention/pallas_call | solution.py:298
  14.4 0.0 collective-permute-done.4.refs_2_
  14.4 1.3 %collective-permute-done.3.refs_3_ = bf16[2,5,64,128]{3,2,1,0:T(8,128)(2,1)S(1)} collective-permute-done((bf16[2,5,64,128]{3,2,1,0:T(8,128)(2,1)S(1)}, bf16[2,5,64,128]{3,2,1,0:T(8,128)(2,1)S(1)}, u32[]{:S(2)}, u32[]{:S(2)}) %collective-permute-start.3) | collective-permute-done | bytes 163872 | tf_op jit(solution)/shard_map/ppermute | solution.py:631
  15.8 0.0 collective-permute-done.5.refs_2_
  15.8 1.6 %collective-permute-start.6 = (bf16[2,5,64,128]{3,2,1,0:T(8,128)(2,1)S(1)}, bf16[2,5,64,128]{3,2,1,0:T(8,128)(2,1)S(1)}, u32[]{:S(2)}, u32[]{:S(2)}) collective-permute-start(bf16[2,5,64,128]{3,2,1,0:T(8,128)(2,1)S(1)} %collective-permute-done.3.refs_3_), channel_id=1, source_target_pairs={{0,8},{1,9},{2,0},{3,1},{4,6},{5,7},{6,14},{7,15},{8,16},{9,17},{1... | collective-permute-start | bytes 491528 | tf_op jit(solution)/shard_map/ppermute | solution.py:631
  17.3 0.0 collective-permute-start.8
  17.3 0.5 %collective-permute-start.10 = (bf16[2,5,64,128]{3,2,1,0:T(8,128)(2,1)S(1)}, bf16[2,5,64,128]{3,2,1,0:T(8,128)(2,1)S(1)}, u32[]{:S(2)}, u32[]{:S(2)}) collective-permute-start(bf16[2,5,64,128]{3,2,1,0:T(8,128)(2,1)S(1)} %collective-permute-done.3.refs_3_), channel_id=1, source_target_pairs={{0,1},{1,0},{2,3},{3,2},{4,5},{5,4},{6,7},{7,6},{8,9},{9,8},{10,11... | collective-permute-start | bytes 491528 | tf_op jit(solution)/shard_map/ppermute | solution.py:629
  17.9 1.4 %cache_attention.5 = (bf16[8,3072,128]{2,1,0:T(8,128)(2,1)S(1)}, bf16[8,3072,128]{2,1,0:T(8,128)(2,1)S(1)}, f32[4,128,128]{2,1,0:T(8,128)S(1)}, f32[4,128,128]{2,1,0:T(8,128)S(1)}) custom-call(s32[8]{0:T(128)S(4)} %get-tuple-element.56.refs_0_, s32[8]{0:T(128)S(4)} %get-tuple-element.57.refs_1_.refs_6_, ...), custom_call_target="tpu_custom_call", output_to_operand_aliasing={{0}: (5, {}), {1}: (6, {})} | custom-call | flops 600000000 | bytes 10000000 | tf_op jit(solution)/shard_map/cache_attention/pallas_call | solution.py:298
  19.2 0.0 collective-permute-done.7.refs_1_
  19.3 1.8 %collective-permute-done.6.refs_5_ = bf16[2,5,64,128]{3,2,1,0:T(8,128)(2,1)S(1)} collective-permute-done((bf16[2,5,64,128]{3,2,1,0:T(8,128)(2,1)S(1)}, bf16[2,5,64,128]{3,2,1,0:T(8,128)(2,1)S(1)}, u32[]{:S(2)}, u32[]{:S(2)}) %collective-permute-start.6) | collective-permute-done | bytes 163872 | tf_op jit(solution)/shard_map/ppermute | solution.py:631
  21.1 0.0 collective-permute-done.8.refs_4_
  21.1 1.6 %collective-permute-start.9 = (bf16[2,5,64,128]{3,2,1,0:T(8,128)(2,1)S(1)}, bf16[2,5,64,128]{3,2,1,0:T(8,128)(2,1)S(1)}, u32[]{:S(2)}, u32[]{:S(2)}) collective-permute-start(bf16[2,5,64,128]{3,2,1,0:T(8,128)(2,1)S(1)} %collective-permute-done.6.refs_5_), channel_id=1, source_target_pairs={{0,8},{1,9},{2,0},{3,1},{4,6},{5,7},{6,14},{7,15},{8,16},{9,17},{1... | collective-permute-start | bytes 491528 | tf_op jit(solution)/shard_map/ppermute | solution.py:631
  22.7 0.0 collective-permute-start.11
  22.7 0.5 %collective-permute-start.12 = (bf16[2,5,64,128]{3,2,1,0:T(8,128)(2,1)S(1)}, bf16[2,5,64,128]{3,2,1,0:T(8,128)(2,1)S(1)}, u32[]{:S(2)}, u32[]{:S(2)}) collective-permute-start(bf16[2,5,64,128]{3,2,1,0:T(8,128)(2,1)S(1)} %collective-permute-done.7.refs_1_), channel_id=1, source_target_pairs={{0,4},{1,5},{2,6},{3,7},{4,0},{5,1},{6,2},{7,3},{8,12},{9,13},{10,... | collective-permute-start | bytes 491528 | tf_op jit(solution)/shard_map/ppermute | solution.py:628
  23.2 0.5 %collective-permute-start.15 = (bf16[2,5,64,128]{3,2,1,0:T(8,128)(2,1)S(1)}, bf16[2,5,64,128]{3,2,1,0:T(8,128)(2,1)S(1)}, u32[]{:S(2)}, u32[]{:S(2)}) collective-permute-start(bf16[2,5,64,128]{3,2,1,0:T(8,128)(2,1)S(1)} %collective-permute-done.6.refs_5_), channel_id=1, source_target_pairs={{0,1},{1,0},{2,3},{3,2},{4,5},{5,4},{6,7},{7,6},{8,9},{9,8},{10,11... | collective-permute-start | bytes 491528 | tf_op jit(solution)/shard_map/ppermute | solution.py:629
  23.7 0.0 slice-done
  23.7 0.0 slice-done.1
  23.7 0.0 slice-done.2
  23.7 0.0 slice-done.3
  23.7 0.0 copy-done
  23.7 3.0 %project.1 = (f32[2,32,512]{2,1,0:T(8,128)S(1)}, bf16[2,32,4096]{2,1,0:T(8,128)(2,1)S(1)}) custom-call(bf16[2,8192,512]{2,1,0:T(8,128)(2,1)S(1)} %bitcast.5, bf16[32,4096]{1,0:T(8,128)(2,1)S(1)} %bitcast.7, bf16[32,4096]{1,0:T(8,128)(2,1)S(1)} %collective-permute-done.4.refs_2_, f32[4,128,128]{2,1,0:T(8,128)S(1)} %get-tuple-element.75.refs_3_.refs_12_), custom_call_target="tpu_custom_call" | custom-call | flops 600000000 | bytes 10000000 | tf_op jit(solution)/shard_map/project/pallas_call | solution.py:336
  26.7 0.0 collective-permute-done.10.refs_3_
  26.7 0.0 collective-permute-done.9.refs_7_
  26.7 0.0 collective-permute-done.11.refs_6_
  26.7 0.0 collective-permute-done.12.refs_2_
  26.7 1.6 %collective-permute-start.13 = (bf16[2,5,64,128]{3,2,1,0:T(8,128)(2,1)S(1)}, bf16[2,5,64,128]{3,2,1,0:T(8,128)(2,1)S(1)}, u32[]{:S(2)}, u32[]{:S(2)}) collective-permute-start(bf16[2,5,64,128]{3,2,1,0:T(8,128)(2,1)S(1)} %collective-permute-done.9.refs_7_), channel_id=1, source_target_pairs={{0,1},{1,0},{2,3},{3,2},{4,5},{5,4},{6,7},{7,6},{8,9},{9,8},{10,11... | collective-permute-start | bytes 491528 | tf_op jit(solution)/shard_map/ppermute | solution.py:654
  28.3 4.2 %merge.3 = (bf16[2,8192,512]{2,1,0:T(8,128)(2,1)}, bf16[2,64,512]{2,1,0:T(8,128)(2,1)S(1)}, f32[2,32,64]{2,1,0:T(8,128)S(1)}) custom-call(bf16[2,5,64,128]{3,2,1,0:T(8,128)(2,1)S(1)} %get-tuple-element.55.refs_5_.refs_0_, bf16[2,5,64,128]{3,2,1,0:T(8,128)(2,1)S(1)} %collective-permute-done.2.refs_1_, ...), custom_call_target="tpu_custom_call" | custom-call | flops 600000000 | bytes 10000000 | tf_op jit(solution)/shard_map/merge/pallas_call | solution.py:571
  32.5 0.0 collective-permute-done.15.refs_4_
  32.5 0.1 collective-permute-start.16
  32.6 0.5 %collective-permute-start.14 = (bf16[2,5,64,128]{3,2,1,0:T(8,128)(2,1)S(1)}, bf16[2,5,64,128]{3,2,1,0:T(8,128)(2,1)S(1)}, u32[]{:S(2)}, u32[]{:S(2)}) collective-permute-start(bf16[2,5,64,128]{3,2,1,0:T(8,128)(2,1)S(1)} %collective-permute-done.10.refs_3_), channel_id=1, source_target_pairs={{0,4},{1,5},{2,6},{3,7},{4,0},{5,1},{6,2},{7,3},{8,12},{9,13},{10,... | collective-permute-start | bytes 491528 | tf_op jit(solution)/shard_map/ppermute | solution.py:655
  33.1 2.7 %merge.4 = (bf16[2,8192,512]{2,1,0:T(8,128)(2,1)}, f32[2,32,64]{2,1,0:T(8,128)S(1)}) custom-call(bf16[2,4,64,128]{3,2,1,0:T(8,128)(2,1)S(1)} %get-tuple-element.90.refs_0_, bf16[2,5,64,128]{3,2,1,0:T(8,128)(2,1)S(1)} %collective-permute-done.7.refs_1_, bf16[2,5,64,128]{3,2,1,0:T(8,128)(2,1)S(1)} %collective-permute-done.12.refs_2_, ...), custom_call_target="tpu_custom_call", output_to_operand_aliasing={{0}: (9, {})} | custom-call | flops 600000000 | bytes 10000000 | tf_op jit(solution)/shard_map/merge/pallas_call | solution.py:571
  35.8 0.0 collective-permute-done.16.refs_2_
  35.8 0.0 collective-permute-done.13.refs_0_
  35.8 0.0 collective-permute-done.14.refs_1_
  35.8 2.9 %merge.5 = (bf16[2,8192,512]{2,1,0:T(8,128)(2,1)}, bf16[4,8,32,128]{3,2,1,0:T(8,128)(2,1)}) custom-call(bf16[2,5,64,128]{3,2,1,0:T(8,128)(2,1)S(1)} %collective-permute-done.13.refs_0_, bf16[2,5,64,128]{3,2,1,0:T(8,128)(2,1)S(1)} %collective-permute-done.14.refs_1_, ...), custom_call_target="tpu_custom_call", output_to_operand_aliasing={{0}: (16, {})} | custom-call | flops 600000000 | bytes 10000000 | tf_op jit(solution)/shard_map/merge/pallas_call | solution.py:571
  (6 shorter events, 0.0 us)
Async XLA Ops:
  0.6 1.9 %collective-permute-start = (bf16[2,64,512]{2,1,0:T(8,128)(2,1)}, bf16[2,64,512]{2,1,0:T(8,128)(2,1)S(1)}, u32[]{:S(2)}, u32[]{:S(2)}) collective-permute-start(bf16[2,64,512]{2,1,0:T(8,128)(2,1)} %bitcast.14), channel_id=1, source_target_pairs={{0,4},{1,5},{2,6},{3,7},{4,0},{5,1},{6,2},{7,3},{8,12},{9,13},{10,... | collective-permute-start | bytes 393224 | tf_op jit(solution)/shard_map/ppermute | solution.py:609
  1.1 1.4 %collective-permute-start.1 = (bf16[2,64,64]{2,1,0:T(8,128)(2,1)}, bf16[2,64,64]{2,1,0:T(8,128)(2,1)S(1)}, u32[]{:S(2)}, u32[]{:S(2)}) collective-permute-start(bf16[2,64,64]{2,1,0:T(8,128)(2,1)} %up.1), channel_id=1, source_target_pairs={{0,4},{1,5},{2,6},{3,7},{4,0},{5,1},{6,2},{7,3},{8,12},{9,13},{10,... | collective-permute-start | bytes 49160 | tf_op jit(solution)/shard_map/ppermute | solution.py:609
  2.6 7.7 %collective-permute-start.2 = (bf16[2,5,64,128]{3,2,1,0:T(8,128)(2,1)S(1)}, bf16[2,5,64,128]{3,2,1,0:T(8,128)(2,1)S(1)}, u32[]{:S(2)}, u32[]{:S(2)}) collective-permute-start(bf16[2,5,64,128]{3,2,1,0:T(8,128)(2,1)S(1)} %get-tuple-element.55.refs_5_.refs_0_), channel_id=1, source_target_pairs={{0,8},{1,9},{2,0},{3,1},{4,6},{5,7},{6,14},{7,15},{8,16},{9,17},{1... | collective-permute-start | bytes 491528 | tf_op jit(solution)/shard_map/ppermute | solution.py:621
  5.6 8.9 %collective-permute-start.4 = (bf16[32,4096]{1,0:T(8,128)(2,1)}, bf16[32,4096]{1,0:T(8,128)(2,1)S(1)}, u32[]{:S(2)}, u32[]{:S(2)}) collective-permute-start(bf16[32,4096]{1,0:T(8,128)(2,1)} %bitcast.6), channel_id=1, source_target_pairs={{1,0},{0,1},{3,2},{2,3},{5,4},{4,5},{7,6},{6,7},{9,8},{8,9},{11,10... | collective-permute-start | bytes 786440 | tf_op jit(solution)/shard_map/ppermute | solution.py:622
  10.4 5.4 %collective-permute-start.3 = (bf16[2,5,64,128]{3,2,1,0:T(8,128)(2,1)S(1)}, bf16[2,5,64,128]{3,2,1,0:T(8,128)(2,1)S(1)}, u32[]{:S(2)}, u32[]{:S(2)}) collective-permute-start(bf16[2,5,64,128]{3,2,1,0:T(8,128)(2,1)S(1)} %collective-permute-done.2.refs_1_), channel_id=1, source_target_pairs={{0,8},{1,9},{2,0},{3,1},{4,6},{5,7},{6,14},{7,15},{8,16},{9,17},{1... | collective-permute-start | bytes 491528 | tf_op jit(solution)/shard_map/ppermute | solution.py:631
  12.0 3.7 %collective-permute-start.5 = (bf16[2,5,64,128]{3,2,1,0:T(8,128)(2,1)S(1)}, bf16[2,5,64,128]{3,2,1,0:T(8,128)(2,1)S(1)}, u32[]{:S(2)}, u32[]{:S(2)}) collective-permute-start(bf16[2,5,64,128]{3,2,1,0:T(8,128)(2,1)S(1)} %collective-permute-done.2.refs_1_), channel_id=1, source_target_pairs={{0,4},{1,5},{2,6},{3,7},{4,0},{5,1},{6,2},{7,3},{8,12},{9,13},{10,... | collective-permute-start | bytes 491528 | tf_op jit(solution)/shard_map/ppermute | solution.py:630
  12.0 7.2 %collective-permute-start.7 = (bf16[2,5,64,128]{3,2,1,0:T(8,128)(2,1)S(1)}, bf16[2,5,64,128]{3,2,1,0:T(8,128)(2,1)S(1)}, u32[]{:S(2)}, u32[]{:S(2)}) collective-permute-start(bf16[2,5,64,128]{3,2,1,0:T(8,128)(2,1)S(1)} %collective-permute-done.2.refs_1_), channel_id=1, source_target_pairs={{0,1},{1,0},{2,3},{3,2},{4,5},{5,4},{6,7},{7,6},{8,9},{9,8},{10,11... | collective-permute-start | bytes 491528 | tf_op jit(solution)/shard_map/ppermute | solution.py:629
  12.6 11.2 %slice-start = ((s8[16777216]{0:T(1024)(128)(4,1)}), s8[4194304]{0:T(1024)(128)(4,1)S(1)}, s32[]{:S(2)}) async-start(s8[16777216]{0:T(1024)(128)(4,1)} %bitcast.4), calls=%async_computation | async-start | bytes 8388608
  12.6 11.2 %slice-start.1 = ((s8[16777216]{0:T(1024)(128)(4,1)}), s8[4194304]{0:T(1024)(128)(4,1)S(1)}, s32[]{:S(2)}) async-start(s8[16777216]{0:T(1024)(128)(4,1)} %bitcast.4), calls=%async_computation.1 | async-start | bytes 8388608
  15.8 8.0 %slice-start.2 = ((s8[16777216]{0:T(1024)(128)(4,1)}), s8[4194304]{0:T(1024)(128)(4,1)S(1)}, s32[]{:S(2)}) async-start(s8[16777216]{0:T(1024)(128)(4,1)} %bitcast.4), calls=%async_computation.2 | async-start | bytes 8388608
  15.8 5.3 %collective-permute-start.6 = (bf16[2,5,64,128]{3,2,1,0:T(8,128)(2,1)S(1)}, bf16[2,5,64,128]{3,2,1,0:T(8,128)(2,1)S(1)}, u32[]{:S(2)}, u32[]{:S(2)}) collective-permute-start(bf16[2,5,64,128]{3,2,1,0:T(8,128)(2,1)S(1)} %collective-permute-done.3.refs_3_), channel_id=1, source_target_pairs={{0,8},{1,9},{2,0},{3,1},{4,6},{5,7},{6,14},{7,15},{8,16},{9,17},{1... | collective-permute-start | bytes 491528 | tf_op jit(solution)/shard_map/ppermute | solution.py:631
  17.3 3.7 %collective-permute-start.8 = (bf16[2,5,64,128]{3,2,1,0:T(8,128)(2,1)S(1)}, bf16[2,5,64,128]{3,2,1,0:T(8,128)(2,1)S(1)}, u32[]{:S(2)}, u32[]{:S(2)}) collective-permute-start(bf16[2,5,64,128]{3,2,1,0:T(8,128)(2,1)S(1)} %collective-permute-done.3.refs_3_), channel_id=1, source_target_pairs={{0,4},{1,5},{2,6},{3,7},{4,0},{5,1},{6,2},{7,3},{8,12},{9,13},{10,... | collective-permute-start | bytes 491528 | tf_op jit(solution)/shard_map/ppermute | solution.py:630
  17.3 9.4 %collective-permute-start.10 = (bf16[2,5,64,128]{3,2,1,0:T(8,128)(2,1)S(1)}, bf16[2,5,64,128]{3,2,1,0:T(8,128)(2,1)S(1)}, u32[]{:S(2)}, u32[]{:S(2)}) collective-permute-start(bf16[2,5,64,128]{3,2,1,0:T(8,128)(2,1)S(1)} %collective-permute-done.3.refs_3_), channel_id=1, source_target_pairs={{0,1},{1,0},{2,3},{3,2},{4,5},{5,4},{6,7},{7,6},{8,9},{9,8},{10,11... | collective-permute-start | bytes 491528 | tf_op jit(solution)/shard_map/ppermute | solution.py:629
  17.9 5.8 %slice-start.3 = ((s8[16777216]{0:T(1024)(128)(4,1)}), s8[4194304]{0:T(1024)(128)(4,1)S(1)}, s32[]{:S(2)}) async-start(s8[16777216]{0:T(1024)(128)(4,1)} %bitcast.4), calls=%async_computation.3 | async-start | bytes 8388608
  17.9 5.8 %copy-start = (bf16[4,8,4096]{2,1,0:T(8,128)(2,1)S(1)}, bf16[4,8,4096]{2,1,0:T(8,128)(2,1)}, u32[]{:S(2)}) copy-start(bf16[4,8,4096]{2,1,0:T(8,128)(2,1)} %param.8) | copy-start | bytes 786436
  21.1 5.6 %collective-permute-start.9 = (bf16[2,5,64,128]{3,2,1,0:T(8,128)(2,1)S(1)}, bf16[2,5,64,128]{3,2,1,0:T(8,128)(2,1)S(1)}, u32[]{:S(2)}, u32[]{:S(2)}) collective-permute-start(bf16[2,5,64,128]{3,2,1,0:T(8,128)(2,1)S(1)} %collective-permute-done.6.refs_5_), channel_id=1, source_target_pairs={{0,8},{1,9},{2,0},{3,1},{4,6},{5,7},{6,14},{7,15},{8,16},{9,17},{1... | collective-permute-start | bytes 491528 | tf_op jit(solution)/shard_map/ppermute | solution.py:631
  22.7 4.1 %collective-permute-start.11 = (bf16[2,5,64,128]{3,2,1,0:T(8,128)(2,1)S(1)}, bf16[2,5,64,128]{3,2,1,0:T(8,128)(2,1)S(1)}, u32[]{:S(2)}, u32[]{:S(2)}) collective-permute-start(bf16[2,5,64,128]{3,2,1,0:T(8,128)(2,1)S(1)} %collective-permute-done.6.refs_5_), channel_id=1, source_target_pairs={{0,4},{1,5},{2,6},{3,7},{4,0},{5,1},{6,2},{7,3},{8,12},{9,13},{10,... | collective-permute-start | bytes 491528 | tf_op jit(solution)/shard_map/ppermute | solution.py:630
  22.7 4.1 %collective-permute-start.12 = (bf16[2,5,64,128]{3,2,1,0:T(8,128)(2,1)S(1)}, bf16[2,5,64,128]{3,2,1,0:T(8,128)(2,1)S(1)}, u32[]{:S(2)}, u32[]{:S(2)}) collective-permute-start(bf16[2,5,64,128]{3,2,1,0:T(8,128)(2,1)S(1)} %collective-permute-done.7.refs_1_), channel_id=1, source_target_pairs={{0,4},{1,5},{2,6},{3,7},{4,0},{5,1},{6,2},{7,3},{8,12},{9,13},{10,... | collective-permute-start | bytes 491528 | tf_op jit(solution)/shard_map/ppermute | solution.py:628
  23.2 9.3 %collective-permute-start.15 = (bf16[2,5,64,128]{3,2,1,0:T(8,128)(2,1)S(1)}, bf16[2,5,64,128]{3,2,1,0:T(8,128)(2,1)S(1)}, u32[]{:S(2)}, u32[]{:S(2)}) collective-permute-start(bf16[2,5,64,128]{3,2,1,0:T(8,128)(2,1)S(1)} %collective-permute-done.6.refs_5_), channel_id=1, source_target_pairs={{0,1},{1,0},{2,3},{3,2},{4,5},{5,4},{6,7},{7,6},{8,9},{9,8},{10,11... | collective-permute-start | bytes 491528 | tf_op jit(solution)/shard_map/ppermute | solution.py:629
  26.7 9.1 %collective-permute-start.13 = (bf16[2,5,64,128]{3,2,1,0:T(8,128)(2,1)S(1)}, bf16[2,5,64,128]{3,2,1,0:T(8,128)(2,1)S(1)}, u32[]{:S(2)}, u32[]{:S(2)}) collective-permute-start(bf16[2,5,64,128]{3,2,1,0:T(8,128)(2,1)S(1)} %collective-permute-done.9.refs_7_), channel_id=1, source_target_pairs={{0,1},{1,0},{2,3},{3,2},{4,5},{5,4},{6,7},{7,6},{8,9},{9,8},{10,11... | collective-permute-start | bytes 491528 | tf_op jit(solution)/shard_map/ppermute | solution.py:654
  32.5 3.3 %collective-permute-start.16 = (bf16[2,5,64,128]{3,2,1,0:T(8,128)(2,1)S(1)}, bf16[2,5,64,128]{3,2,1,0:T(8,128)(2,1)S(1)}, u32[]{:S(2)}, u32[]{:S(2)}) collective-permute-start(bf16[2,5,64,128]{3,2,1,0:T(8,128)(2,1)S(1)} %collective-permute-done.15.refs_4_), channel_id=1, source_target_pairs={{0,4},{1,5},{2,6},{3,7},{4,0},{5,1},{6,2},{7,3},{8,12},{9,13},{10,... | collective-permute-start | bytes 491528 | tf_op jit(solution)/shard_map/ppermute | solution.py:659
  32.6 3.3 %collective-permute-start.14 = (bf16[2,5,64,128]{3,2,1,0:T(8,128)(2,1)S(1)}, bf16[2,5,64,128]{3,2,1,0:T(8,128)(2,1)S(1)}, u32[]{:S(2)}, u32[]{:S(2)}) collective-permute-start(bf16[2,5,64,128]{3,2,1,0:T(8,128)(2,1)S(1)} %collective-permute-done.10.refs_3_), channel_id=1, source_target_pairs={{0,4},{1,5},{2,6},{3,7},{4,0},{5,1},{6,2},{7,3},{8,12},{9,13},{10,... | collective-permute-start | bytes 491528 | tf_op jit(solution)/shard_map/ppermute | solution.py:655

commit v3 on v2

--- a/solution.py
+++ b/solution.py
@@ -477,9 +477,13 @@
                 )
                 w = weights[k, pl.ds(start + begin, chunk), cols]
                 m_buf[j, rows, cols] = (w.astype(jnp.float32) + added).astype(jnp.bfloat16)
-        copy = pltpu.make_async_copy(m_buf.at[j], m_hbm.at[k, pl.ds(start, depth), :], sems.at[j])
-        copy.start()
-        copies.append(copy)
+            copy = pltpu.make_async_copy(
+                m_buf.at[j, pl.ds(begin, chunk)],
+                m_hbm.at[k, pl.ds(start + begin, chunk), :],
+                sems.at[j, begin // chunk],
+            )
+            copy.start()
+            copies.append(copy)
 
     if not last:
         low[...] = jnp.zeros_like(low) if first else low_in[...]
@@ -534,7 +538,8 @@
     low_shape = (pairs, tokens, rank)
     operands = [e[3] for e in entries] + [pinned(states, pltpu.VMEM), pinned(weights, pltpu.VMEM)]
     specs = [VMEM] * len(operands)
-    scratch = [pltpu.VMEM((n, depth, width), jnp.bfloat16), pltpu.SemaphoreType.DMA((n,))]
+    scratch = [pltpu.VMEM((n, depth, width), jnp.bfloat16)]
+    scratch.append(pltpu.SemaphoreType.DMA((n, max(1, depth // 256))))
     aliases = {}
     n_caches, scale = 0, 0.0
     if state is not None and final is None:

time: 39.1 us -> 39.1 us (level)
  waiting for transfers between devices: 3.35 us -> 4.16 us
  Pallas kernels: 20.5 us -> 19.7 us
    pallas_call x3, Pallas kernels: 6.54 us -> 5.72 us  [cache_attention(): pl.pallas_call(functools.partial(attend_cache, pairs, ready, sizes, scale...]
    ppermute x3, waiting for transfers between devices: 3.17 us -> 3.91 us  [shards(): sent = send(came, perm=ring)]
  transfers between devices with their start and end apart: 17 -> 17, of which waited for: 3 -> 4; matrix products, arithmetic and copies ran while one was open for 0% -> 0% of each run, Pallas kernels for 45% -> 43%
where the time goes in v3:
time: 39.1 us; the launch traced here: 38.9 us
  Pallas kernels  19.7 us (50%)
  starting transfers between devices  14 us (36%)
  waiting for transfers between devices  4.16 us (11%)
  between operations  0.97 us (2%)
    pallas_call x3, Pallas kernels, merge(): pl.pallas_call(functools.partial(merge_some, lay, [e[:3] for e in entries...  9.8 us
    pallas_call x3, Pallas kernels, cache_attention(): pl.pallas_call(functools.partial(attend_cache, pairs, ready, sizes, scale...  5.72 us
    ppermute x3, starting transfers between devices, shards(): sent = send(came, perm=ring)  4.78 us
    ppermute x3, waiting for transfers between devices, shards(): sent = send(came, perm=ring)  3.91 us
    pallas_call x1, Pallas kernels, project(): pl.pallas_call(functools.partial(project_old, lay, len(hidden)), out_shap...  2.96 us
    ppermute x1, starting transfers between devices, shards(): sent = send(pair, perm=ring)  2.91 us
    ppermute x3, starting transfers between devices, shards(): across = [(step, send(came, perm=planes))]  1.61 us
    ppermute x1, starting transfers between devices, shards(): late = [(last_step, 0, 1, send(came, perm=planes))]  1.56 us
  transfers between devices with their start and end apart: 17, of which 4 were waited for; matrix products, arithmetic and copies ran while one was open for 0% of the time, Pallas kernels for 43%

profile of v3, /device:TPU:0, one launch (start us, length us, event | category | flops | bytes accessed | tf_op | source)
XLA Modules:
  0.0 38.9 jit_solution(15648785522710268488)
XLA Ops:
  0.6 0.5 %collective-permute-start = (bf16[2,64,512]{2,1,0:T(8,128)(2,1)}, bf16[2,64,512]{2,1,0:T(8,128)(2,1)S(1)}, u32[]{:S(2)}, u32[]{:S(2)}) collective-permute-start(bf16[2,64,512]{2,1,0:T(8,128)(2,1)} %bitcast.14), channel_id=1, source_target_pairs={{0,4},{1,5},{2,6},{3,7},{4,0},{5,1},{6,2},{7,3},{8,12},{9,13},{10,... | collective-permute-start | bytes 393224 | tf_op jit(solution)/shard_map/ppermute | solution.py:614
  1.1 0.1 collective-permute-start.1
  1.2 1.2 %begin.1 = (bf16[2,5,64,128]{3,2,1,0:T(8,128)(2,1)S(1)}, bf16[2,4,64,128]{3,2,1,0:T(8,128)(2,1)S(1)}, s32[8]{0:T(128)S(4)}, s32[8]{0:T(128)S(4)}, bf16[4,8,32,128]{3,2,1,0:T(8,128)(2,1)S(1)}) custom-call(bf16[2,64,512]{2,1,0:T(8,128)(2,1)} %bitcast.15, bf16[2,64,64]{2,1,0:T(8,128)(2,1)} %up.1, s32[8]{0:T(128)} %len_hbm.1, bf16[4,8,32,128]{3,2,1,0:T(8,128)(2,1)} %q_hbm.1), custom_call_target="tpu_custom_call" | custom-call | flops 600000000 | bytes 10000000 | tf_op jit(solution)/shard_map/begin/pallas_call | solution.py:147
  2.4 0.1 collective-permute-done.1.up
  2.6 0.0 collective-permute-done.down
  2.6 0.1 pack_other.1
  2.6 2.9 %collective-permute-start.2 = (bf16[2,5,64,128]{3,2,1,0:T(8,128)(2,1)S(1)}, bf16[2,5,64,128]{3,2,1,0:T(8,128)(2,1)S(1)}, u32[]{:S(2)}, u32[]{:S(2)}) collective-permute-start(bf16[2,5,64,128]{3,2,1,0:T(8,128)(2,1)S(1)} %get-tuple-element.55.refs_5_.refs_0_), channel_id=1, source_target_pairs={{0,8},{1,9},{2,0},{3,1},{4,6},{5,7},{6,14},{7,15},{8,16},{9,17},{1... | collective-permute-start | bytes 491528 | tf_op jit(solution)/shard_map/ppermute | solution.py:626
  5.6 1.5 %collective-permute-start.4 = (bf16[32,4096]{1,0:T(8,128)(2,1)}, bf16[32,4096]{1,0:T(8,128)(2,1)S(1)}, u32[]{:S(2)}, u32[]{:S(2)}) collective-permute-start(bf16[32,4096]{1,0:T(8,128)(2,1)} %bitcast.6), channel_id=1, source_target_pairs={{1,0},{0,1},{3,2},{2,3},{5,4},{4,5},{7,6},{6,7},{9,8},{8,9},{11,10... | collective-permute-start | bytes 786440 | tf_op jit(solution)/shard_map/ppermute | solution.py:627
  7.0 3.3 %cache_attention.3 = (bf16[8,3072,128]{2,1,0:T(8,128)(2,1)S(1)}, bf16[8,3072,128]{2,1,0:T(8,128)(2,1)S(1)}, f32[2,128,128]{2,1,0:T(8,128)S(1)}, f32[2,128,128]{2,1,0:T(8,128)S(1)}) custom-call(s32[8]{0:T(128)S(4)} %get-tuple-element.56.refs_0_, s32[8]{0:T(128)S(4)} %get-tuple-element.57.refs_1_.refs_6_, ...), custom_call_target="tpu_custom_call" | custom-call | flops 600000000 | bytes 10000000 | tf_op jit(solution)/shard_map/cache_attention/pallas_call | solution.py:298
  10.4 0.0 collective-permute-done.2.refs_1_
  10.4 1.6 %collective-permute-start.3 = (bf16[2,5,64,128]{3,2,1,0:T(8,128)(2,1)S(1)}, bf16[2,5,64,128]{3,2,1,0:T(8,128)(2,1)S(1)}, u32[]{:S(2)}, u32[]{:S(2)}) collective-permute-start(bf16[2,5,64,128]{3,2,1,0:T(8,128)(2,1)S(1)} %collective-permute-done.2.refs_1_), channel_id=1, source_target_pairs={{0,8},{1,9},{2,0},{3,1},{4,6},{5,7},{6,14},{7,15},{8,16},{9,17},{1... | collective-permute-start | bytes 491528 | tf_op jit(solution)/shard_map/ppermute | solution.py:636
  12.0 0.0 collective-permute-start.5
  12.0 0.5 %collective-permute-start.7 = (bf16[2,5,64,128]{3,2,1,0:T(8,128)(2,1)S(1)}, bf16[2,5,64,128]{3,2,1,0:T(8,128)(2,1)S(1)}, u32[]{:S(2)}, u32[]{:S(2)}) collective-permute-start(bf16[2,5,64,128]{3,2,1,0:T(8,128)(2,1)S(1)} %collective-permute-done.2.refs_1_), channel_id=1, source_target_pairs={{0,1},{1,0},{2,3},{3,2},{4,5},{5,4},{6,7},{7,6},{8,9},{9,8},{10,11... | collective-permute-start | bytes 491528 | tf_op jit(solution)/shard_map/ppermute | solution.py:634
  12.6 1.2 %cache_attention.4 = (bf16[8,3072,128]{2,1,0:T(8,128)(2,1)S(1)}, bf16[8,3072,128]{2,1,0:T(8,128)(2,1)S(1)}, f32[2,128,128]{2,1,0:T(8,128)S(1)}, f32[2,128,128]{2,1,0:T(8,128)S(1)}) custom-call(s32[8]{0:T(128)S(4)} %get-tuple-element.56.refs_0_, s32[8]{0:T(128)S(4)} %get-tuple-element.57.refs_1_.refs_6_, ...), custom_call_target="tpu_custom_call", output_to_operand_aliasing={{0}: (5, {}), {1}: (6, {})} | custom-call | flops 600000000 | bytes 10000000 | tf_op jit(solution)/shard_map/cache_attention/pallas_call | solution.py:298
  13.7 0.1 collective-permute-done.4.refs_2_
  13.8 1.9 %collective-permute-done.3.refs_3_ = bf16[2,5,64,128]{3,2,1,0:T(8,128)(2,1)S(1)} collective-permute-done((bf16[2,5,64,128]{3,2,1,0:T(8,128)(2,1)S(1)}, bf16[2,5,64,128]{3,2,1,0:T(8,128)(2,1)S(1)}, u32[]{:S(2)}, u32[]{:S(2)}) %collective-permute-start.3) | collective-permute-done | bytes 163872 | tf_op jit(solution)/shard_map/ppermute | solution.py:636
  15.8 0.0 collective-permute-done.5.refs_2_
  15.8 1.6 %collective-permute-start.6 = (bf16[2,5,64,128]{3,2,1,0:T(8,128)(2,1)S(1)}, bf16[2,5,64,128]{3,2,1,0:T(8,128)(2,1)S(1)}, u32[]{:S(2)}, u32[]{:S(2)}) collective-permute-start(bf16[2,5,64,128]{3,2,1,0:T(8,128)(2,1)S(1)} %collective-permute-done.3.refs_3_), channel_id=1, source_target_pairs={{0,8},{1,9},{2,0},{3,1},{4,6},{5,7},{6,14},{7,15},{8,16},{9,17},{1... | collective-permute-start | bytes 491528 | tf_op jit(solution)/shard_map/ppermute | solution.py:636
  17.3 0.0 collective-permute-start.8
  17.3 0.5 %collective-permute-start.10 = (bf16[2,5,64,128]{3,2,1,0:T(8,128)(2,1)S(1)}, bf16[2,5,64,128]{3,2,1,0:T(8,128)(2,1)S(1)}, u32[]{:S(2)}, u32[]{:S(2)}) collective-permute-start(bf16[2,5,64,128]{3,2,1,0:T(8,128)(2,1)S(1)} %collective-permute-done.3.refs_3_), channel_id=1, source_target_pairs={{0,1},{1,0},{2,3},{3,2},{4,5},{5,4},{6,7},{7,6},{8,9},{9,8},{10,11... | collective-permute-start | bytes 491528 | tf_op jit(solution)/shard_map/ppermute | solution.py:634
  17.9 1.2 %cache_attention.5 = (bf16[8,3072,128]{2,1,0:T(8,128)(2,1)S(1)}, bf16[8,3072,128]{2,1,0:T(8,128)(2,1)S(1)}, f32[4,128,128]{2,1,0:T(8,128)S(1)}, f32[4,128,128]{2,1,0:T(8,128)S(1)}) custom-call(s32[8]{0:T(128)S(4)} %get-tuple-element.56.refs_0_, s32[8]{0:T(128)S(4)} %get-tuple-element.57.refs_1_.refs_6_, ...), custom_call_target="tpu_custom_call", output_to_operand_aliasing={{0}: (5, {}), {1}: (6, {})} | custom-call | flops 600000000 | bytes 10000000 | tf_op jit(solution)/shard_map/cache_attention/pallas_call | solution.py:298
  19.1 0.0 collective-permute-done.7.refs_1_
  19.1 2.0 %collective-permute-done.6.refs_5_ = bf16[2,5,64,128]{3,2,1,0:T(8,128)(2,1)S(1)} collective-permute-done((bf16[2,5,64,128]{3,2,1,0:T(8,128)(2,1)S(1)}, bf16[2,5,64,128]{3,2,1,0:T(8,128)(2,1)S(1)}, u32[]{:S(2)}, u32[]{:S(2)}) %collective-permute-start.6) | collective-permute-done | bytes 163872 | tf_op jit(solution)/shard_map/ppermute | solution.py:636
  21.1 0.0 collective-permute-done.8.refs_4_
  21.1 1.6 %collective-permute-start.9 = (bf16[2,5,64,128]{3,2,1,0:T(8,128)(2,1)S(1)}, bf16[2,5,64,128]{3,2,1,0:T(8,128)(2,1)S(1)}, u32[]{:S(2)}, u32[]{:S(2)}) collective-permute-start(bf16[2,5,64,128]{3,2,1,0:T(8,128)(2,1)S(1)} %collective-permute-done.6.refs_5_), channel_id=1, source_target_pairs={{0,8},{1,9},{2,0},{3,1},{4,6},{5,7},{6,14},{7,15},{8,16},{9,17},{1... | collective-permute-start | bytes 491528 | tf_op jit(solution)/shard_map/ppermute | solution.py:636
  22.7 0.0 collective-permute-start.11
  22.7 0.5 %collective-permute-start.12 = (bf16[2,5,64,128]{3,2,1,0:T(8,128)(2,1)S(1)}, bf16[2,5,64,128]{3,2,1,0:T(8,128)(2,1)S(1)}, u32[]{:S(2)}, u32[]{:S(2)}) collective-permute-start(bf16[2,5,64,128]{3,2,1,0:T(8,128)(2,1)S(1)} %collective-permute-done.7.refs_1_), channel_id=1, source_target_pairs={{0,4},{1,5},{2,6},{3,7},{4,0},{5,1},{6,2},{7,3},{8,12},{9,13},{10,... | collective-permute-start | bytes 491528 | tf_op jit(solution)/shard_map/ppermute | solution.py:633
  23.2 0.5 %collective-permute-start.15 = (bf16[2,5,64,128]{3,2,1,0:T(8,128)(2,1)S(1)}, bf16[2,5,64,128]{3,2,1,0:T(8,128)(2,1)S(1)}, u32[]{:S(2)}, u32[]{:S(2)}) collective-permute-start(bf16[2,5,64,128]{3,2,1,0:T(8,128)(2,1)S(1)} %collective-permute-done.6.refs_5_), channel_id=1, source_target_pairs={{0,1},{1,0},{2,3},{3,2},{4,5},{5,4},{6,7},{7,6},{8,9},{9,8},{10,11... | collective-permute-start | bytes 491528 | tf_op jit(solution)/shard_map/ppermute | solution.py:634
  23.7 0.0 slice-done
  23.7 0.0 slice-done.1
  23.7 0.0 slice-done.2
  23.7 0.0 slice-done.3
  23.7 0.0 copy-done
  23.7 3.0 %project.1 = (f32[2,32,512]{2,1,0:T(8,128)S(1)}, bf16[2,32,4096]{2,1,0:T(8,128)(2,1)S(1)}) custom-call(bf16[2,8192,512]{2,1,0:T(8,128)(2,1)S(1)} %bitcast.5, bf16[32,4096]{1,0:T(8,128)(2,1)S(1)} %bitcast.7, bf16[32,4096]{1,0:T(8,128)(2,1)S(1)} %collective-permute-done.4.refs_2_, f32[4,128,128]{2,1,0:T(8,128)S(1)} %get-tuple-element.75.refs_3_.refs_12_), custom_call_target="tpu_custom_call" | custom-call | flops 600000000 | bytes 10000000 | tf_op jit(solution)/shard_map/project/pallas_call | solution.py:336
  26.7 0.0 collective-permute-done.10.refs_3_
  26.7 0.0 collective-permute-done.9.refs_7_
  26.7 0.0 collective-permute-done.11.refs_6_
  26.7 0.0 collective-permute-done.12.refs_2_
  26.7 1.6 %collective-permute-start.13 = (bf16[2,5,64,128]{3,2,1,0:T(8,128)(2,1)S(1)}, bf16[2,5,64,128]{3,2,1,0:T(8,128)(2,1)S(1)}, u32[]{:S(2)}, u32[]{:S(2)}) collective-permute-start(bf16[2,5,64,128]{3,2,1,0:T(8,128)(2,1)S(1)} %collective-permute-done.9.refs_7_), channel_id=1, source_target_pairs={{0,1},{1,0},{2,3},{3,2},{4,5},{5,4},{6,7},{7,6},{8,9},{9,8},{10,11... | collective-permute-start | bytes 491528 | tf_op jit(solution)/shard_map/ppermute | solution.py:659
  28.3 4.2 %merge.3 = (bf16[2,8192,512]{2,1,0:T(8,128)(2,1)}, bf16[2,64,512]{2,1,0:T(8,128)(2,1)S(1)}, f32[2,32,64]{2,1,0:T(8,128)S(1)}) custom-call(bf16[2,5,64,128]{3,2,1,0:T(8,128)(2,1)S(1)} %get-tuple-element.55.refs_5_.refs_0_, bf16[2,5,64,128]{3,2,1,0:T(8,128)(2,1)S(1)} %collective-permute-done.2.refs_1_, ...), custom_call_target="tpu_custom_call" | custom-call | flops 600000000 | bytes 10000000 | tf_op jit(solution)/shard_map/merge/pallas_call | solution.py:576
  32.5 0.0 collective-permute-done.15.refs_4_
  32.5 0.1 collective-permute-start.16
  32.6 0.5 %collective-permute-start.14 = (bf16[2,5,64,128]{3,2,1,0:T(8,128)(2,1)S(1)}, bf16[2,5,64,128]{3,2,1,0:T(8,128)(2,1)S(1)}, u32[]{:S(2)}, u32[]{:S(2)}) collective-permute-start(bf16[2,5,64,128]{3,2,1,0:T(8,128)(2,1)S(1)} %collective-permute-done.10.refs_3_), channel_id=1, source_target_pairs={{0,4},{1,5},{2,6},{3,7},{4,0},{5,1},{6,2},{7,3},{8,12},{9,13},{10,... | collective-permute-start | bytes 491528 | tf_op jit(solution)/shard_map/ppermute | solution.py:660
  33.1 2.7 %merge.4 = (bf16[2,8192,512]{2,1,0:T(8,128)(2,1)}, f32[2,32,64]{2,1,0:T(8,128)S(1)}) custom-call(bf16[2,4,64,128]{3,2,1,0:T(8,128)(2,1)S(1)} %get-tuple-element.90.refs_0_, bf16[2,5,64,128]{3,2,1,0:T(8,128)(2,1)S(1)} %collective-permute-done.7.refs_1_, bf16[2,5,64,128]{3,2,1,0:T(8,128)(2,1)S(1)} %collective-permute-done.12.refs_2_, ...), custom_call_target="tpu_custom_call", output_to_operand_aliasing={{0}: (9, {})} | custom-call | flops 600000000 | bytes 10000000 | tf_op jit(solution)/shard_map/merge/pallas_call | solution.py:576
  35.9 0.0 collective-permute-done.16.refs_2_
  35.9 0.0 collective-permute-done.13.refs_0_
  35.9 0.0 collective-permute-done.14.refs_1_
  35.9 2.8 %merge.5 = (bf16[2,8192,512]{2,1,0:T(8,128)(2,1)}, bf16[4,8,32,128]{3,2,1,0:T(8,128)(2,1)}) custom-call(bf16[2,5,64,128]{3,2,1,0:T(8,128)(2,1)S(1)} %collective-permute-done.13.refs_0_, bf16[2,5,64,128]{3,2,1,0:T(8,128)(2,1)S(1)} %collective-permute-done.14.refs_1_, ...), custom_call_target="tpu_custom_call", output_to_operand_aliasing={{0}: (16, {})} | custom-call | flops 600000000 | bytes 10000000 | tf_op jit(solution)/shard_map/merge/pallas_call | solution.py:576
  (6 shorter events, 0.0 us)
Async XLA Ops:
  0.6 1.9 %collective-permute-start = (bf16[2,64,512]{2,1,0:T(8,128)(2,1)}, bf16[2,64,512]{2,1,0:T(8,128)(2,1)S(1)}, u32[]{:S(2)}, u32[]{:S(2)}) collective-permute-start(bf16[2,64,512]{2,1,0:T(8,128)(2,1)} %bitcast.14), channel_id=1, source_target_pairs={{0,4},{1,5},{2,6},{3,7},{4,0},{5,1},{6,2},{7,3},{8,12},{9,13},{10,... | collective-permute-start | bytes 393224 | tf_op jit(solution)/shard_map/ppermute | solution.py:614
  1.1 1.4 %collective-permute-start.1 = (bf16[2,64,64]{2,1,0:T(8,128)(2,1)}, bf16[2,64,64]{2,1,0:T(8,128)(2,1)S(1)}, u32[]{:S(2)}, u32[]{:S(2)}) collective-permute-start(bf16[2,64,64]{2,1,0:T(8,128)(2,1)} %up.1), channel_id=1, source_target_pairs={{0,4},{1,5},{2,6},{3,7},{4,0},{5,1},{6,2},{7,3},{8,12},{9,13},{10,... | collective-permute-start | bytes 49160 | tf_op jit(solution)/shard_map/ppermute | solution.py:614
  2.6 7.7 %collective-permute-start.2 = (bf16[2,5,64,128]{3,2,1,0:T(8,128)(2,1)S(1)}, bf16[2,5,64,128]{3,2,1,0:T(8,128)(2,1)S(1)}, u32[]{:S(2)}, u32[]{:S(2)}) collective-permute-start(bf16[2,5,64,128]{3,2,1,0:T(8,128)(2,1)S(1)} %get-tuple-element.55.refs_5_.refs_0_), channel_id=1, source_target_pairs={{0,8},{1,9},{2,0},{3,1},{4,6},{5,7},{6,14},{7,15},{8,16},{9,17},{1... | collective-permute-start | bytes 491528 | tf_op jit(solution)/shard_map/ppermute | solution.py:626
  5.6 8.3 %collective-permute-start.4 = (bf16[32,4096]{1,0:T(8,128)(2,1)}, bf16[32,4096]{1,0:T(8,128)(2,1)S(1)}, u32[]{:S(2)}, u32[]{:S(2)}) collective-permute-start(bf16[32,4096]{1,0:T(8,128)(2,1)} %bitcast.6), channel_id=1, source_target_pairs={{1,0},{0,1},{3,2},{2,3},{5,4},{4,5},{7,6},{6,7},{9,8},{8,9},{11,10... | collective-permute-start | bytes 786440 | tf_op jit(solution)/shard_map/ppermute | solution.py:627
  10.4 5.4 %collective-permute-start.3 = (bf16[2,5,64,128]{3,2,1,0:T(8,128)(2,1)S(1)}, bf16[2,5,64,128]{3,2,1,0:T(8,128)(2,1)S(1)}, u32[]{:S(2)}, u32[]{:S(2)}) collective-permute-start(bf16[2,5,64,128]{3,2,1,0:T(8,128)(2,1)S(1)} %collective-permute-done.2.refs_1_), channel_id=1, source_target_pairs={{0,8},{1,9},{2,0},{3,1},{4,6},{5,7},{6,14},{7,15},{8,16},{9,17},{1... | collective-permute-start | bytes 491528 | tf_op jit(solution)/shard_map/ppermute | solution.py:636
  12.0 3.7 %collective-permute-start.5 = (bf16[2,5,64,128]{3,2,1,0:T(8,128)(2,1)S(1)}, bf16[2,5,64,128]{3,2,1,0:T(8,128)(2,1)S(1)}, u32[]{:S(2)}, u32[]{:S(2)}) collective-permute-start(bf16[2,5,64,128]{3,2,1,0:T(8,128)(2,1)S(1)} %collective-permute-done.2.refs_1_), channel_id=1, source_target_pairs={{0,4},{1,5},{2,6},{3,7},{4,0},{5,1},{6,2},{7,3},{8,12},{9,13},{10,... | collective-permute-start | bytes 491528 | tf_op jit(solution)/shard_map/ppermute | solution.py:635
  12.0 7.1 %collective-permute-start.7 = (bf16[2,5,64,128]{3,2,1,0:T(8,128)(2,1)S(1)}, bf16[2,5,64,128]{3,2,1,0:T(8,128)(2,1)S(1)}, u32[]{:S(2)}, u32[]{:S(2)}) collective-permute-start(bf16[2,5,64,128]{3,2,1,0:T(8,128)(2,1)S(1)} %collective-permute-done.2.refs_1_), channel_id=1, source_target_pairs={{0,1},{1,0},{2,3},{3,2},{4,5},{5,4},{6,7},{7,6},{8,9},{9,8},{10,11... | collective-permute-start | bytes 491528 | tf_op jit(solution)/shard_map/ppermute | solution.py:634
  12.6 11.2 %slice-start = ((s8[16777216]{0:T(1024)(128)(4,1)}), s8[4194304]{0:T(1024)(128)(4,1)S(1)}, s32[]{:S(2)}) async-start(s8[16777216]{0:T(1024)(128)(4,1)} %bitcast.4), calls=%async_computation | async-start | bytes 8388608
  12.6 11.2 %slice-start.1 = ((s8[16777216]{0:T(1024)(128)(4,1)}), s8[4194304]{0:T(1024)(128)(4,1)S(1)}, s32[]{:S(2)}) async-start(s8[16777216]{0:T(1024)(128)(4,1)} %bitcast.4), calls=%async_computation.1 | async-start | bytes 8388608
  15.8 8.0 %slice-start.2 = ((s8[16777216]{0:T(1024)(128)(4,1)}), s8[4194304]{0:T(1024)(128)(4,1)S(1)}, s32[]{:S(2)}) async-start(s8[16777216]{0:T(1024)(128)(4,1)} %bitcast.4), calls=%async_computation.2 | async-start | bytes 8388608
  15.8 5.3 %collective-permute-start.6 = (bf16[2,5,64,128]{3,2,1,0:T(8,128)(2,1)S(1)}, bf16[2,5,64,128]{3,2,1,0:T(8,128)(2,1)S(1)}, u32[]{:S(2)}, u32[]{:S(2)}) collective-permute-start(bf16[2,5,64,128]{3,2,1,0:T(8,128)(2,1)S(1)} %collective-permute-done.3.refs_3_), channel_id=1, source_target_pairs={{0,8},{1,9},{2,0},{3,1},{4,6},{5,7},{6,14},{7,15},{8,16},{9,17},{1... | collective-permute-start | bytes 491528 | tf_op jit(solution)/shard_map/ppermute | solution.py:636
  17.3 3.7 %collective-permute-start.8 = (bf16[2,5,64,128]{3,2,1,0:T(8,128)(2,1)S(1)}, bf16[2,5,64,128]{3,2,1,0:T(8,128)(2,1)S(1)}, u32[]{:S(2)}, u32[]{:S(2)}) collective-permute-start(bf16[2,5,64,128]{3,2,1,0:T(8,128)(2,1)S(1)} %collective-permute-done.3.refs_3_), channel_id=1, source_target_pairs={{0,4},{1,5},{2,6},{3,7},{4,0},{5,1},{6,2},{7,3},{8,12},{9,13},{10,... | collective-permute-start | bytes 491528 | tf_op jit(solution)/shard_map/ppermute | solution.py:635
  17.3 9.4 %collective-permute-start.10 = (bf16[2,5,64,128]{3,2,1,0:T(8,128)(2,1)S(1)}, bf16[2,5,64,128]{3,2,1,0:T(8,128)(2,1)S(1)}, u32[]{:S(2)}, u32[]{:S(2)}) collective-permute-start(bf16[2,5,64,128]{3,2,1,0:T(8,128)(2,1)S(1)} %collective-permute-done.3.refs_3_), channel_id=1, source_target_pairs={{0,1},{1,0},{2,3},{3,2},{4,5},{5,4},{6,7},{7,6},{8,9},{9,8},{10,11... | collective-permute-start | bytes 491528 | tf_op jit(solution)/shard_map/ppermute | solution.py:634
  17.9 5.8 %slice-start.3 = ((s8[16777216]{0:T(1024)(128)(4,1)}), s8[4194304]{0:T(1024)(128)(4,1)S(1)}, s32[]{:S(2)}) async-start(s8[16777216]{0:T(1024)(128)(4,1)} %bitcast.4), calls=%async_computation.3 | async-start | bytes 8388608
  17.9 5.8 %copy-start = (bf16[4,8,4096]{2,1,0:T(8,128)(2,1)S(1)}, bf16[4,8,4096]{2,1,0:T(8,128)(2,1)}, u32[]{:S(2)}) copy-start(bf16[4,8,4096]{2,1,0:T(8,128)(2,1)} %param.8) | copy-start | bytes 786436
  21.1 5.6 %collective-permute-start.9 = (bf16[2,5,64,128]{3,2,1,0:T(8,128)(2,1)S(1)}, bf16[2,5,64,128]{3,2,1,0:T(8,128)(2,1)S(1)}, u32[]{:S(2)}, u32[]{:S(2)}) collective-permute-start(bf16[2,5,64,128]{3,2,1,0:T(8,128)(2,1)S(1)} %collective-permute-done.6.refs_5_), channel_id=1, source_target_pairs={{0,8},{1,9},{2,0},{3,1},{4,6},{5,7},{6,14},{7,15},{8,16},{9,17},{1... | collective-permute-start | bytes 491528 | tf_op jit(solution)/shard_map/ppermute | solution.py:636
  22.7 4.1 %collective-permute-start.11 = (bf16[2,5,64,128]{3,2,1,0:T(8,128)(2,1)S(1)}, bf16[2,5,64,128]{3,2,1,0:T(8,128)(2,1)S(1)}, u32[]{:S(2)}, u32[]{:S(2)}) collective-permute-start(bf16[2,5,64,128]{3,2,1,0:T(8,128)(2,1)S(1)} %collective-permute-done.6.refs_5_), channel_id=1, source_target_pairs={{0,4},{1,5},{2,6},{3,7},{4,0},{5,1},{6,2},{7,3},{8,12},{9,13},{10,... | collective-permute-start | bytes 491528 | tf_op jit(solution)/shard_map/ppermute | solution.py:635
  22.7 4.1 %collective-permute-start.12 = (bf16[2,5,64,128]{3,2,1,0:T(8,128)(2,1)S(1)}, bf16[2,5,64,128]{3,2,1,0:T(8,128)(2,1)S(1)}, u32[]{:S(2)}, u32[]{:S(2)}) collective-permute-start(bf16[2,5,64,128]{3,2,1,0:T(8,128)(2,1)S(1)} %collective-permute-done.7.refs_1_), channel_id=1, source_target_pairs={{0,4},{1,5},{2,6},{3,7},{4,0},{5,1},{6,2},{7,3},{8,12},{9,13},{10,... | collective-permute-start | bytes 491528 | tf_op jit(solution)/shard_map/ppermute | solution.py:633
  23.2 9.4 %collective-permute-start.15 = (bf16[2,5,64,128]{3,2,1,0:T(8,128)(2,1)S(1)}, bf16[2,5,64,128]{3,2,1,0:T(8,128)(2,1)S(1)}, u32[]{:S(2)}, u32[]{:S(2)}) collective-permute-start(bf16[2,5,64,128]{3,2,1,0:T(8,128)(2,1)S(1)} %collective-permute-done.6.refs_5_), channel_id=1, source_target_pairs={{0,1},{1,0},{2,3},{3,2},{4,5},{5,4},{6,7},{7,6},{8,9},{9,8},{10,11... | collective-permute-start | bytes 491528 | tf_op jit(solution)/shard_map/ppermute | solution.py:634
  26.7 9.1 %collective-permute-start.13 = (bf16[2,5,64,128]{3,2,1,0:T(8,128)(2,1)S(1)}, bf16[2,5,64,128]{3,2,1,0:T(8,128)(2,1)S(1)}, u32[]{:S(2)}, u32[]{:S(2)}) collective-permute-start(bf16[2,5,64,128]{3,2,1,0:T(8,128)(2,1)S(1)} %collective-permute-done.9.refs_7_), channel_id=1, source_target_pairs={{0,1},{1,0},{2,3},{3,2},{4,5},{5,4},{6,7},{7,6},{8,9},{9,8},{10,11... | collective-permute-start | bytes 491528 | tf_op jit(solution)/shard_map/ppermute | solution.py:659
  32.5 3.3 %collective-permute-start.16 = (bf16[2,5,64,128]{3,2,1,0:T(8,128)(2,1)S(1)}, bf16[2,5,64,128]{3,2,1,0:T(8,128)(2,1)S(1)}, u32[]{:S(2)}, u32[]{:S(2)}) collective-permute-start(bf16[2,5,64,128]{3,2,1,0:T(8,128)(2,1)S(1)} %collective-permute-done.15.refs_4_), channel_id=1, source_target_pairs={{0,4},{1,5},{2,6},{3,7},{4,0},{5,1},{6,2},{7,3},{8,12},{9,13},{10,... | collective-permute-start | bytes 491528 | tf_op jit(solution)/shard_map/ppermute | solution.py:664
  32.6 3.3 %collective-permute-start.14 = (bf16[2,5,64,128]{3,2,1,0:T(8,128)(2,1)S(1)}, bf16[2,5,64,128]{3,2,1,0:T(8,128)(2,1)S(1)}, u32[]{:S(2)}, u32[]{:S(2)}) collective-permute-start(bf16[2,5,64,128]{3,2,1,0:T(8,128)(2,1)S(1)} %collective-permute-done.10.refs_3_), channel_id=1, source_target_pairs={{0,4},{1,5},{2,6},{3,7},{4,0},{5,1},{6,2},{7,3},{8,12},{9,13},{10,... | collective-permute-start | bytes 491528 | tf_op jit(solution)/shard_map/ppermute | solution.py:660

commit v4 on v3

--- a/solution.py
+++ b/solution.py
@@ -394,7 +394,7 @@
     ]
 
 
-def merge_some(lay, plan, first, n_caches, scale, *refs):
+def merge_some(lay, plan, up_plan, first, n_caches, scale, *refs):
     refs = list(refs)
 
     def take(n):
@@ -403,7 +403,7 @@
         return out
 
     last = n_caches > 0
-    downs = take(len(plan))
+    downs, up_only = take(len(plan)), take(len(up_plan))
     h_buf, weights = take(2)
     if last:
         old, order, q_ref = take(3)
@@ -444,7 +444,7 @@
         out_copy.start()
     elif first:
         columns = width // place.per_lane
-        for down, index, _ in groups[0][1]:
+        for down, index, _ in groups[0][1] + place.find(up_plan, up_only):
 
             @pl.when(index // place.per_lane == place.tp)
             def _():
@@ -460,30 +460,36 @@
             )
 
     chunk = min(depth, 256)
+    both = min(len(group) for _, group in groups)
+    turns = [list(pair) for pair in zip(*(group[:both] for _, group in groups))]
+    turns += [[shard] for _, group in groups for shard in group[both:]]
     copies = []
-    for j, (down, index, k) in enumerate(shards):
-        start = pl.multiple_of(index * depth, depth)
+    j = 0
+    for turn in turns:
         for begin in range(0, depth, chunk):
             rows = slice(begin, begin + chunk)
             tile = begin // lanes
-            d = jnp.concatenate([down[tile + i] for i in range(chunk // lanes)], axis=1)
-            for side in range(width // cut):
-                cols = slice(side * cut, (side + 1) * cut)
-                added = lax.dot_general(
-                    d,
-                    u_buf[k, :, cols],
-                    (((0,), (0,)), ((), ())),
-                    preferred_element_type=jnp.float32,
-                )
-                w = weights[k, pl.ds(start + begin, chunk), cols]
-                m_buf[j, rows, cols] = (w.astype(jnp.float32) + added).astype(jnp.bfloat16)
+            for i, (down, index, k) in enumerate(turn):
+                start = pl.multiple_of(index * depth, depth)
+                d = jnp.concatenate([down[tile + i] for i in range(chunk // lanes)], axis=1)
+                for side in range(width // cut):
+                    cols = slice(side * cut, (side + 1) * cut)
+                    added = lax.dot_general(
+                        d,
+                        u_buf[k, :, cols],
+                        (((0,), (0,)), ((), ())),
+                        preferred_element_type=jnp.float32,
+                    )
+                    w = weights[k, pl.ds(start + begin, chunk), cols]
+                    m_buf[j + i, rows, cols] = (w.astype(jnp.float32) + added).astype(jnp.bfloat16)
+        for down, index, k in turn:
+            start = pl.multiple_of(index * depth, depth)
             copy = pltpu.make_async_copy(
-                m_buf.at[j, pl.ds(begin, chunk)],
-                m_hbm.at[k, pl.ds(start + begin, chunk), :],
-                sems.at[j, begin // chunk],
+                m_buf.at[j], m_hbm.at[k, pl.ds(start, depth), :], sems.at[j]
             )
             copy.start()
             copies.append(copy)
+            j += 1
 
     if not last:
         low[...] = jnp.zeros_like(low) if first else low_in[...]
@@ -528,7 +534,7 @@
         out_buf[:, order[spot]] = piece.reshape(steps, heads, size)
 
 
-def merge(lay, shape, entries, states, weights, state, final, after):
+def merge(lay, shape, entries, up_only, states, weights, state, final, after):
     pairs, total, width = shape
     tokens, rank = states.shape[1], entries[0][3].shape[-2]
     depth = total // (lay.fsdp * lay.grp)
@@ -536,10 +542,10 @@
     n = 2 * len(entries)
     merged = pltpu.HBM(shape, jnp.bfloat16)
     low_shape = (pairs, tokens, rank)
-    operands = [e[3] for e in entries] + [pinned(states, pltpu.VMEM), pinned(weights, pltpu.VMEM)]
+    operands = [e[3] for e in entries + up_only]
+    operands += [pinned(states, pltpu.VMEM), pinned(weights, pltpu.VMEM)]
     specs = [VMEM] * len(operands)
-    scratch = [pltpu.VMEM((n, depth, width), jnp.bfloat16)]
-    scratch.append(pltpu.SemaphoreType.DMA((n, max(1, depth // 256))))
+    scratch = [pltpu.VMEM((n, depth, width), jnp.bfloat16), pltpu.SemaphoreType.DMA((n,))]
     aliases = {}
     n_caches, scale = 0, 0.0
     if state is not None and final is None:
@@ -574,7 +580,15 @@
         ]
         n_caches, scale = len(caches) // 2, LOG2E / math.sqrt(queries.shape[3])
     return pl.pallas_call(
-        functools.partial(merge_some, lay, [e[:3] for e in entries], state is None, n_caches, scale),
+        functools.partial(
+            merge_some,
+            lay,
+            [e[:3] for e in entries],
+            [e[:3] for e in up_only],
+            state is None,
+            n_caches,
+            scale,
+        ),
         out_shape=out_shape,
         in_specs=specs + [ANY] * len(after),
         out_specs=out_specs,
@@ -654,21 +668,24 @@
         crossing = across
     weights = projection_weight_matrices
     entries.append((last_step, 0, 0, came))
+    other_plane = [e for e in entries if e[2]]
     own_plane = [e for e in entries if not e[2]]
-    others = [e for e in entries if e[2]]
+    own_plane = own_plane[-1:] + own_plane[:-1]
+    others = own_plane[len(other_plane) :]
+    now = own_plane[: len(other_plane)] + other_plane
     late = [(last_step, 0, 1, send(came, perm=planes))]
     late += [(s, 1, 1, send(x, perm=swap)) for s, x in crossed]
-    m, u, low = merge(lay, shape, own_plane, states, weights, None, None, [token])
+    m, u, low = merge(lay, shape, now, others, states, weights, None, None, [token])
     (step, x), = crossing
     x, low = after_all(x, low)
     late.append((step, 1, 1, send(x, perm=swap)))
     others.append((step, 0, 1, x))
-    m, low = merge(lay, shape, others, states, weights, [m, u, low], None, [])
+    m, low = merge(lay, shape, others, [], states, weights, [m, u, low], None, [])
     arrived, low = after_all([x for _, _, _, x in late], low)
     late = [(*e[:3], x) for e, x in zip(late, arrived)]
     _, order, q = rows_args
     final = (olds, order, q, caches)
-    return tuple(merge(lay, shape, late, states, weights, [m, u, low], final, []))
+    return tuple(merge(lay, shape, late, [], states, weights, [m, u, low], final, []))
 
 
 def solution(mesh):

time: 39.1 us -> 39.4 us (level)
  Pallas kernels: 19.7 us -> 21 us
  waiting for transfers between devices: 4.16 us -> 3.15 us
    pallas_call x3, Pallas kernels: 5.72 us -> 6.71 us  [cache_attention(): pl.pallas_call(functools.partial(attend_cache, pairs, ready, sizes, scale...]
    ppermute x3, waiting for transfers between devices: 3.91 us -> 2.97 us  [shards(): sent = send(came, perm=ring)]
    ppermute x3, starting transfers between devices: 0.01 us -> 0.58 us  [shards(): swapped = send(came, perm=swap)]
    ppermute x1, starting transfers between devices: 0.51 us -> 0.01 us  [shards(): over_there = [(s, send(x, perm=swap)) for s, x in crossed]]
    ppermute x1, starting transfers between devices: 0.5 us -> 0.01 us  [shards(): late += [(s, 1, 1, send(x, perm=swap)) for s, x in crossed]]
    ppermute x1, starting transfers between devices: 0.07 us -> 0.54 us  [shards(): late.append((step, 1, 1, send(x, perm=swap)))]
  transfers between devices with their start and end apart: 17 -> 17, of which waited for: 4 -> 3; matrix products, arithmetic and copies ran while one was open for 0% -> 0% of each run, Pallas kernels for 43% -> 46%
where the time goes in v4:
time: 39.4 us; the launch traced here: 39.2 us
  Pallas kernels  21 us (53%)
  starting transfers between devices  14.1 us (36%)
  waiting for transfers between devices  3.15 us (8%)
  between operations  1 us (3%)
    pallas_call x3, Pallas kernels, merge(): pl.pallas_call(functools.partial(merge_some, lay, [e[:3] for e in entries...  10 us
    pallas_call x3, Pallas kernels, cache_attention(): pl.pallas_call(functools.partial(attend_cache, pairs, ready, sizes, scale...  6.71 us
    ppermute x3, starting transfers between devices, shards(): sent = send(came, perm=ring)  4.79 us
    ppermute x3, waiting for transfers between devices, shards(): sent = send(came, perm=ring)  2.97 us
    pallas_call x1, Pallas kernels, project(): pl.pallas_call(functools.partial(project_old, lay, len(hidden)), out_shap...  2.95 us
    ppermute x1, starting transfers between devices, shards(): sent = send(pair, perm=ring)  2.91 us
    ppermute x3, starting transfers between devices, shards(): across = [(step, send(came, perm=planes))]  1.61 us
    ppermute x1, starting transfers between devices, shards(): late = [(last_step, 0, 1, send(came, perm=planes))]  1.56 us
  transfers between devices with their start and end apart: 17, of which 3 were waited for; matrix products, arithmetic and copies ran while one was open for 0% of the time, Pallas kernels for 46%

profile of v4, /device:TPU:0, one launch (start us, length us, event | category | flops | bytes accessed | tf_op | source)
XLA Modules:
  0.0 39.2 jit_solution(12469504938332420267)
XLA Ops:
  0.6 0.5 %collective-permute-start = (bf16[2,64,512]{2,1,0:T(8,128)(2,1)}, bf16[2,64,512]{2,1,0:T(8,128)(2,1)S(1)}, u32[]{:S(2)}, u32[]{:S(2)}) collective-permute-start(bf16[2,64,512]{2,1,0:T(8,128)(2,1)} %bitcast.14), channel_id=1, source_target_pairs={{0,4},{1,5},{2,6},{3,7},{4,0},{5,1},{6,2},{7,3},{8,12},{9,13},{10,... | collective-permute-start | bytes 393224 | tf_op jit(solution)/shard_map/ppermute | solution.py:628
  1.1 0.1 collective-permute-start.1
  1.2 1.2 %begin.1 = (bf16[2,5,64,128]{3,2,1,0:T(8,128)(2,1)S(1)}, bf16[2,4,64,128]{3,2,1,0:T(8,128)(2,1)S(1)}, s32[8]{0:T(128)S(4)}, s32[8]{0:T(128)S(4)}, bf16[4,8,32,128]{3,2,1,0:T(8,128)(2,1)S(1)}) custom-call(bf16[2,64,512]{2,1,0:T(8,128)(2,1)} %bitcast.15, bf16[2,64,64]{2,1,0:T(8,128)(2,1)} %up.1, s32[8]{0:T(128)} %len_hbm.1, bf16[4,8,32,128]{3,2,1,0:T(8,128)(2,1)} %q_hbm.1), custom_call_target="tpu_custom_call" | custom-call | flops 600000000 | bytes 10000000 | tf_op jit(solution)/shard_map/begin/pallas_call | solution.py:147
  2.4 0.1 collective-permute-done.1.up
  2.6 0.0 collective-permute-done.down
  2.6 0.1 pack_other.1
  2.6 2.9 %collective-permute-start.2 = (bf16[2,5,64,128]{3,2,1,0:T(8,128)(2,1)S(1)}, bf16[2,5,64,128]{3,2,1,0:T(8,128)(2,1)S(1)}, u32[]{:S(2)}, u32[]{:S(2)}) collective-permute-start(bf16[2,5,64,128]{3,2,1,0:T(8,128)(2,1)S(1)} %get-tuple-element.55.refs_5_.refs_1_), channel_id=1, source_target_pairs={{0,8},{1,9},{2,0},{3,1},{4,6},{5,7},{6,14},{7,15},{8,16},{9,17},{1... | collective-permute-start | bytes 491528 | tf_op jit(solution)/shard_map/ppermute | solution.py:640
  5.6 1.5 %collective-permute-start.4 = (bf16[32,4096]{1,0:T(8,128)(2,1)}, bf16[32,4096]{1,0:T(8,128)(2,1)S(1)}, u32[]{:S(2)}, u32[]{:S(2)}) collective-permute-start(bf16[32,4096]{1,0:T(8,128)(2,1)} %bitcast.6), channel_id=1, source_target_pairs={{1,0},{0,1},{3,2},{2,3},{5,4},{4,5},{7,6},{6,7},{9,8},{8,9},{11,10... | collective-permute-start | bytes 786440 | tf_op jit(solution)/shard_map/ppermute | solution.py:641
  7.0 3.3 %cache_attention.3 = (bf16[8,3072,128]{2,1,0:T(8,128)(2,1)S(1)}, bf16[8,3072,128]{2,1,0:T(8,128)(2,1)S(1)}, f32[2,128,128]{2,1,0:T(8,128)S(1)}, f32[2,128,128]{2,1,0:T(8,128)S(1)}) custom-call(s32[8]{0:T(128)S(4)} %get-tuple-element.56.refs_0_, s32[8]{0:T(128)S(4)} %get-tuple-element.57.refs_1_.refs_6_, ...), custom_call_target="tpu_custom_call" | custom-call | flops 600000000 | bytes 10000000 | tf_op jit(solution)/shard_map/cache_attention/pallas_call | solution.py:298
  10.4 0.0 collective-permute-done.2.refs_2_
  10.4 0.1 collective-permute-start.5
  10.5 1.6 %collective-permute-start.3 = (bf16[2,5,64,128]{3,2,1,0:T(8,128)(2,1)S(1)}, bf16[2,5,64,128]{3,2,1,0:T(8,128)(2,1)S(1)}, u32[]{:S(2)}, u32[]{:S(2)}) collective-permute-start(bf16[2,5,64,128]{3,2,1,0:T(8,128)(2,1)S(1)} %collective-permute-done.2.refs_2_), channel_id=1, source_target_pairs={{0,8},{1,9},{2,0},{3,1},{4,6},{5,7},{6,14},{7,15},{8,16},{9,17},{1... | collective-permute-start | bytes 491528 | tf_op jit(solution)/shard_map/ppermute | solution.py:650
  12.1 0.5 %collective-permute-start.7 = (bf16[2,5,64,128]{3,2,1,0:T(8,128)(2,1)S(1)}, bf16[2,5,64,128]{3,2,1,0:T(8,128)(2,1)S(1)}, u32[]{:S(2)}, u32[]{:S(2)}) collective-permute-start(bf16[2,5,64,128]{3,2,1,0:T(8,128)(2,1)S(1)} %collective-permute-done.2.refs_2_), channel_id=1, source_target_pairs={{0,1},{1,0},{2,3},{3,2},{4,5},{5,4},{6,7},{7,6},{8,9},{9,8},{10,11... | collective-permute-start | bytes 491528 | tf_op jit(solution)/shard_map/ppermute | solution.py:648
  12.6 1.7 %cache_attention.4 = (bf16[8,3072,128]{2,1,0:T(8,128)(2,1)S(1)}, bf16[8,3072,128]{2,1,0:T(8,128)(2,1)S(1)}, f32[2,128,128]{2,1,0:T(8,128)S(1)}, f32[2,128,128]{2,1,0:T(8,128)S(1)}) custom-call(s32[8]{0:T(128)S(4)} %get-tuple-element.56.refs_0_, s32[8]{0:T(128)S(4)} %get-tuple-element.57.refs_1_.refs_6_, ...), custom_call_target="tpu_custom_call", output_to_operand_aliasing={{0}: (5, {}), {1}: (6, {})} | custom-call | flops 600000000 | bytes 10000000 | tf_op jit(solution)/shard_map/cache_attention/pallas_call | solution.py:298
  14.3 0.0 collective-permute-done.4.refs_2_
  14.3 0.0 collective-permute-done.5.refs_3_
  14.3 1.5 %collective-permute-done.3.refs_8_.refs_0_ = bf16[2,5,64,128]{3,2,1,0:T(8,128)(2,1)S(1)} collective-permute-done((bf16[2,5,64,128]{3,2,1,0:T(8,128)(2,1)S(1)}, bf16[2,5,64,128]{3,2,1,0:T(8,128)(2,1)S(1)}, u32[]{:S(2)}, u32[]{:S(2)}) %collective-permute-start.3) | collective-permute-done | bytes 163872 | tf_op jit(solution)/shard_map/ppermute | solution.py:650
  15.8 0.0 collective-permute-start.8
  15.8 1.6 %collective-permute-start.6 = (bf16[2,5,64,128]{3,2,1,0:T(8,128)(2,1)S(1)}, bf16[2,5,64,128]{3,2,1,0:T(8,128)(2,1)S(1)}, u32[]{:S(2)}, u32[]{:S(2)}) collective-permute-start(bf16[2,5,64,128]{3,2,1,0:T(8,128)(2,1)S(1)} %collective-permute-done.3.refs_8_.refs_0_), channel_id=1, source_target_pairs={{0,8},{1,9},{2,0},{3,1},{4,6},{5,7},{6,14},{7,15},{8,16},{9,17},{1... | collective-permute-start | bytes 491528 | tf_op jit(solution)/shard_map/ppermute | solution.py:650
  17.4 0.5 %collective-permute-start.10 = (bf16[2,5,64,128]{3,2,1,0:T(8,128)(2,1)S(1)}, bf16[2,5,64,128]{3,2,1,0:T(8,128)(2,1)S(1)}, u32[]{:S(2)}, u32[]{:S(2)}) collective-permute-start(bf16[2,5,64,128]{3,2,1,0:T(8,128)(2,1)S(1)} %collective-permute-done.3.refs_8_.refs_0_), channel_id=1, source_target_pairs={{0,1},{1,0},{2,3},{3,2},{4,5},{5,4},{6,7},{7,6},{8,9},{9,8},{10,11... | collective-permute-start | bytes 491528 | tf_op jit(solution)/shard_map/ppermute | solution.py:648
  18.0 1.7 %cache_attention.5 = (bf16[8,3072,128]{2,1,0:T(8,128)(2,1)S(1)}, bf16[8,3072,128]{2,1,0:T(8,128)(2,1)S(1)}, f32[4,128,128]{2,1,0:T(8,128)S(1)}, f32[4,128,128]{2,1,0:T(8,128)S(1)}) custom-call(s32[8]{0:T(128)S(4)} %get-tuple-element.56.refs_0_, s32[8]{0:T(128)S(4)} %get-tuple-element.57.refs_1_.refs_6_, ...), custom_call_target="tpu_custom_call", output_to_operand_aliasing={{0}: (5, {}), {1}: (6, {})} | custom-call | flops 600000000 | bytes 10000000 | tf_op jit(solution)/shard_map/cache_attention/pallas_call | solution.py:298
  19.7 0.0 collective-permute-done.7.refs_5_
  19.7 0.0 collective-permute-done.8.refs_9_.refs_1_
  19.7 1.4 %collective-permute-done.6.refs_10_.refs_2_ = bf16[2,5,64,128]{3,2,1,0:T(8,128)(2,1)S(1)} collective-permute-done((bf16[2,5,64,128]{3,2,1,0:T(8,128)(2,1)S(1)}, bf16[2,5,64,128]{3,2,1,0:T(8,128)(2,1)S(1)}, u32[]{:S(2)}, u32[]{:S(2)}) %collective-permute-start.6) | collective-permute-done | bytes 163872 | tf_op jit(solution)/shard_map/ppermute | solution.py:650
  21.2 1.6 %collective-permute-start.9 = (bf16[2,5,64,128]{3,2,1,0:T(8,128)(2,1)S(1)}, bf16[2,5,64,128]{3,2,1,0:T(8,128)(2,1)S(1)}, u32[]{:S(2)}, u32[]{:S(2)}) collective-permute-start(bf16[2,5,64,128]{3,2,1,0:T(8,128)(2,1)S(1)} %collective-permute-done.6.refs_10_.refs_2_), channel_id=1, source_target_pairs={{0,8},{1,9},{2,0},{3,1},{4,6},{5,7},{6,14},{7,15},{8,16},{9,17},{1... | collective-permute-start | bytes 491528 | tf_op jit(solution)/shard_map/ppermute | solution.py:650
  22.7 0.0 collective-permute-start.12
  22.7 0.5 %collective-permute-start.11 = (bf16[2,5,64,128]{3,2,1,0:T(8,128)(2,1)S(1)}, bf16[2,5,64,128]{3,2,1,0:T(8,128)(2,1)S(1)}, u32[]{:S(2)}, u32[]{:S(2)}) collective-permute-start(bf16[2,5,64,128]{3,2,1,0:T(8,128)(2,1)S(1)} %collective-permute-done.6.refs_10_.refs_2_), channel_id=1, source_target_pairs={{0,4},{1,5},{2,6},{3,7},{4,0},{5,1},{6,2},{7,3},{8,12},{9,13},{10,... | collective-permute-start | bytes 491528 | tf_op jit(solution)/shard_map/ppermute | solution.py:649
  23.3 0.5 %collective-permute-start.15 = (bf16[2,5,64,128]{3,2,1,0:T(8,128)(2,1)S(1)}, bf16[2,5,64,128]{3,2,1,0:T(8,128)(2,1)S(1)}, u32[]{:S(2)}, u32[]{:S(2)}) collective-permute-start(bf16[2,5,64,128]{3,2,1,0:T(8,128)(2,1)S(1)} %collective-permute-done.6.refs_10_.refs_2_), channel_id=1, source_target_pairs={{0,1},{1,0},{2,3},{3,2},{4,5},{5,4},{6,7},{7,6},{8,9},{9,8},{10,11... | collective-permute-start | bytes 491528 | tf_op jit(solution)/shard_map/ppermute | solution.py:648
  23.8 0.0 slice-done
  23.8 0.0 slice-done.1
  23.8 0.0 slice-done.2
  23.8 0.0 slice-done.3
  23.8 0.0 copy-done
  23.8 3.0 %project.1 = (f32[2,32,512]{2,1,0:T(8,128)S(1)}, bf16[2,32,4096]{2,1,0:T(8,128)(2,1)S(1)}) custom-call(bf16[2,8192,512]{2,1,0:T(8,128)(2,1)S(1)} %bitcast.5, bf16[32,4096]{1,0:T(8,128)(2,1)S(1)} %bitcast.7, bf16[32,4096]{1,0:T(8,128)(2,1)S(1)} %collective-permute-done.4.refs_2_, f32[4,128,128]{2,1,0:T(8,128)S(1)} %get-tuple-element.75.refs_3_.refs_12_), custom_call_target="tpu_custom_call" | custom-call | flops 600000000 | bytes 10000000 | tf_op jit(solution)/shard_map/project/pallas_call | solution.py:336
  26.8 0.0 collective-permute-done.10.refs_7_
  26.8 0.0 collective-permute-done.9.refs_0_
  26.8 0.0 collective-permute-done.12.refs_6_
  26.8 0.0 collective-permute-done.11.refs_11_.refs_3_
  26.8 1.6 %collective-permute-start.13 = (bf16[2,5,64,128]{3,2,1,0:T(8,128)(2,1)S(1)}, bf16[2,5,64,128]{3,2,1,0:T(8,128)(2,1)S(1)}, u32[]{:S(2)}, u32[]{:S(2)}) collective-permute-start(bf16[2,5,64,128]{3,2,1,0:T(8,128)(2,1)S(1)} %collective-permute-done.9.refs_0_), channel_id=1, source_target_pairs={{0,1},{1,0},{2,3},{3,2},{4,5},{5,4},{6,7},{7,6},{8,9},{9,8},{10,11... | collective-permute-start | bytes 491528 | tf_op jit(solution)/shard_map/ppermute | solution.py:676
  28.4 0.0 collective-permute-start.14
  28.4 4.3 %merge.3 = (bf16[2,8192,512]{2,1,0:T(8,128)(2,1)}, bf16[2,64,512]{2,1,0:T(8,128)(2,1)S(1)}, f32[2,32,64]{2,1,0:T(8,128)S(1)}) custom-call(bf16[2,5,64,128]{3,2,1,0:T(8,128)(2,1)S(1)} %collective-permute-done.9.refs_0_, bf16[2,5,64,128]{3,2,1,0:T(8,128)(2,1)S(1)} %get-tuple-element.55.refs_5_.refs_1_, ...), custom_call_target="tpu_custom_call" | custom-call | flops 600000000 | bytes 10000000 | tf_op jit(solution)/shard_map/merge/pallas_call | solution.py:582
  32.7 0.0 collective-permute-done.15.refs_4_
  32.7 0.5 %collective-permute-start.16 = (bf16[2,5,64,128]{3,2,1,0:T(8,128)(2,1)S(1)}, bf16[2,5,64,128]{3,2,1,0:T(8,128)(2,1)S(1)}, u32[]{:S(2)}, u32[]{:S(2)}) collective-permute-start(bf16[2,5,64,128]{3,2,1,0:T(8,128)(2,1)S(1)} %collective-permute-done.15.refs_4_), channel_id=1, source_target_pairs={{0,4},{1,5},{2,6},{3,7},{4,0},{5,1},{6,2},{7,3},{8,12},{9,13},{10,... | collective-permute-start | bytes 491528 | tf_op jit(solution)/shard_map/ppermute | solution.py:681
  33.2 2.9 %merge.4 = (bf16[2,8192,512]{2,1,0:T(8,128)(2,1)}, f32[2,32,64]{2,1,0:T(8,128)S(1)}) custom-call(bf16[2,5,64,128]{3,2,1,0:T(8,128)(2,1)S(1)} %collective-permute-done.3.refs_8_.refs_0_, bf16[2,5,64,128]{3,2,1,0:T(8,128)(2,1)S(1)} %collective-permute-done.8.refs_9_.refs_1_, ...), custom_call_target="tpu_custom_call", output_to_operand_aliasing={{0}: (9, {})} | custom-call | flops 600000000 | bytes 10000000 | tf_op jit(solution)/shard_map/merge/pallas_call | solution.py:582
  36.1 0.0 collective-permute-done.13.refs_0_
  36.1 0.0 collective-permute-done.14.refs_1_
  36.1 0.0 collective-permute-done.16.refs_2_
  36.2 2.9 %merge.5 = (bf16[2,8192,512]{2,1,0:T(8,128)(2,1)}, bf16[4,8,32,128]{3,2,1,0:T(8,128)(2,1)}) custom-call(bf16[2,5,64,128]{3,2,1,0:T(8,128)(2,1)S(1)} %collective-permute-done.13.refs_0_, bf16[2,5,64,128]{3,2,1,0:T(8,128)(2,1)S(1)} %collective-permute-done.14.refs_1_, ...), custom_call_target="tpu_custom_call", output_to_operand_aliasing={{0}: (16, {})} | custom-call | flops 600000000 | bytes 10000000 | tf_op jit(solution)/shard_map/merge/pallas_call | solution.py:582
  (6 shorter events, 0.0 us)
Async XLA Ops:
  0.6 1.9 %collective-permute-start = (bf16[2,64,512]{2,1,0:T(8,128)(2,1)}, bf16[2,64,512]{2,1,0:T(8,128)(2,1)S(1)}, u32[]{:S(2)}, u32[]{:S(2)}) collective-permute-start(bf16[2,64,512]{2,1,0:T(8,128)(2,1)} %bitcast.14), channel_id=1, source_target_pairs={{0,4},{1,5},{2,6},{3,7},{4,0},{5,1},{6,2},{7,3},{8,12},{9,13},{10,... | collective-permute-start | bytes 393224 | tf_op jit(solution)/shard_map/ppermute | solution.py:628
  1.1 1.4 %collective-permute-start.1 = (bf16[2,64,64]{2,1,0:T(8,128)(2,1)}, bf16[2,64,64]{2,1,0:T(8,128)(2,1)S(1)}, u32[]{:S(2)}, u32[]{:S(2)}) collective-permute-start(bf16[2,64,64]{2,1,0:T(8,128)(2,1)} %up.1), channel_id=1, source_target_pairs={{0,4},{1,5},{2,6},{3,7},{4,0},{5,1},{6,2},{7,3},{8,12},{9,13},{10,... | collective-permute-start | bytes 49160 | tf_op jit(solution)/shard_map/ppermute | solution.py:628
  2.6 7.7 %collective-permute-start.2 = (bf16[2,5,64,128]{3,2,1,0:T(8,128)(2,1)S(1)}, bf16[2,5,64,128]{3,2,1,0:T(8,128)(2,1)S(1)}, u32[]{:S(2)}, u32[]{:S(2)}) collective-permute-start(bf16[2,5,64,128]{3,2,1,0:T(8,128)(2,1)S(1)} %get-tuple-element.55.refs_5_.refs_1_), channel_id=1, source_target_pairs={{0,8},{1,9},{2,0},{3,1},{4,6},{5,7},{6,14},{7,15},{8,16},{9,17},{1... | collective-permute-start | bytes 491528 | tf_op jit(solution)/shard_map/ppermute | solution.py:640
  5.6 8.7 %collective-permute-start.4 = (bf16[32,4096]{1,0:T(8,128)(2,1)}, bf16[32,4096]{1,0:T(8,128)(2,1)S(1)}, u32[]{:S(2)}, u32[]{:S(2)}) collective-permute-start(bf16[32,4096]{1,0:T(8,128)(2,1)} %bitcast.6), channel_id=1, source_target_pairs={{1,0},{0,1},{3,2},{2,3},{5,4},{4,5},{7,6},{6,7},{9,8},{8,9},{11,10... | collective-permute-start | bytes 786440 | tf_op jit(solution)/shard_map/ppermute | solution.py:641
  10.4 3.9 %collective-permute-start.5 = (bf16[2,5,64,128]{3,2,1,0:T(8,128)(2,1)S(1)}, bf16[2,5,64,128]{3,2,1,0:T(8,128)(2,1)S(1)}, u32[]{:S(2)}, u32[]{:S(2)}) collective-permute-start(bf16[2,5,64,128]{3,2,1,0:T(8,128)(2,1)S(1)} %collective-permute-done.2.refs_2_), channel_id=1, source_target_pairs={{0,4},{1,5},{2,6},{3,7},{4,0},{5,1},{6,2},{7,3},{8,12},{9,13},{10,... | collective-permute-start | bytes 491528 | tf_op jit(solution)/shard_map/ppermute | solution.py:649
  10.5 5.4 %collective-permute-start.3 = (bf16[2,5,64,128]{3,2,1,0:T(8,128)(2,1)S(1)}, bf16[2,5,64,128]{3,2,1,0:T(8,128)(2,1)S(1)}, u32[]{:S(2)}, u32[]{:S(2)}) collective-permute-start(bf16[2,5,64,128]{3,2,1,0:T(8,128)(2,1)S(1)} %collective-permute-done.2.refs_2_), channel_id=1, source_target_pairs={{0,8},{1,9},{2,0},{3,1},{4,6},{5,7},{6,14},{7,15},{8,16},{9,17},{1... | collective-permute-start | bytes 491528 | tf_op jit(solution)/shard_map/ppermute | solution.py:650
  12.1 7.6 %collective-permute-start.7 = (bf16[2,5,64,128]{3,2,1,0:T(8,128)(2,1)S(1)}, bf16[2,5,64,128]{3,2,1,0:T(8,128)(2,1)S(1)}, u32[]{:S(2)}, u32[]{:S(2)}) collective-permute-start(bf16[2,5,64,128]{3,2,1,0:T(8,128)(2,1)S(1)} %collective-permute-done.2.refs_2_), channel_id=1, source_target_pairs={{0,1},{1,0},{2,3},{3,2},{4,5},{5,4},{6,7},{7,6},{8,9},{9,8},{10,11... | collective-permute-start | bytes 491528 | tf_op jit(solution)/shard_map/ppermute | solution.py:648
  12.6 11.2 %slice-start = ((s8[16777216]{0:T(1024)(128)(4,1)}), s8[4194304]{0:T(1024)(128)(4,1)S(1)}, s32[]{:S(2)}) async-start(s8[16777216]{0:T(1024)(128)(4,1)} %bitcast.4), calls=%async_computation | async-start | bytes 8388608
  12.6 11.2 %slice-start.1 = ((s8[16777216]{0:T(1024)(128)(4,1)}), s8[4194304]{0:T(1024)(128)(4,1)S(1)}, s32[]{:S(2)}) async-start(s8[16777216]{0:T(1024)(128)(4,1)} %bitcast.4), calls=%async_computation.1 | async-start | bytes 8388608
  15.8 8.0 %slice-start.2 = ((s8[16777216]{0:T(1024)(128)(4,1)}), s8[4194304]{0:T(1024)(128)(4,1)S(1)}, s32[]{:S(2)}) async-start(s8[16777216]{0:T(1024)(128)(4,1)} %bitcast.4), calls=%async_computation.2 | async-start | bytes 8388608
  15.8 3.9 %collective-permute-start.8 = (bf16[2,5,64,128]{3,2,1,0:T(8,128)(2,1)S(1)}, bf16[2,5,64,128]{3,2,1,0:T(8,128)(2,1)S(1)}, u32[]{:S(2)}, u32[]{:S(2)}) collective-permute-start(bf16[2,5,64,128]{3,2,1,0:T(8,128)(2,1)S(1)} %collective-permute-done.3.refs_8_.refs_0_), channel_id=1, source_target_pairs={{0,4},{1,5},{2,6},{3,7},{4,0},{5,1},{6,2},{7,3},{8,12},{9,13},{10,... | collective-permute-start | bytes 491528 | tf_op jit(solution)/shard_map/ppermute | solution.py:649
  15.8 5.3 %collective-permute-start.6 = (bf16[2,5,64,128]{3,2,1,0:T(8,128)(2,1)S(1)}, bf16[2,5,64,128]{3,2,1,0:T(8,128)(2,1)S(1)}, u32[]{:S(2)}, u32[]{:S(2)}) collective-permute-start(bf16[2,5,64,128]{3,2,1,0:T(8,128)(2,1)S(1)} %collective-permute-done.3.refs_8_.refs_0_), channel_id=1, source_target_pairs={{0,8},{1,9},{2,0},{3,1},{4,6},{5,7},{6,14},{7,15},{8,16},{9,17},{1... | collective-permute-start | bytes 491528 | tf_op jit(solution)/shard_map/ppermute | solution.py:650
  17.4 9.4 %collective-permute-start.10 = (bf16[2,5,64,128]{3,2,1,0:T(8,128)(2,1)S(1)}, bf16[2,5,64,128]{3,2,1,0:T(8,128)(2,1)S(1)}, u32[]{:S(2)}, u32[]{:S(2)}) collective-permute-start(bf16[2,5,64,128]{3,2,1,0:T(8,128)(2,1)S(1)} %collective-permute-done.3.refs_8_.refs_0_), channel_id=1, source_target_pairs={{0,1},{1,0},{2,3},{3,2},{4,5},{5,4},{6,7},{7,6},{8,9},{9,8},{10,11... | collective-permute-start | bytes 491528 | tf_op jit(solution)/shard_map/ppermute | solution.py:648
  18.0 5.8 %slice-start.3 = ((s8[16777216]{0:T(1024)(128)(4,1)}), s8[4194304]{0:T(1024)(128)(4,1)S(1)}, s32[]{:S(2)}) async-start(s8[16777216]{0:T(1024)(128)(4,1)} %bitcast.4), calls=%async_computation.3 | async-start | bytes 8388608
  18.0 5.8 %copy-start = (bf16[4,8,4096]{2,1,0:T(8,128)(2,1)S(1)}, bf16[4,8,4096]{2,1,0:T(8,128)(2,1)}, u32[]{:S(2)}) copy-start(bf16[4,8,4096]{2,1,0:T(8,128)(2,1)} %param.8) | copy-start | bytes 786436
  21.2 5.6 %collective-permute-start.9 = (bf16[2,5,64,128]{3,2,1,0:T(8,128)(2,1)S(1)}, bf16[2,5,64,128]{3,2,1,0:T(8,128)(2,1)S(1)}, u32[]{:S(2)}, u32[]{:S(2)}) collective-permute-start(bf16[2,5,64,128]{3,2,1,0:T(8,128)(2,1)S(1)} %collective-permute-done.6.refs_10_.refs_2_), channel_id=1, source_target_pairs={{0,8},{1,9},{2,0},{3,1},{4,6},{5,7},{6,14},{7,15},{8,16},{9,17},{1... | collective-permute-start | bytes 491528 | tf_op jit(solution)/shard_map/ppermute | solution.py:650
  22.7 4.1 %collective-permute-start.12 = (bf16[2,5,64,128]{3,2,1,0:T(8,128)(2,1)S(1)}, bf16[2,5,64,128]{3,2,1,0:T(8,128)(2,1)S(1)}, u32[]{:S(2)}, u32[]{:S(2)}) collective-permute-start(bf16[2,5,64,128]{3,2,1,0:T(8,128)(2,1)S(1)} %collective-permute-done.7.refs_5_), channel_id=1, source_target_pairs={{0,4},{1,5},{2,6},{3,7},{4,0},{5,1},{6,2},{7,3},{8,12},{9,13},{10,... | collective-permute-start | bytes 491528 | tf_op jit(solution)/shard_map/ppermute | solution.py:647
  22.7 4.1 %collective-permute-start.11 = (bf16[2,5,64,128]{3,2,1,0:T(8,128)(2,1)S(1)}, bf16[2,5,64,128]{3,2,1,0:T(8,128)(2,1)S(1)}, u32[]{:S(2)}, u32[]{:S(2)}) collective-permute-start(bf16[2,5,64,128]{3,2,1,0:T(8,128)(2,1)S(1)} %collective-permute-done.6.refs_10_.refs_2_), channel_id=1, source_target_pairs={{0,4},{1,5},{2,6},{3,7},{4,0},{5,1},{6,2},{7,3},{8,12},{9,13},{10,... | collective-permute-start | bytes 491528 | tf_op jit(solution)/shard_map/ppermute | solution.py:649
  23.3 9.4 %collective-permute-start.15 = (bf16[2,5,64,128]{3,2,1,0:T(8,128)(2,1)S(1)}, bf16[2,5,64,128]{3,2,1,0:T(8,128)(2,1)S(1)}, u32[]{:S(2)}, u32[]{:S(2)}) collective-permute-start(bf16[2,5,64,128]{3,2,1,0:T(8,128)(2,1)S(1)} %collective-permute-done.6.refs_10_.refs_2_), channel_id=1, source_target_pairs={{0,1},{1,0},{2,3},{3,2},{4,5},{5,4},{6,7},{7,6},{8,9},{9,8},{10,11... | collective-permute-start | bytes 491528 | tf_op jit(solution)/shard_map/ppermute | solution.py:648
  26.8 9.3 %collective-permute-start.13 = (bf16[2,5,64,128]{3,2,1,0:T(8,128)(2,1)S(1)}, bf16[2,5,64,128]{3,2,1,0:T(8,128)(2,1)S(1)}, u32[]{:S(2)}, u32[]{:S(2)}) collective-permute-start(bf16[2,5,64,128]{3,2,1,0:T(8,128)(2,1)S(1)} %collective-permute-done.9.refs_0_), channel_id=1, source_target_pairs={{0,1},{1,0},{2,3},{3,2},{4,5},{5,4},{6,7},{7,6},{8,9},{9,8},{10,11... | collective-permute-start | bytes 491528 | tf_op jit(solution)/shard_map/ppermute | solution.py:676
  28.4 7.8 %collective-permute-start.14 = (bf16[2,5,64,128]{3,2,1,0:T(8,128)(2,1)S(1)}, bf16[2,5,64,128]{3,2,1,0:T(8,128)(2,1)S(1)}, u32[]{:S(2)}, u32[]{:S(2)}) collective-permute-start(bf16[2,5,64,128]{3,2,1,0:T(8,128)(2,1)S(1)} %collective-permute-done.10.refs_7_), channel_id=1, source_target_pairs={{0,4},{1,5},{2,6},{3,7},{4,0},{5,1},{6,2},{7,3},{8,12},{9,13},{10,... | collective-permute-start | bytes 491528 | tf_op jit(solution)/shard_map/ppermute | solution.py:677
  32.7 3.4 %collective-permute-start.16 = (bf16[2,5,64,128]{3,2,1,0:T(8,128)(2,1)S(1)}, bf16[2,5,64,128]{3,2,1,0:T(8,128)(2,1)S(1)}, u32[]{:S(2)}, u32[]{:S(2)}) collective-permute-start(bf16[2,5,64,128]{3,2,1,0:T(8,128)(2,1)S(1)} %collective-permute-done.15.refs_4_), channel_id=1, source_target_pairs={{0,4},{1,5},{2,6},{3,7},{4,0},{5,1},{6,2},{7,3},{8,12},{9,13},{10,... | collective-permute-start | bytes 491528 | tf_op jit(solution)/shard_map/ppermute | solution.py:681

commit v5 on v2

--- a/solution.py
+++ b/solution.py
@@ -424,25 +424,7 @@
     shards = place.find(plan, downs)
     groups = by_projection(place, plan, shards)
 
-    if last:
-        low[...] = low_in[...]
-        for part, group in groups:
-            low[part] += place.low(group, h_buf, tiles)
-        new = []
-        for k in range(pairs):
-            high = low[k].astype(jnp.bfloat16)
-            rest = (low[k] - high.astype(jnp.float32)).astype(jnp.bfloat16)
-            new.append(
-                (
-                    old[k]
-                    + jnp.dot(high, u_buf[k], preferred_element_type=jnp.float32)
-                    + jnp.dot(rest, u_buf[k], preferred_element_type=jnp.float32)
-                ).astype(jnp.bfloat16)
-            )
-        add_new_tokens(q_ref, order, caches, new, out_buf, scale)
-        out_copy = pltpu.make_async_copy(out_buf, out_hbm, out_sem)
-        out_copy.start()
-    elif first:
+    if first:
         columns = width // place.per_lane
         for down, index, _ in groups[0][1]:
 
@@ -485,6 +467,24 @@
         low[...] = jnp.zeros_like(low) if first else low_in[...]
         for part, group in groups:
             low[part] += place.low(group, h_buf, tiles)
+    if last:
+        low[...] = low_in[...]
+        for part, group in groups:
+            low[part] += place.low(group, h_buf, tiles)
+        new = []
+        for k in range(pairs):
+            high = low[k].astype(jnp.bfloat16)
+            rest = (low[k] - high.astype(jnp.float32)).astype(jnp.bfloat16)
+            new.append(
+                (
+                    old[k]
+                    + jnp.dot(high, u_buf[k], preferred_element_type=jnp.float32)
+                    + jnp.dot(rest, u_buf[k], preferred_element_type=jnp.float32)
+                ).astype(jnp.bfloat16)
+            )
+        add_new_tokens(q_ref, order, caches, new, out_buf, scale)
+        out_copy = pltpu.make_async_copy(out_buf, out_hbm, out_sem)
+        out_copy.start()
     for copy in copies + ([out_copy] if last else []):
         copy.wait()
 

time: 39.1 us -> 38.5 us (0.985)
  Pallas kernels: 20.5 us -> 19.1 us
  starting transfers between devices: 14 us -> 14.9 us
    ppermute x3, starting transfers between devices: 1.6 us -> 2.91 us  [shards(): across = [(step, send(came, perm=planes))]]
    pallas_call x3, Pallas kernels: 6.54 us -> 5.36 us  [cache_attention(): pl.pallas_call(functools.partial(attend_cache, pairs, ready, sizes, scale...]
    ppermute x1, starting transfers between devices: 1.56 us -> 1.12 us  [shards(): late = [(last_step, 0, 1, send(came, perm=planes))]]
  transfers between devices with their start and end apart: 17 -> 17, of which waited for: 3 -> 3; matrix products, arithmetic and copies ran while one was open for 0% -> 0% of each run, Pallas kernels for 45% -> 43%
where the time goes in v5:
time: 38.5 us; the launch traced here: 38 us
  Pallas kernels  19.1 us (50%)
  starting transfers between devices  14.9 us (39%)
  waiting for transfers between devices  3.04 us (8%)
  between operations  0.97 us (3%)
    pallas_call x3, Pallas kernels, merge(): pl.pallas_call(functools.partial(merge_some, lay, [e[:3] for e in entries...  9.53 us
    pallas_call x3, Pallas kernels, cache_attention(): pl.pallas_call(functools.partial(attend_cache, pairs, ready, sizes, scale...  5.36 us
    ppermute x3, starting transfers between devices, shards(): sent = send(came, perm=ring)  4.77 us
    pallas_call x1, Pallas kernels, project(): pl.pallas_call(functools.partial(project_old, lay, len(hidden)), out_shap...  2.96 us
    ppermute x3, starting transfers between devices, shards(): across = [(step, send(came, perm=planes))]  2.91 us
    ppermute x1, starting transfers between devices, shards(): sent = send(pair, perm=ring)  2.91 us
    ppermute x3, waiting for transfers between devices, shards(): sent = send(came, perm=ring)  2.85 us
    ppermute x1, starting transfers between devices, shards(): send(tokens, perm=lay.feature_step(i))  1.49 us
  transfers between devices with their start and end apart: 17, of which 3 were waited for; matrix products, arithmetic and copies ran while one was open for 0% of the time, Pallas kernels for 43%

profile of v5, /device:TPU:0, one launch (start us, length us, event | category | flops | bytes accessed | tf_op | source)
XLA Modules:
  0.0 38.0 jit_solution(16554275401455297173)
XLA Ops:
  0.6 0.5 %collective-permute-start = (bf16[2,64,512]{2,1,0:T(8,128)(2,1)}, bf16[2,64,512]{2,1,0:T(8,128)(2,1)S(1)}, u32[]{:S(2)}, u32[]{:S(2)}) collective-permute-start(bf16[2,64,512]{2,1,0:T(8,128)(2,1)} %bitcast.14), channel_id=1, source_target_pairs={{0,4},{1,5},{2,6},{3,7},{4,0},{5,1},{6,2},{7,3},{8,12},{9,13},{10,... | collective-permute-start | bytes 393224 | tf_op jit(solution)/shard_map/ppermute | solution.py:609
  1.1 0.1 collective-permute-start.1
  1.2 1.2 %begin.1 = (bf16[2,5,64,128]{3,2,1,0:T(8,128)(2,1)S(1)}, bf16[2,4,64,128]{3,2,1,0:T(8,128)(2,1)S(1)}, s32[8]{0:T(128)S(4)}, s32[8]{0:T(128)S(4)}, bf16[4,8,32,128]{3,2,1,0:T(8,128)(2,1)S(1)}) custom-call(bf16[2,64,512]{2,1,0:T(8,128)(2,1)} %bitcast.15, bf16[2,64,64]{2,1,0:T(8,128)(2,1)} %up.1, s32[8]{0:T(128)} %len_hbm.1, bf16[4,8,32,128]{3,2,1,0:T(8,128)(2,1)} %q_hbm.1), custom_call_target="tpu_custom_call" | custom-call | flops 600000000 | bytes 10000000 | tf_op jit(solution)/shard_map/begin/pallas_call | solution.py:147
  2.4 0.1 collective-permute-done.1.up
  2.6 0.0 collective-permute-done.down
  2.6 0.1 pack_other.1
  2.6 2.9 %collective-permute-start.2 = (bf16[2,5,64,128]{3,2,1,0:T(8,128)(2,1)S(1)}, bf16[2,5,64,128]{3,2,1,0:T(8,128)(2,1)S(1)}, u32[]{:S(2)}, u32[]{:S(2)}) collective-permute-start(bf16[2,5,64,128]{3,2,1,0:T(8,128)(2,1)S(1)} %get-tuple-element.55.refs_5_.refs_0_), channel_id=1, source_target_pairs={{0,8},{1,9},{2,0},{3,1},{4,6},{5,7},{6,14},{7,15},{8,16},{9,17},{1... | collective-permute-start | bytes 491528 | tf_op jit(solution)/shard_map/ppermute | solution.py:621
  5.6 1.5 %collective-permute-start.4 = (bf16[32,4096]{1,0:T(8,128)(2,1)}, bf16[32,4096]{1,0:T(8,128)(2,1)S(1)}, u32[]{:S(2)}, u32[]{:S(2)}) collective-permute-start(bf16[32,4096]{1,0:T(8,128)(2,1)} %bitcast.6), channel_id=1, source_target_pairs={{1,0},{0,1},{3,2},{2,3},{5,4},{4,5},{7,6},{6,7},{9,8},{8,9},{11,10... | collective-permute-start | bytes 786440 | tf_op jit(solution)/shard_map/ppermute | solution.py:622
  7.0 2.7 %cache_attention.3 = (bf16[8,3072,128]{2,1,0:T(8,128)(2,1)S(1)}, bf16[8,3072,128]{2,1,0:T(8,128)(2,1)S(1)}, f32[2,128,128]{2,1,0:T(8,128)S(1)}, f32[2,128,128]{2,1,0:T(8,128)S(1)}) custom-call(s32[8]{0:T(128)S(4)} %get-tuple-element.56.refs_0_, s32[8]{0:T(128)S(4)} %get-tuple-element.57.refs_1_.refs_6_, ...), custom_call_target="tpu_custom_call" | custom-call | flops 600000000 | bytes 10000000 | tf_op jit(solution)/shard_map/cache_attention/pallas_call | solution.py:298
  9.8 0.0 collective-permute-done.2.refs_1_
  9.8 1.6 %collective-permute-start.3 = (bf16[2,5,64,128]{3,2,1,0:T(8,128)(2,1)S(1)}, bf16[2,5,64,128]{3,2,1,0:T(8,128)(2,1)S(1)}, u32[]{:S(2)}, u32[]{:S(2)}) collective-permute-start(bf16[2,5,64,128]{3,2,1,0:T(8,128)(2,1)S(1)} %collective-permute-done.2.refs_1_), channel_id=1, source_target_pairs={{0,8},{1,9},{2,0},{3,1},{4,6},{5,7},{6,14},{7,15},{8,16},{9,17},{1... | collective-permute-start | bytes 491528 | tf_op jit(solution)/shard_map/ppermute | solution.py:631
  11.4 0.0 collective-permute-start.5
  11.4 1.0 %collective-permute-start.7 = (bf16[2,5,64,128]{3,2,1,0:T(8,128)(2,1)S(1)}, bf16[2,5,64,128]{3,2,1,0:T(8,128)(2,1)S(1)}, u32[]{:S(2)}, u32[]{:S(2)}) collective-permute-start(bf16[2,5,64,128]{3,2,1,0:T(8,128)(2,1)S(1)} %collective-permute-done.2.refs_1_), channel_id=1, source_target_pairs={{0,1},{1,0},{2,3},{3,2},{4,5},{5,4},{6,7},{7,6},{8,9},{9,8},{10,11... | collective-permute-start | bytes 491528 | tf_op jit(solution)/shard_map/ppermute | solution.py:629
  12.4 1.4 %cache_attention.4 = (bf16[8,3072,128]{2,1,0:T(8,128)(2,1)S(1)}, bf16[8,3072,128]{2,1,0:T(8,128)(2,1)S(1)}, f32[2,128,128]{2,1,0:T(8,128)S(1)}, f32[2,128,128]{2,1,0:T(8,128)S(1)}) custom-call(s32[8]{0:T(128)S(4)} %get-tuple-element.56.refs_0_, s32[8]{0:T(128)S(4)} %get-tuple-element.57.refs_1_.refs_6_, ...), custom_call_target="tpu_custom_call", output_to_operand_aliasing={{0}: (5, {}), {1}: (6, {})} | custom-call | flops 600000000 | bytes 10000000 | tf_op jit(solution)/shard_map/cache_attention/pallas_call | solution.py:298
  13.8 0.0 collective-permute-done.4.refs_2_
  13.8 1.3 %collective-permute-done.3.refs_3_ = bf16[2,5,64,128]{3,2,1,0:T(8,128)(2,1)S(1)} collective-permute-done((bf16[2,5,64,128]{3,2,1,0:T(8,128)(2,1)S(1)}, bf16[2,5,64,128]{3,2,1,0:T(8,128)(2,1)S(1)}, u32[]{:S(2)}, u32[]{:S(2)}) %collective-permute-start.3) | collective-permute-done | bytes 163872 | tf_op jit(solution)/shard_map/ppermute | solution.py:631
  15.1 0.0 collective-permute-done.5.refs_2_
  15.1 1.6 %collective-permute-start.6 = (bf16[2,5,64,128]{3,2,1,0:T(8,128)(2,1)S(1)}, bf16[2,5,64,128]{3,2,1,0:T(8,128)(2,1)S(1)}, u32[]{:S(2)}, u32[]{:S(2)}) collective-permute-start(bf16[2,5,64,128]{3,2,1,0:T(8,128)(2,1)S(1)} %collective-permute-done.3.refs_3_), channel_id=1, source_target_pairs={{0,8},{1,9},{2,0},{3,1},{4,6},{5,7},{6,14},{7,15},{8,16},{9,17},{1... | collective-permute-start | bytes 491528 | tf_op jit(solution)/shard_map/ppermute | solution.py:631
  16.7 0.0 collective-permute-start.8
  16.7 1.0 %collective-permute-start.10 = (bf16[2,5,64,128]{3,2,1,0:T(8,128)(2,1)S(1)}, bf16[2,5,64,128]{3,2,1,0:T(8,128)(2,1)S(1)}, u32[]{:S(2)}, u32[]{:S(2)}) collective-permute-start(bf16[2,5,64,128]{3,2,1,0:T(8,128)(2,1)S(1)} %collective-permute-done.3.refs_3_), channel_id=1, source_target_pairs={{0,1},{1,0},{2,3},{3,2},{4,5},{5,4},{6,7},{7,6},{8,9},{9,8},{10,11... | collective-permute-start | bytes 491528 | tf_op jit(solution)/shard_map/ppermute | solution.py:629
  17.7 1.2 %cache_attention.5 = (bf16[8,3072,128]{2,1,0:T(8,128)(2,1)S(1)}, bf16[8,3072,128]{2,1,0:T(8,128)(2,1)S(1)}, f32[4,128,128]{2,1,0:T(8,128)S(1)}, f32[4,128,128]{2,1,0:T(8,128)S(1)}) custom-call(s32[8]{0:T(128)S(4)} %get-tuple-element.56.refs_0_, s32[8]{0:T(128)S(4)} %get-tuple-element.57.refs_1_.refs_6_, ...), custom_call_target="tpu_custom_call", output_to_operand_aliasing={{0}: (5, {}), {1}: (6, {})} | custom-call | flops 600000000 | bytes 10000000 | tf_op jit(solution)/shard_map/cache_attention/pallas_call | solution.py:298
  18.9 0.0 collective-permute-done.7.refs_1_
  18.9 1.5 %collective-permute-done.6.refs_5_ = bf16[2,5,64,128]{3,2,1,0:T(8,128)(2,1)S(1)} collective-permute-done((bf16[2,5,64,128]{3,2,1,0:T(8,128)(2,1)S(1)}, bf16[2,5,64,128]{3,2,1,0:T(8,128)(2,1)S(1)}, u32[]{:S(2)}, u32[]{:S(2)}) %collective-permute-start.6) | collective-permute-done | bytes 163872 | tf_op jit(solution)/shard_map/ppermute | solution.py:631
  20.5 0.0 collective-permute-done.8.refs_4_
  20.5 1.6 %collective-permute-start.9 = (bf16[2,5,64,128]{3,2,1,0:T(8,128)(2,1)S(1)}, bf16[2,5,64,128]{3,2,1,0:T(8,128)(2,1)S(1)}, u32[]{:S(2)}, u32[]{:S(2)}) collective-permute-start(bf16[2,5,64,128]{3,2,1,0:T(8,128)(2,1)S(1)} %collective-permute-done.6.refs_5_), channel_id=1, source_target_pairs={{0,8},{1,9},{2,0},{3,1},{4,6},{5,7},{6,14},{7,15},{8,16},{9,17},{1... | collective-permute-start | bytes 491528 | tf_op jit(solution)/shard_map/ppermute | solution.py:631
  22.0 0.0 collective-permute-start.11
  22.0 0.5 %collective-permute-start.12 = (bf16[2,5,64,128]{3,2,1,0:T(8,128)(2,1)S(1)}, bf16[2,5,64,128]{3,2,1,0:T(8,128)(2,1)S(1)}, u32[]{:S(2)}, u32[]{:S(2)}) collective-permute-start(bf16[2,5,64,128]{3,2,1,0:T(8,128)(2,1)S(1)} %collective-permute-done.7.refs_1_), channel_id=1, source_target_pairs={{0,4},{1,5},{2,6},{3,7},{4,0},{5,1},{6,2},{7,3},{8,12},{9,13},{10,... | collective-permute-start | bytes 491528 | tf_op jit(solution)/shard_map/ppermute | solution.py:628
  22.6 1.0 %collective-permute-start.15 = (bf16[2,5,64,128]{3,2,1,0:T(8,128)(2,1)S(1)}, bf16[2,5,64,128]{3,2,1,0:T(8,128)(2,1)S(1)}, u32[]{:S(2)}, u32[]{:S(2)}) collective-permute-start(bf16[2,5,64,128]{3,2,1,0:T(8,128)(2,1)S(1)} %collective-permute-done.6.refs_5_), channel_id=1, source_target_pairs={{0,1},{1,0},{2,3},{3,2},{4,5},{5,4},{6,7},{7,6},{8,9},{9,8},{10,11... | collective-permute-start | bytes 491528 | tf_op jit(solution)/shard_map/ppermute | solution.py:629
  23.5 0.0 slice-done
  23.5 0.0 slice-done.1
  23.5 0.0 slice-done.2
  23.5 0.0 slice-done.3
  23.5 0.0 copy-done
  23.6 3.0 %project.1 = (f32[2,32,512]{2,1,0:T(8,128)S(1)}, bf16[2,32,4096]{2,1,0:T(8,128)(2,1)S(1)}) custom-call(bf16[2,8192,512]{2,1,0:T(8,128)(2,1)S(1)} %bitcast.5, bf16[32,4096]{1,0:T(8,128)(2,1)S(1)} %bitcast.7, bf16[32,4096]{1,0:T(8,128)(2,1)S(1)} %collective-permute-done.4.refs_2_, f32[4,128,128]{2,1,0:T(8,128)S(1)} %get-tuple-element.75.refs_3_.refs_12_), custom_call_target="tpu_custom_call" | custom-call | flops 600000000 | bytes 10000000 | tf_op jit(solution)/shard_map/project/pallas_call | solution.py:336
  26.5 0.0 collective-permute-done.10.refs_3_
  26.5 0.0 collective-permute-done.9.refs_7_
  26.5 0.0 collective-permute-done.11.refs_6_
  26.5 0.0 collective-permute-done.12.refs_2_
  26.6 1.1 %collective-permute-start.13 = (bf16[2,5,64,128]{3,2,1,0:T(8,128)(2,1)S(1)}, bf16[2,5,64,128]{3,2,1,0:T(8,128)(2,1)S(1)}, u32[]{:S(2)}, u32[]{:S(2)}) collective-permute-start(bf16[2,5,64,128]{3,2,1,0:T(8,128)(2,1)S(1)} %collective-permute-done.9.refs_7_), channel_id=1, source_target_pairs={{0,1},{1,0},{2,3},{3,2},{4,5},{5,4},{6,7},{7,6},{8,9},{9,8},{10,11... | collective-permute-start | bytes 491528 | tf_op jit(solution)/shard_map/ppermute | solution.py:654
  27.7 4.2 %merge.3 = (bf16[2,8192,512]{2,1,0:T(8,128)(2,1)}, bf16[2,64,512]{2,1,0:T(8,128)(2,1)S(1)}, f32[2,32,64]{2,1,0:T(8,128)S(1)}) custom-call(bf16[2,5,64,128]{3,2,1,0:T(8,128)(2,1)S(1)} %get-tuple-element.55.refs_5_.refs_0_, bf16[2,5,64,128]{3,2,1,0:T(8,128)(2,1)S(1)} %collective-permute-done.2.refs_1_, ...), custom_call_target="tpu_custom_call" | custom-call | flops 600000000 | bytes 10000000 | tf_op jit(solution)/shard_map/merge/pallas_call | solution.py:571
  31.9 0.0 collective-permute-done.15.refs_4_
  31.9 0.1 collective-permute-start.16
  31.9 0.5 %collective-permute-start.14 = (bf16[2,5,64,128]{3,2,1,0:T(8,128)(2,1)S(1)}, bf16[2,5,64,128]{3,2,1,0:T(8,128)(2,1)S(1)}, u32[]{:S(2)}, u32[]{:S(2)}) collective-permute-start(bf16[2,5,64,128]{3,2,1,0:T(8,128)(2,1)S(1)} %collective-permute-done.10.refs_3_), channel_id=1, source_target_pairs={{0,4},{1,5},{2,6},{3,7},{4,0},{5,1},{6,2},{7,3},{8,12},{9,13},{10,... | collective-permute-start | bytes 491528 | tf_op jit(solution)/shard_map/ppermute | solution.py:655
  32.4 2.7 %merge.4 = (bf16[2,8192,512]{2,1,0:T(8,128)(2,1)}, f32[2,32,64]{2,1,0:T(8,128)S(1)}) custom-call(bf16[2,4,64,128]{3,2,1,0:T(8,128)(2,1)S(1)} %get-tuple-element.90.refs_0_, bf16[2,5,64,128]{3,2,1,0:T(8,128)(2,1)S(1)} %collective-permute-done.7.refs_1_, bf16[2,5,64,128]{3,2,1,0:T(8,128)(2,1)S(1)} %collective-permute-done.12.refs_2_, ...), custom_call_target="tpu_custom_call", output_to_operand_aliasing={{0}: (9, {})} | custom-call | flops 600000000 | bytes 10000000 | tf_op jit(solution)/shard_map/merge/pallas_call | solution.py:571
  35.2 0.0 collective-permute-done.16.refs_2_
  35.2 0.0 collective-permute-done.13.refs_0_
  35.2 0.0 collective-permute-done.14.refs_1_
  35.2 2.6 %merge.5 = (bf16[2,8192,512]{2,1,0:T(8,128)(2,1)}, bf16[4,8,32,128]{3,2,1,0:T(8,128)(2,1)}) custom-call(bf16[2,5,64,128]{3,2,1,0:T(8,128)(2,1)S(1)} %collective-permute-done.13.refs_0_, bf16[2,5,64,128]{3,2,1,0:T(8,128)(2,1)S(1)} %collective-permute-done.14.refs_1_, ...), custom_call_target="tpu_custom_call", output_to_operand_aliasing={{0}: (16, {})} | custom-call | flops 600000000 | bytes 10000000 | tf_op jit(solution)/shard_map/merge/pallas_call | solution.py:571
  (6 shorter events, 0.0 us)
Async XLA Ops:
  0.6 1.9 %collective-permute-start = (bf16[2,64,512]{2,1,0:T(8,128)(2,1)}, bf16[2,64,512]{2,1,0:T(8,128)(2,1)S(1)}, u32[]{:S(2)}, u32[]{:S(2)}) collective-permute-start(bf16[2,64,512]{2,1,0:T(8,128)(2,1)} %bitcast.14), channel_id=1, source_target_pairs={{0,4},{1,5},{2,6},{3,7},{4,0},{5,1},{6,2},{7,3},{8,12},{9,13},{10,... | collective-permute-start | bytes 393224 | tf_op jit(solution)/shard_map/ppermute | solution.py:609
  1.1 1.4 %collective-permute-start.1 = (bf16[2,64,64]{2,1,0:T(8,128)(2,1)}, bf16[2,64,64]{2,1,0:T(8,128)(2,1)S(1)}, u32[]{:S(2)}, u32[]{:S(2)}) collective-permute-start(bf16[2,64,64]{2,1,0:T(8,128)(2,1)} %up.1), channel_id=1, source_target_pairs={{0,4},{1,5},{2,6},{3,7},{4,0},{5,1},{6,2},{7,3},{8,12},{9,13},{10,... | collective-permute-start | bytes 49160 | tf_op jit(solution)/shard_map/ppermute | solution.py:609
  2.6 7.1 %collective-permute-start.2 = (bf16[2,5,64,128]{3,2,1,0:T(8,128)(2,1)S(1)}, bf16[2,5,64,128]{3,2,1,0:T(8,128)(2,1)S(1)}, u32[]{:S(2)}, u32[]{:S(2)}) collective-permute-start(bf16[2,5,64,128]{3,2,1,0:T(8,128)(2,1)S(1)} %get-tuple-element.55.refs_5_.refs_0_), channel_id=1, source_target_pairs={{0,8},{1,9},{2,0},{3,1},{4,6},{5,7},{6,14},{7,15},{8,16},{9,17},{1... | collective-permute-start | bytes 491528 | tf_op jit(solution)/shard_map/ppermute | solution.py:621
  5.6 8.3 %collective-permute-start.4 = (bf16[32,4096]{1,0:T(8,128)(2,1)}, bf16[32,4096]{1,0:T(8,128)(2,1)S(1)}, u32[]{:S(2)}, u32[]{:S(2)}) collective-permute-start(bf16[32,4096]{1,0:T(8,128)(2,1)} %bitcast.6), channel_id=1, source_target_pairs={{1,0},{0,1},{3,2},{2,3},{5,4},{4,5},{7,6},{6,7},{9,8},{8,9},{11,10... | collective-permute-start | bytes 786440 | tf_op jit(solution)/shard_map/ppermute | solution.py:622
  9.8 5.4 %collective-permute-start.3 = (bf16[2,5,64,128]{3,2,1,0:T(8,128)(2,1)S(1)}, bf16[2,5,64,128]{3,2,1,0:T(8,128)(2,1)S(1)}, u32[]{:S(2)}, u32[]{:S(2)}) collective-permute-start(bf16[2,5,64,128]{3,2,1,0:T(8,128)(2,1)S(1)} %collective-permute-done.2.refs_1_), channel_id=1, source_target_pairs={{0,8},{1,9},{2,0},{3,1},{4,6},{5,7},{6,14},{7,15},{8,16},{9,17},{1... | collective-permute-start | bytes 491528 | tf_op jit(solution)/shard_map/ppermute | solution.py:631
  11.4 3.7 %collective-permute-start.5 = (bf16[2,5,64,128]{3,2,1,0:T(8,128)(2,1)S(1)}, bf16[2,5,64,128]{3,2,1,0:T(8,128)(2,1)S(1)}, u32[]{:S(2)}, u32[]{:S(2)}) collective-permute-start(bf16[2,5,64,128]{3,2,1,0:T(8,128)(2,1)S(1)} %collective-permute-done.2.refs_1_), channel_id=1, source_target_pairs={{0,4},{1,5},{2,6},{3,7},{4,0},{5,1},{6,2},{7,3},{8,12},{9,13},{10,... | collective-permute-start | bytes 491528 | tf_op jit(solution)/shard_map/ppermute | solution.py:630
  11.4 7.5 %collective-permute-start.7 = (bf16[2,5,64,128]{3,2,1,0:T(8,128)(2,1)S(1)}, bf16[2,5,64,128]{3,2,1,0:T(8,128)(2,1)S(1)}, u32[]{:S(2)}, u32[]{:S(2)}) collective-permute-start(bf16[2,5,64,128]{3,2,1,0:T(8,128)(2,1)S(1)} %collective-permute-done.2.refs_1_), channel_id=1, source_target_pairs={{0,1},{1,0},{2,3},{3,2},{4,5},{5,4},{6,7},{7,6},{8,9},{9,8},{10,11... | collective-permute-start | bytes 491528 | tf_op jit(solution)/shard_map/ppermute | solution.py:629
  12.4 11.2 %slice-start = ((s8[16777216]{0:T(1024)(128)(4,1)}), s8[4194304]{0:T(1024)(128)(4,1)S(1)}, s32[]{:S(2)}) async-start(s8[16777216]{0:T(1024)(128)(4,1)} %bitcast.4), calls=%async_computation | async-start | bytes 8388608
  12.4 11.2 %slice-start.1 = ((s8[16777216]{0:T(1024)(128)(4,1)}), s8[4194304]{0:T(1024)(128)(4,1)S(1)}, s32[]{:S(2)}) async-start(s8[16777216]{0:T(1024)(128)(4,1)} %bitcast.4), calls=%async_computation.1 | async-start | bytes 8388608
  15.1 8.4 %slice-start.2 = ((s8[16777216]{0:T(1024)(128)(4,1)}), s8[4194304]{0:T(1024)(128)(4,1)S(1)}, s32[]{:S(2)}) async-start(s8[16777216]{0:T(1024)(128)(4,1)} %bitcast.4), calls=%async_computation.2 | async-start | bytes 8388608
  15.1 5.3 %collective-permute-start.6 = (bf16[2,5,64,128]{3,2,1,0:T(8,128)(2,1)S(1)}, bf16[2,5,64,128]{3,2,1,0:T(8,128)(2,1)S(1)}, u32[]{:S(2)}, u32[]{:S(2)}) collective-permute-start(bf16[2,5,64,128]{3,2,1,0:T(8,128)(2,1)S(1)} %collective-permute-done.3.refs_3_), channel_id=1, source_target_pairs={{0,8},{1,9},{2,0},{3,1},{4,6},{5,7},{6,14},{7,15},{8,16},{9,17},{1... | collective-permute-start | bytes 491528 | tf_op jit(solution)/shard_map/ppermute | solution.py:631
  16.7 3.7 %collective-permute-start.8 = (bf16[2,5,64,128]{3,2,1,0:T(8,128)(2,1)S(1)}, bf16[2,5,64,128]{3,2,1,0:T(8,128)(2,1)S(1)}, u32[]{:S(2)}, u32[]{:S(2)}) collective-permute-start(bf16[2,5,64,128]{3,2,1,0:T(8,128)(2,1)S(1)} %collective-permute-done.3.refs_3_), channel_id=1, source_target_pairs={{0,4},{1,5},{2,6},{3,7},{4,0},{5,1},{6,2},{7,3},{8,12},{9,13},{10,... | collective-permute-start | bytes 491528 | tf_op jit(solution)/shard_map/ppermute | solution.py:630
  16.7 9.8 %collective-permute-start.10 = (bf16[2,5,64,128]{3,2,1,0:T(8,128)(2,1)S(1)}, bf16[2,5,64,128]{3,2,1,0:T(8,128)(2,1)S(1)}, u32[]{:S(2)}, u32[]{:S(2)}) collective-permute-start(bf16[2,5,64,128]{3,2,1,0:T(8,128)(2,1)S(1)} %collective-permute-done.3.refs_3_), channel_id=1, source_target_pairs={{0,1},{1,0},{2,3},{3,2},{4,5},{5,4},{6,7},{7,6},{8,9},{9,8},{10,11... | collective-permute-start | bytes 491528 | tf_op jit(solution)/shard_map/ppermute | solution.py:629
  17.7 5.8 %slice-start.3 = ((s8[16777216]{0:T(1024)(128)(4,1)}), s8[4194304]{0:T(1024)(128)(4,1)S(1)}, s32[]{:S(2)}) async-start(s8[16777216]{0:T(1024)(128)(4,1)} %bitcast.4), calls=%async_computation.3 | async-start | bytes 8388608
  17.7 5.8 %copy-start = (bf16[4,8,4096]{2,1,0:T(8,128)(2,1)S(1)}, bf16[4,8,4096]{2,1,0:T(8,128)(2,1)}, u32[]{:S(2)}) copy-start(bf16[4,8,4096]{2,1,0:T(8,128)(2,1)} %param.8) | copy-start | bytes 786436
  20.5 6.1 %collective-permute-start.9 = (bf16[2,5,64,128]{3,2,1,0:T(8,128)(2,1)S(1)}, bf16[2,5,64,128]{3,2,1,0:T(8,128)(2,1)S(1)}, u32[]{:S(2)}, u32[]{:S(2)}) collective-permute-start(bf16[2,5,64,128]{3,2,1,0:T(8,128)(2,1)S(1)} %collective-permute-done.6.refs_5_), channel_id=1, source_target_pairs={{0,8},{1,9},{2,0},{3,1},{4,6},{5,7},{6,14},{7,15},{8,16},{9,17},{1... | collective-permute-start | bytes 491528 | tf_op jit(solution)/shard_map/ppermute | solution.py:631
  22.0 4.5 %collective-permute-start.11 = (bf16[2,5,64,128]{3,2,1,0:T(8,128)(2,1)S(1)}, bf16[2,5,64,128]{3,2,1,0:T(8,128)(2,1)S(1)}, u32[]{:S(2)}, u32[]{:S(2)}) collective-permute-start(bf16[2,5,64,128]{3,2,1,0:T(8,128)(2,1)S(1)} %collective-permute-done.6.refs_5_), channel_id=1, source_target_pairs={{0,4},{1,5},{2,6},{3,7},{4,0},{5,1},{6,2},{7,3},{8,12},{9,13},{10,... | collective-permute-start | bytes 491528 | tf_op jit(solution)/shard_map/ppermute | solution.py:630
  22.0 4.5 %collective-permute-start.12 = (bf16[2,5,64,128]{3,2,1,0:T(8,128)(2,1)S(1)}, bf16[2,5,64,128]{3,2,1,0:T(8,128)(2,1)S(1)}, u32[]{:S(2)}, u32[]{:S(2)}) collective-permute-start(bf16[2,5,64,128]{3,2,1,0:T(8,128)(2,1)S(1)} %collective-permute-done.7.refs_1_), channel_id=1, source_target_pairs={{0,4},{1,5},{2,6},{3,7},{4,0},{5,1},{6,2},{7,3},{8,12},{9,13},{10,... | collective-permute-start | bytes 491528 | tf_op jit(solution)/shard_map/ppermute | solution.py:628
  22.6 9.3 %collective-permute-start.15 = (bf16[2,5,64,128]{3,2,1,0:T(8,128)(2,1)S(1)}, bf16[2,5,64,128]{3,2,1,0:T(8,128)(2,1)S(1)}, u32[]{:S(2)}, u32[]{:S(2)}) collective-permute-start(bf16[2,5,64,128]{3,2,1,0:T(8,128)(2,1)S(1)} %collective-permute-done.6.refs_5_), channel_id=1, source_target_pairs={{0,1},{1,0},{2,3},{3,2},{4,5},{5,4},{6,7},{7,6},{8,9},{9,8},{10,11... | collective-permute-start | bytes 491528 | tf_op jit(solution)/shard_map/ppermute | solution.py:629
  26.6 8.6 %collective-permute-start.13 = (bf16[2,5,64,128]{3,2,1,0:T(8,128)(2,1)S(1)}, bf16[2,5,64,128]{3,2,1,0:T(8,128)(2,1)S(1)}, u32[]{:S(2)}, u32[]{:S(2)}) collective-permute-start(bf16[2,5,64,128]{3,2,1,0:T(8,128)(2,1)S(1)} %collective-permute-done.9.refs_7_), channel_id=1, source_target_pairs={{0,1},{1,0},{2,3},{3,2},{4,5},{5,4},{6,7},{7,6},{8,9},{9,8},{10,11... | collective-permute-start | bytes 491528 | tf_op jit(solution)/shard_map/ppermute | solution.py:654
  31.9 3.3 %collective-permute-start.16 = (bf16[2,5,64,128]{3,2,1,0:T(8,128)(2,1)S(1)}, bf16[2,5,64,128]{3,2,1,0:T(8,128)(2,1)S(1)}, u32[]{:S(2)}, u32[]{:S(2)}) collective-permute-start(bf16[2,5,64,128]{3,2,1,0:T(8,128)(2,1)S(1)} %collective-permute-done.15.refs_4_), channel_id=1, source_target_pairs={{0,4},{1,5},{2,6},{3,7},{4,0},{5,1},{6,2},{7,3},{8,12},{9,13},{10,... | collective-permute-start | bytes 491528 | tf_op jit(solution)/shard_map/ppermute | solution.py:659
  31.9 3.3 %collective-permute-start.14 = (bf16[2,5,64,128]{3,2,1,0:T(8,128)(2,1)S(1)}, bf16[2,5,64,128]{3,2,1,0:T(8,128)(2,1)S(1)}, u32[]{:S(2)}, u32[]{:S(2)}) collective-permute-start(bf16[2,5,64,128]{3,2,1,0:T(8,128)(2,1)S(1)} %collective-permute-done.10.refs_3_), channel_id=1, source_target_pairs={{0,4},{1,5},{2,6},{3,7},{4,0},{5,1},{6,2},{7,3},{8,12},{9,13},{10,... | collective-permute-start | bytes 491528 | tf_op jit(solution)/shard_map/ppermute | solution.py:655
